TPU v7x, 512 devices: a whole 4x4x16 slice. The times are simulated.
512 devices in a mesh: pipe: 8 (over y, core), expert: 64 (over z, x).
Axes of the slice: x: 4, y: 4, z: 16, core: 2. Of those that a mesh axis runs over, the one named last changes fastest.
Arguments:
- state: bfloat16 [8, 2, 64, 16, 896], P('pipe', None, 'expert'), may hold values from -6 to 6
- up_weight: bfloat16 [8, 64, 896, 1024], P('pipe', 'expert'), may hold values from -0.0625 to 0.0625
- down_weight: bfloat16 [8, 64, 1024, 896], P('pipe', 'expert'), may hold values from -0.1875 to 0.1875
- norm_gain: float32 [8, 7168], P('pipe'), may hold values from 0.1 to 1.9
- routes: int32 [2, 2, 8, 128, 2], P(None, None, 'pipe'), may hold values from 0 to 7, all different within a row; in each aligned block of 16 rows (0 to 15, 16 to 31, ..., all dimensions but the last counted through in order) at most 8 rows name the same one
- route_weight: float32 [2, 2, 8, 128, 2], P(None, None, 'pipe'), may hold values from 0.1 to 1
Outputs:
- final_state: bfloat16 [8, 2, 64, 16, 896], P('pipe', None, 'expert')
Inputs may be any that keep to these rules, and one draw needn't show every extreme that they name: `routes`: each token names 2 different experts; among the 16 tokens of one group at one step, stream and section no expert is named by more than 8 tokens.
All inputs are finite; a program needn't handle non-finite values.
Results may differ from a plain program's by a relative error of at most 0.0059.
Values may be sent and summed in bfloat16 or wider, within the bound.
No kernel may reach another device: no remote copies, remote signals or barrier semaphores. Data moves between devices by JAX's collectives and lax.ppermute only.
A program may use at most 64 MiB of HBM per device.

v0:
```python
import jax
import jax.numpy as jnp
from jax import lax
from jax.sharding import PartitionSpec as P


def swapped(value, axis, stride):
    return lax.ppermute(value, axis, [(i, i ^ 1 << stride) for i in range(lax.axis_size(axis))])


def from_behind(value, axis, steps):
    count = lax.axis_size(axis)
    pairs = [(source, (source + steps) % count) for source in range(count)]
    return lax.ppermute(value, axis, pairs)


def route_blocks(data, group_id, outbound):
    shape = data.shape
    groups = shape[1]
    levels = groups.bit_length() - 1
    for level in range(levels):
        low = 2**level
        split = data.reshape(shape[0], groups // (2 * low), 2, low, shape[2], shape[3])
        mine = (group_id >> level) % 2
        other = 1 - mine
        outgoing = lax.dynamic_index_in_dim(split, other, axis=2, keepdims=False)
        if outbound:
            arrived = swapped(outgoing, "expert", 3 + level)
        else:
            arrived = swapped(outgoing, "expert", 3 + level)
        merged = lax.dynamic_update_index_in_dim(split, arrived, other, axis=2)
        data = merged.reshape(shape)
    return data


def hidden_units(partial_value, slice_id):
    block = partial_value
    for level in range(3):
        half = block.shape[1] // 2
        mine = (slice_id >> level) % 2
        outgoing = lax.dynamic_slice_in_dim(block, (1 - mine) * half, half, 1)
        kept = lax.dynamic_slice_in_dim(block, mine * half, half, 1)
        block = kept + swapped(outgoing, "expert", level)
    active = jax.nn.silu(block).astype(jnp.bfloat16)
    for level in (2, 1, 0):
        mine = (slice_id >> level) % 2
        arrived = swapped(active, "expert", level)
        span = active.shape[1]
        joined = jnp.concatenate([arrived, arrived], axis=1)
        active = lax.dynamic_update_slice_in_dim(joined, active, mine * span, 1)
    return active


def section_layer(blocks, gain_slice, up_local, down_local, chosen, weights, group_id, slice_id):
    streams, tok_grp, width = blocks.shape
    topk = chosen.shape[2]
    xf = blocks.astype(jnp.float32)
    squares = jnp.sum(xf * xf, axis=2)
    for level in range(3):
        squares = squares + swapped(squares, "expert", level)
    full_width = width * 8
    normed = (xf * lax.rsqrt(squares / full_width + 1e-06)[..., None] * gain_slice).astype(
        jnp.bfloat16
    )
    groups = lax.axis_size("expert") // 8
    capacity = min(tok_grp, 2 * tok_grp * topk // groups)
    expert_ids = jnp.arange(groups, dtype=jnp.int32)
    matches = chosen[:, :, :, None] == expert_ids
    hits = jnp.sum(matches.astype(jnp.int32), axis=2)
    ranks = jnp.cumsum(hits, axis=1) - hits
    slot_ids = jnp.arange(capacity, dtype=jnp.int32)
    placed = jnp.where((hits[..., None] == 1) & (ranks[..., None] == slot_ids), 1.0, 0.0)
    outgoing = jnp.einsum(
        "mtjc,mtd->mjcd", placed.astype(jnp.bfloat16), normed, preferred_element_type=jnp.float32
    ).astype(jnp.bfloat16)
    received = route_blocks(outgoing, group_id, True)
    rows = received.reshape(streams * groups * capacity, width)
    partial_value = jnp.dot(rows, up_local, preferred_element_type=jnp.float32)
    hidden = hidden_units(partial_value, slice_id)
    produced = jnp.dot(hidden, down_local, preferred_element_type=jnp.float32).astype(jnp.bfloat16)
    returned = route_blocks(produced.reshape(streams, groups, capacity, width), group_id, False)
    flat_out = returned.reshape(streams, groups * capacity, width)
    choice_rank = jnp.take_along_axis(ranks, chosen, axis=2)
    slot_index = (chosen * capacity + choice_rank).reshape(streams, tok_grp * topk)
    fetched = jnp.take_along_axis(flat_out, slot_index[:, :, None], axis=1)
    fetched = fetched.reshape(streams, tok_grp, topk, width).astype(jnp.float32)
    mixed = jnp.sum(weights[..., None] * fetched, axis=2)
    return (xf + mixed).astype(jnp.bfloat16)


def shards(state, up_weight, down_weight, norm_gain, routes, route_weight):
    expert_index = lax.axis_index("expert")
    group_id = expert_index // 8
    slice_id = expert_index % 8
    width = state.shape[4]
    tok_grp = state.shape[3]
    gain_slice = lax.dynamic_slice_in_dim(norm_gain[0], slice_id * width, width, 0)
    current = state[0, :, 0]
    for step in range(routes.shape[0]):
        chosen = lax.dynamic_slice_in_dim(routes[step, :, 0], group_id * tok_grp, tok_grp, 1)
        weights = lax.dynamic_slice_in_dim(route_weight[step, :, 0], group_id * tok_grp, tok_grp, 1)
        result = section_layer(
            current,
            gain_slice,
            up_weight[0, 0],
            down_weight[0, 0],
            chosen,
            weights,
            group_id,
            slice_id,
        )
        forward = from_behind(result[0], "pipe", 1)
        backward = from_behind(result[1], "pipe", -1)
        current = jnp.stack([forward, backward], axis=0)
    return current[None, :, None]


def solution(mesh):
    return jax.shard_map(
        shards,
        mesh=mesh,
        in_specs=(
            P("pipe", None, "expert", None, None),
            P("pipe", "expert", None, None),
            P("pipe", "expert", None, None),
            P("pipe", None),
            P(None, None, "pipe", None, None),
            P(None, None, "pipe", None, None),
        ),
        out_specs=P("pipe", None, "expert", None, None),
        check_vma=False,
    )
```

profile of v0, /device:TPU:1, one launch (start us, length us, event | category | flops | bytes accessed | tf_op | source)
XLA Modules:
  0.0 315.7 jit_solution(1641788946795150800)
XLA Ops:
  1.1 3.9 %collective-permute-start = (f32[2,16]{1,0:T(2,128)S(1)}, f32[2,16]{1,0:T(2,128)S(1)}, u32[]{:S(2)}, u32[]{:S(2)}) collective-permute-start(f32[2,16]{1,0:T(2,128)S(1)} %fusion.18), channel_id=1, source_target_pairs={{0,1},{1,0},{2,3},{3,2},{4,5},{5,4},{6,7},{7,6},{8,9},{9,8},{10,11... | collective-permute-start | bytes 392 | tf_op jit(solution)/shard_map/ppermute | solution.py:8
  6.7 4.4 %collective-permute-start.1 = (f32[2,16]{1,0:T(2,128)S(1)}, f32[2,16]{1,0:T(2,128)S(1)}, u32[]{:S(2)}, u32[]{:S(2)}) collective-permute-start(f32[2,16]{1,0:T(2,128)S(1)} %add.193), channel_id=1, source_target_pairs={{0,2},{1,3},{2,0},{3,1},{4,6},{5,7},{6,4},{7,5},{8,10},{9,11},{10,... | collective-permute-start | bytes 392 | tf_op jit(solution)/shard_map/ppermute | solution.py:8
  12.5 3.5 %collective-permute-start.2 = (f32[2,16]{1,0:T(2,128)S(1)}, f32[2,16]{1,0:T(2,128)S(1)}, u32[]{:S(2)}, u32[]{:S(2)}) collective-permute-start(f32[2,16]{1,0:T(2,128)S(1)} %add.194), channel_id=1, source_target_pairs={{0,4},{1,5},{2,6},{3,7},{4,0},{5,1},{6,2},{7,3},{8,12},{9,13},{10,... | collective-permute-start | bytes 392 | tf_op jit(solution)/shard_map/ppermute | solution.py:8
  18.1 4.9 %collective-permute-start.3 = (bf16[2,4,1,8,896]{4,3,1,0,2:T(8,128)(2,1)S(1)}, bf16[2,4,1,8,896]{4,3,1,0,2:T(8,128)(2,1)S(1)}, u32[]{:S(2)}, u32[]{:S(2)}) collective-permute-start(bf16[2,4,1,8,896]{4,3,1,0,2:T(8,128)(2,1)S(1)} %dynamic-slice_bitcast_fusion.11), channel_id=1, source_target_pairs={{0,8},{1,9},{2,10},{3,11},{4,12},{5,13},{6,14},{7,15},{8,0},{9,1},... | collective-permute-start | bytes 344072 | tf_op jit(solution)/shard_map/ppermute | solution.py:8
  23.0 2.2 collective-permute-done.3
  25.2 8.8 %collective-permute-start.4 = (bf16[2,2,2,8,896]{4,3,2,1,0:T(8,128)(2,1)S(1)}, bf16[2,2,2,8,896]{4,3,2,1,0:T(8,128)(2,1)S(1)}, u32[]{:S(2)}, u32[]{:S(2)}) collective-permute-start(bf16[2,2,2,8,896]{4,3,2,1,0:T(8,128)(2,1)S(1)} %dynamic-slice_bitcast_fusion.10), channel_id=1, source_target_pairs={{0,16},{1,17},{2,18},{3,19},{4,20},{5,21},{6,22},{7,23},{8,24},{9,... | collective-permute-start | bytes 344072 | tf_op jit(solution)/shard_map/ppermute | solution.py:8
  34.1 2.1 collective-permute-done.4
  36.3 17.3 %collective-permute-start.5 = (bf16[2,1,4,8,896]{4,3,2,0,1:T(8,128)(2,1)S(1)}, bf16[2,1,4,8,896]{4,3,2,0,1:T(8,128)(2,1)S(1)}, u32[]{:S(2)}, u32[]{:S(2)}) collective-permute-start(bf16[2,1,4,8,896]{4,3,2,0,1:T(8,128)(2,1)S(1)} %dynamic-slice_bitcast_fusion.9), channel_id=1, source_target_pairs={{0,32},{1,33},{2,34},{3,35},{4,36},{5,37},{6,38},{7,39},{8,40},{9,... | collective-permute-start | bytes 344072 | tf_op jit(solution)/shard_map/ppermute | solution.py:8
  53.6 2.2 collective-permute-done.5
  56.3 2.6 collective-permute-start.6
  59.0 4.7 %collective-permute-done.6 = f32[128,512]{1,0:T(8,128)S(1)} collective-permute-done((f32[128,512]{1,0:T(8,128)S(1)}, f32[128,512]{1,0:T(8,128)S(1)}, u32[]{:S(2)}, u32[]{:S(2)}) %collective-permute-start.6) | collective-permute-done | bytes 262176 | tf_op jit(solution)/shard_map/ppermute | solution.py:8
  63.8 4.4 %collective-permute-start.7 = (f32[128,256]{1,0:T(8,128)S(1)}, f32[128,256]{1,0:T(8,128)S(1)}, u32[]{:S(2)}, u32[]{:S(2)}) collective-permute-start(f32[128,256]{1,0:T(8,128)S(1)} %constant_dynamic-slice_fusion.6), channel_id=1, source_target_pairs={{0,2},{1,3},{2,0},{3,1},{4,6},{5,7},{6,4},{7,5},{8,10},{9,11},{10,... | collective-permute-start | bytes 393224 | tf_op jit(solution)/shard_map/ppermute | solution.py:8
  68.2 3.3 %collective-permute-done.7 = f32[128,256]{1,0:T(8,128)S(1)} collective-permute-done((f32[128,256]{1,0:T(8,128)S(1)}, f32[128,256]{1,0:T(8,128)S(1)}, u32[]{:S(2)}, u32[]{:S(2)}) %collective-permute-start.7) | collective-permute-done | bytes 131104 | tf_op jit(solution)/shard_map/ppermute | solution.py:8
  73.5 3.1 collective-permute-done.8
  78.6 2.9 collective-permute-done.9
  81.5 5.0 %collective-permute-start.10 = (bf16[128,256]{1,0:T(8,128)(2,1)S(1)}, bf16[128,256]{1,0:T(8,128)(2,1)S(1)}, u32[]{:S(2)}, u32[]{:S(2)}) collective-permute-start(bf16[128,256]{1,0:T(8,128)(2,1)S(1)} %constant_dynamic-update-slice_fusion.5), channel_id=1, source_target_pairs={{0,2},{1,3},{2,0},{3,1},{4,6},{5,7},{6,4},{7,5},{8,10},{9,11},{10,... | collective-permute-start | bytes 196616 | tf_op jit(solution)/shard_map/ppermute | solution.py:8
  91.5 3.6 %collective-permute-done.11 = bf16[128,512]{1,0:T(8,128)(2,1)S(1)} collective-permute-done((bf16[128,512]{1,0:T(8,128)(2,1)S(1)}, bf16[128,512]{1,0:T(8,128)(2,1)S(1)}, u32[]{:S(2)}, u32[]{:S(2)}) %collective-permute-start.11) | collective-permute-done | bytes 131104 | tf_op jit(solution)/shard_map/ppermute | solution.py:8
  95.1 2.0 fusion.8
  97.1 4.0 %collective-permute-start.12 = (bf16[2,4,1,8,896]{4,3,1,0,2:T(8,128)(2,1)S(1)}, bf16[2,4,1,8,896]{4,3,1,0,2:T(8,128)(2,1)S(1)}, u32[]{:S(2)}, u32[]{:S(2)}) collective-permute-start(bf16[2,4,1,8,896]{4,3,1,0,2:T(8,128)(2,1)S(1)} %dynamic-slice_bitcast_fusion.8), channel_id=1, source_target_pairs={{0,8},{1,9},{2,10},{3,11},{4,12},{5,13},{6,14},{7,15},{8,0},{9,1},... | collective-permute-start | bytes 344072 | tf_op jit(solution)/shard_map/ppermute | solution.py:8
  101.2 3.6 %collective-permute-done.12 = bf16[2,4,1,8,896]{4,3,1,0,2:T(8,128)(2,1)S(1)} collective-permute-done((bf16[2,4,1,8,896]{4,3,1,0,2:T(8,128)(2,1)S(1)}, bf16[2,4,1,8,896]{4,3,1,0,2:T(8,128)(2,1)S(1)}, u32[]{:S(2)}, u32[]{:S(2)}) %collective-permute-start.12) | collective-permute-done | bytes 114720 | tf_op jit(solution)/shard_map/ppermute | solution.py:8
  104.9 10.8 %collective-permute-start.13 = (bf16[2,2,2,8,896]{4,3,2,1,0:T(8,128)(2,1)S(1)}, bf16[2,2,2,8,896]{4,3,2,1,0:T(8,128)(2,1)S(1)}, u32[]{:S(2)}, u32[]{:S(2)}) collective-permute-start(bf16[2,2,2,8,896]{4,3,2,1,0:T(8,128)(2,1)S(1)} %dynamic-slice_bitcast_fusion.7), channel_id=1, source_target_pairs={{0,16},{1,17},{2,18},{3,19},{4,20},{5,21},{6,22},{7,23},{8,24},{9,... | collective-permute-start | bytes 344072 | tf_op jit(solution)/shard_map/ppermute | solution.py:8
  115.9 2.1 collective-permute-done.13
  118.1 11.5 %collective-permute-start.14 = (bf16[2,1,4,8,896]{4,3,2,0,1:T(8,128)(2,1)S(1)}, bf16[2,1,4,8,896]{4,3,2,0,1:T(8,128)(2,1)S(1)}, u32[]{:S(2)}, u32[]{:S(2)}) collective-permute-start(bf16[2,1,4,8,896]{4,3,2,0,1:T(8,128)(2,1)S(1)} %dynamic-slice_bitcast_fusion.6), channel_id=1, source_target_pairs={{0,32},{1,33},{2,34},{3,35},{4,36},{5,37},{6,38},{7,39},{8,40},{9,... | collective-permute-start | bytes 344072 | tf_op jit(solution)/shard_map/ppermute | solution.py:8
  129.6 2.8 collective-permute-done.14
  134.1 23.4 %collective-permute-start.15 = (bf16[16,896]{1,0:T(8,128)(2,1)S(1)}, bf16[16,896]{1,0:T(8,128)(2,1)S(1)}, u32[]{:S(2)}, u32[]{:S(2)}) collective-permute-start(bf16[16,896]{1,0:T(8,128)(2,1)S(1)} %get-tuple-element.13), channel_id=1, source_target_pairs={{0,64},{64,128},{128,192},{192,256},{256,320},{320,384},{384,448},... | collective-permute-start | bytes 86024 | tf_op jit(solution)/shard_map/ppermute | solution.py:14
  158.5 2.3 collective-permute-done.16
  160.9 2.6 collective-permute-start.17
  165.3 5.1 %collective-permute-start.18 = (f32[2,16]{1,0:T(2,128)S(1)}, f32[2,16]{1,0:T(2,128)S(1)}, u32[]{:S(2)}, u32[]{:S(2)}) collective-permute-start(f32[2,16]{1,0:T(2,128)S(1)} %add.220), channel_id=1, source_target_pairs={{0,2},{1,3},{2,0},{3,1},{4,6},{5,7},{6,4},{7,5},{8,10},{9,11},{10,... | collective-permute-start | bytes 392 | tf_op jit(solution)/shard_map/ppermute | solution.py:8
  171.3 2.5 collective-permute-start.19
  177.9 5.7 %collective-permute-done.20 = bf16[2,4,1,8,896]{4,3,1,0,2:T(8,128)(2,1)S(1)} collective-permute-done((bf16[2,4,1,8,896]{4,3,1,0,2:T(8,128)(2,1)S(1)}, bf16[2,4,1,8,896]{4,3,1,0,2:T(8,128)(2,1)S(1)}, u32[]{:S(2)}, u32[]{:S(2)}) %collective-permute-start.20) | collective-permute-done | bytes 114720 | tf_op jit(solution)/shard_map/ppermute | solution.py:8
  183.6 2.7 collective-permute-start.21
  186.3 13.9 %collective-permute-done.21 = bf16[2,2,2,8,896]{4,3,2,1,0:T(8,128)(2,1)S(1)} collective-permute-done((bf16[2,2,2,8,896]{4,3,2,1,0:T(8,128)(2,1)S(1)}, bf16[2,2,2,8,896]{4,3,2,1,0:T(8,128)(2,1)S(1)}, u32[]{:S(2)}, u32[]{:S(2)}) %collective-permute-start.21) | collective-permute-done | bytes 114720 | tf_op jit(solution)/shard_map/ppermute | solution.py:8
  200.3 13.7 %collective-permute-start.22 = (bf16[2,1,4,8,896]{4,3,2,0,1:T(8,128)(2,1)S(1)}, bf16[2,1,4,8,896]{4,3,2,0,1:T(8,128)(2,1)S(1)}, u32[]{:S(2)}, u32[]{:S(2)}) collective-permute-start(bf16[2,1,4,8,896]{4,3,2,0,1:T(8,128)(2,1)S(1)} %dynamic-slice_bitcast_fusion.3), channel_id=1, source_target_pairs={{0,32},{1,33},{2,34},{3,35},{4,36},{5,37},{6,38},{7,39},{8,40},{9,... | collective-permute-start | bytes 344072 | tf_op jit(solution)/shard_map/ppermute | solution.py:8
  214.0 8.5 %collective-permute-done.22 = bf16[2,1,4,8,896]{4,3,2,0,1:T(8,128)(2,1)S(1)} collective-permute-done((bf16[2,1,4,8,896]{4,3,2,0,1:T(8,128)(2,1)S(1)}, bf16[2,1,4,8,896]{4,3,2,0,1:T(8,128)(2,1)S(1)}, u32[]{:S(2)}, u32[]{:S(2)}) %collective-permute-start.22) | collective-permute-done | bytes 114720 | tf_op jit(solution)/shard_map/ppermute | solution.py:8
  223.1 2.1 collective-permute-start.23
  225.1 7.4 %collective-permute-done.23 = f32[128,512]{1,0:T(8,128)S(1)} collective-permute-done((f32[128,512]{1,0:T(8,128)S(1)}, f32[128,512]{1,0:T(8,128)S(1)}, u32[]{:S(2)}, u32[]{:S(2)}) %collective-permute-start.23) | collective-permute-done | bytes 262176 | tf_op jit(solution)/shard_map/ppermute | solution.py:8
  234.5 5.3 %collective-permute-done.24 = f32[128,256]{1,0:T(8,128)S(1)} collective-permute-done((f32[128,256]{1,0:T(8,128)S(1)}, f32[128,256]{1,0:T(8,128)S(1)}, u32[]{:S(2)}, u32[]{:S(2)}) %collective-permute-start.24) | collective-permute-done | bytes 131104 | tf_op jit(solution)/shard_map/ppermute | solution.py:8
  241.8 3.1 collective-permute-done.25
  246.8 2.7 collective-permute-done.26
  249.6 1.9 collective-permute-start.27
  251.5 4.6 %collective-permute-done.27 = bf16[128,256]{1,0:T(8,128)(2,1)S(1)} collective-permute-done((bf16[128,256]{1,0:T(8,128)(2,1)S(1)}, bf16[128,256]{1,0:T(8,128)(2,1)S(1)}, u32[]{:S(2)}, u32[]{:S(2)}) %collective-permute-start.27) | collective-permute-done | bytes 65568 | tf_op jit(solution)/shard_map/ppermute | solution.py:8
  256.1 2.1 collective-permute-start.28
  258.3 3.9 %collective-permute-done.28 = bf16[128,512]{1,0:T(8,128)(2,1)S(1)} collective-permute-done((bf16[128,512]{1,0:T(8,128)(2,1)S(1)}, bf16[128,512]{1,0:T(8,128)(2,1)S(1)}, u32[]{:S(2)}, u32[]{:S(2)}) %collective-permute-start.28) | collective-permute-done | bytes 131104 | tf_op jit(solution)/shard_map/ppermute | solution.py:8
  264.8 5.2 %collective-permute-done.29 = bf16[2,4,1,8,896]{4,3,1,0,2:T(8,128)(2,1)S(1)} collective-permute-done((bf16[2,4,1,8,896]{4,3,1,0,2:T(8,128)(2,1)S(1)}, bf16[2,4,1,8,896]{4,3,1,0,2:T(8,128)(2,1)S(1)}, u32[]{:S(2)}, u32[]{:S(2)}) %collective-permute-start.29) | collective-permute-done | bytes 114720 | tf_op jit(solution)/shard_map/ppermute | solution.py:8
  272.1 9.5 %collective-permute-done.30 = bf16[2,2,2,8,896]{4,3,2,1,0:T(8,128)(2,1)S(1)} collective-permute-done((bf16[2,2,2,8,896]{4,3,2,1,0:T(8,128)(2,1)S(1)}, bf16[2,2,2,8,896]{4,3,2,1,0:T(8,128)(2,1)S(1)}, u32[]{:S(2)}, u32[]{:S(2)}) %collective-permute-start.30) | collective-permute-done | bytes 114720 | tf_op jit(solution)/shard_map/ppermute | solution.py:8
  281.7 6.2 %collective-permute-start.31 = (bf16[2,1,4,8,896]{4,3,2,0,1:T(8,128)(2,1)S(1)}, bf16[2,1,4,8,896]{4,3,2,0,1:T(8,128)(2,1)S(1)}, u32[]{:S(2)}, u32[]{:S(2)}) collective-permute-start(bf16[2,1,4,8,896]{4,3,2,0,1:T(8,128)(2,1)S(1)} %dynamic-slice_bitcast_fusion), channel_id=1, source_target_pairs={{0,32},{1,33},{2,34},{3,35},{4,36},{5,37},{6,38},{7,39},{8,40},{9,... | collective-permute-start | bytes 344072 | tf_op jit(solution)/shard_map/ppermute | solution.py:8
  287.9 10.1 %collective-permute-done.31 = bf16[2,1,4,8,896]{4,3,2,0,1:T(8,128)(2,1)S(1)} collective-permute-done((bf16[2,1,4,8,896]{4,3,2,0,1:T(8,128)(2,1)S(1)}, bf16[2,1,4,8,896]{4,3,2,0,1:T(8,128)(2,1)S(1)}, u32[]{:S(2)}, u32[]{:S(2)}) %collective-permute-start.31) | collective-permute-done | bytes 114720 | tf_op jit(solution)/shard_map/ppermute | solution.py:8
  299.7 12.1 %collective-permute-start.32 = (bf16[16,896]{1,0:T(8,128)(2,1)S(1)}, bf16[16,896]{1,0:T(8,128)(2,1)S(1)}, u32[]{:S(2)}, u32[]{:S(2)}) collective-permute-start(bf16[16,896]{1,0:T(8,128)(2,1)S(1)} %get-tuple-element.11), channel_id=1, source_target_pairs={{0,64},{64,128},{128,192},{192,256},{256,320},{320,384},{384,448},... | collective-permute-start | bytes 86024 | tf_op jit(solution)/shard_map/ppermute | solution.py:14
  (144 shorter events, 42.3 us)
Async XLA Ops:
  0.0 55.9 %copy-start = (bf16[1,1,896,1024]{3,2,1,0:T(8,128)(2,1)S(1)}, bf16[1,1,896,1024]{3,2,1,0:T(8,128)(2,1)}, u32[]{:S(2)}) copy-start(bf16[1,1,896,1024]{3,2,1,0:T(8,128)(2,1)} %param.11) | copy-start | bytes 5505028
  1.1 5.6 %collective-permute-start = (f32[2,16]{1,0:T(2,128)S(1)}, f32[2,16]{1,0:T(2,128)S(1)}, u32[]{:S(2)}, u32[]{:S(2)}) collective-permute-start(f32[2,16]{1,0:T(2,128)S(1)} %fusion.18), channel_id=1, source_target_pairs={{0,1},{1,0},{2,3},{3,2},{4,5},{5,4},{6,7},{7,6},{8,9},{9,8},{10,11... | collective-permute-start | bytes 392 | tf_op jit(solution)/shard_map/ppermute | solution.py:8
  6.7 5.8 %collective-permute-start.1 = (f32[2,16]{1,0:T(2,128)S(1)}, f32[2,16]{1,0:T(2,128)S(1)}, u32[]{:S(2)}, u32[]{:S(2)}) collective-permute-start(f32[2,16]{1,0:T(2,128)S(1)} %add.193), channel_id=1, source_target_pairs={{0,2},{1,3},{2,0},{3,1},{4,6},{5,7},{6,4},{7,5},{8,10},{9,11},{10,... | collective-permute-start | bytes 392 | tf_op jit(solution)/shard_map/ppermute | solution.py:8
  12.5 4.5 %collective-permute-start.2 = (f32[2,16]{1,0:T(2,128)S(1)}, f32[2,16]{1,0:T(2,128)S(1)}, u32[]{:S(2)}, u32[]{:S(2)}) collective-permute-start(f32[2,16]{1,0:T(2,128)S(1)} %add.194), channel_id=1, source_target_pairs={{0,4},{1,5},{2,6},{3,7},{4,0},{5,1},{6,2},{7,3},{8,12},{9,13},{10,... | collective-permute-start | bytes 392 | tf_op jit(solution)/shard_map/ppermute | solution.py:8
  18.1 7.1 %collective-permute-start.3 = (bf16[2,4,1,8,896]{4,3,1,0,2:T(8,128)(2,1)S(1)}, bf16[2,4,1,8,896]{4,3,1,0,2:T(8,128)(2,1)S(1)}, u32[]{:S(2)}, u32[]{:S(2)}) collective-permute-start(bf16[2,4,1,8,896]{4,3,1,0,2:T(8,128)(2,1)S(1)} %dynamic-slice_bitcast_fusion.11), channel_id=1, source_target_pairs={{0,8},{1,9},{2,10},{3,11},{4,12},{5,13},{6,14},{7,15},{8,0},{9,1},... | collective-permute-start | bytes 344072 | tf_op jit(solution)/shard_map/ppermute | solution.py:8
  25.2 11.0 %collective-permute-start.4 = (bf16[2,2,2,8,896]{4,3,2,1,0:T(8,128)(2,1)S(1)}, bf16[2,2,2,8,896]{4,3,2,1,0:T(8,128)(2,1)S(1)}, u32[]{:S(2)}, u32[]{:S(2)}) collective-permute-start(bf16[2,2,2,8,896]{4,3,2,1,0:T(8,128)(2,1)S(1)} %dynamic-slice_bitcast_fusion.10), channel_id=1, source_target_pairs={{0,16},{1,17},{2,18},{3,19},{4,20},{5,21},{6,22},{7,23},{8,24},{9,... | collective-permute-start | bytes 344072 | tf_op jit(solution)/shard_map/ppermute | solution.py:8
  36.3 19.6 %collective-permute-start.5 = (bf16[2,1,4,8,896]{4,3,2,0,1:T(8,128)(2,1)S(1)}, bf16[2,1,4,8,896]{4,3,2,0,1:T(8,128)(2,1)S(1)}, u32[]{:S(2)}, u32[]{:S(2)}) collective-permute-start(bf16[2,1,4,8,896]{4,3,2,0,1:T(8,128)(2,1)S(1)} %dynamic-slice_bitcast_fusion.9), channel_id=1, source_target_pairs={{0,32},{1,33},{2,34},{3,35},{4,36},{5,37},{6,38},{7,39},{8,40},{9,... | collective-permute-start | bytes 344072 | tf_op jit(solution)/shard_map/ppermute | solution.py:8
  56.3 7.4 %collective-permute-start.6 = (f32[128,512]{1,0:T(8,128)S(1)}, f32[128,512]{1,0:T(8,128)S(1)}, u32[]{:S(2)}, u32[]{:S(2)}) collective-permute-start(f32[128,512]{1,0:T(8,128)S(1)} %constant_dynamic-slice_fusion.7), channel_id=1, source_target_pairs={{0,1},{1,0},{2,3},{3,2},{4,5},{5,4},{6,7},{7,6},{8,9},{9,8},{10,11... | collective-permute-start | bytes 786440 | tf_op jit(solution)/shard_map/ppermute | solution.py:8
  63.8 7.7 %collective-permute-start.7 = (f32[128,256]{1,0:T(8,128)S(1)}, f32[128,256]{1,0:T(8,128)S(1)}, u32[]{:S(2)}, u32[]{:S(2)}) collective-permute-start(f32[128,256]{1,0:T(8,128)S(1)} %constant_dynamic-slice_fusion.6), channel_id=1, source_target_pairs={{0,2},{1,3},{2,0},{3,1},{4,6},{5,7},{6,4},{7,5},{8,10},{9,11},{10,... | collective-permute-start | bytes 393224 | tf_op jit(solution)/shard_map/ppermute | solution.py:8
  71.5 5.0 %collective-permute-start.8 = (f32[128,128]{1,0:T(8,128)S(1)}, f32[128,128]{1,0:T(8,128)S(1)}, u32[]{:S(2)}, u32[]{:S(2)}) collective-permute-start(f32[128,128]{1,0:T(8,128)S(1)} %constant_dynamic-slice_fusion.5), channel_id=1, source_target_pairs={{0,4},{1,5},{2,6},{3,7},{4,0},{5,1},{6,2},{7,3},{8,12},{9,13},{10,... | collective-permute-start | bytes 196616 | tf_op jit(solution)/shard_map/ppermute | solution.py:8
  76.6 5.0 %collective-permute-start.9 = (bf16[128,128]{1,0:T(8,128)(2,1)S(1)}, bf16[128,128]{1,0:T(8,128)(2,1)S(1)}, u32[]{:S(2)}, u32[]{:S(2)}) collective-permute-start(bf16[128,128]{1,0:T(8,128)(2,1)S(1)} %multiply_convert_fusion.1), channel_id=1, source_target_pairs={{0,4},{1,5},{2,6},{3,7},{4,0},{5,1},{6,2},{7,3},{8,12},{9,13},{10,... | collective-permute-start | bytes 98312 | tf_op jit(solution)/shard_map/ppermute | solution.py:8
  81.5 7.8 %collective-permute-start.10 = (bf16[128,256]{1,0:T(8,128)(2,1)S(1)}, bf16[128,256]{1,0:T(8,128)(2,1)S(1)}, u32[]{:S(2)}, u32[]{:S(2)}) collective-permute-start(bf16[128,256]{1,0:T(8,128)(2,1)S(1)} %constant_dynamic-update-slice_fusion.5), channel_id=1, source_target_pairs={{0,2},{1,3},{2,0},{3,1},{4,6},{5,7},{6,4},{7,5},{8,10},{9,11},{10,... | collective-permute-start | bytes 196616 | tf_op jit(solution)/shard_map/ppermute | solution.py:8
  89.1 12.0 %copy-start.3 = (f32[2,2,1,128,2]{3,4,2,1,0:T(2,128)S(1)}, f32[2,2,1,128,2]{3,4,2,1,0:T(2,128)}, u32[]{:S(2)}) copy-start(f32[2,2,1,128,2]{3,4,2,1,0:T(2,128)} %param.15) | copy-start | bytes 12292
  89.4 5.7 %collective-permute-start.11 = (bf16[128,512]{1,0:T(8,128)(2,1)S(1)}, bf16[128,512]{1,0:T(8,128)(2,1)S(1)}, u32[]{:S(2)}, u32[]{:S(2)}) collective-permute-start(bf16[128,512]{1,0:T(8,128)(2,1)S(1)} %constant_dynamic-update-slice_fusion.4), channel_id=1, source_target_pairs={{0,1},{1,0},{2,3},{3,2},{4,5},{5,4},{6,7},{7,6},{8,9},{9,8},{10,11... | collective-permute-start | bytes 393224 | tf_op jit(solution)/shard_map/ppermute | solution.py:8
  97.1 37.0 %copy-start.2 = (bf16[1,2,1,16,896]{4,3,2,1,0:T(8,128)(2,1)S(1)}, bf16[1,2,1,16,896]{4,3,2,1,0:T(8,128)(2,1)}, u32[]{:S(2)}) copy-start(bf16[1,2,1,16,896]{4,3,2,1,0:T(8,128)(2,1)} %param.10) | copy-start | bytes 172036
  97.1 7.7 %collective-permute-start.12 = (bf16[2,4,1,8,896]{4,3,1,0,2:T(8,128)(2,1)S(1)}, bf16[2,4,1,8,896]{4,3,1,0,2:T(8,128)(2,1)S(1)}, u32[]{:S(2)}, u32[]{:S(2)}) collective-permute-start(bf16[2,4,1,8,896]{4,3,1,0,2:T(8,128)(2,1)S(1)} %dynamic-slice_bitcast_fusion.8), channel_id=1, source_target_pairs={{0,8},{1,9},{2,10},{3,11},{4,12},{5,13},{6,14},{7,15},{8,0},{9,1},... | collective-permute-start | bytes 344072 | tf_op jit(solution)/shard_map/ppermute | solution.py:8
  104.9 13.2 %collective-permute-start.13 = (bf16[2,2,2,8,896]{4,3,2,1,0:T(8,128)(2,1)S(1)}, bf16[2,2,2,8,896]{4,3,2,1,0:T(8,128)(2,1)S(1)}, u32[]{:S(2)}, u32[]{:S(2)}) collective-permute-start(bf16[2,2,2,8,896]{4,3,2,1,0:T(8,128)(2,1)S(1)} %dynamic-slice_bitcast_fusion.7), channel_id=1, source_target_pairs={{0,16},{1,17},{2,18},{3,19},{4,20},{5,21},{6,22},{7,23},{8,24},{9,... | collective-permute-start | bytes 344072 | tf_op jit(solution)/shard_map/ppermute | solution.py:8
  118.1 14.3 %collective-permute-start.14 = (bf16[2,1,4,8,896]{4,3,2,0,1:T(8,128)(2,1)S(1)}, bf16[2,1,4,8,896]{4,3,2,0,1:T(8,128)(2,1)S(1)}, u32[]{:S(2)}, u32[]{:S(2)}) collective-permute-start(bf16[2,1,4,8,896]{4,3,2,0,1:T(8,128)(2,1)S(1)} %dynamic-slice_bitcast_fusion.6), channel_id=1, source_target_pairs={{0,32},{1,33},{2,34},{3,35},{4,36},{5,37},{6,38},{7,39},{8,40},{9,... | collective-permute-start | bytes 344072 | tf_op jit(solution)/shard_map/ppermute | solution.py:8
  134.1 24.4 %collective-permute-start.15 = (bf16[16,896]{1,0:T(8,128)(2,1)S(1)}, bf16[16,896]{1,0:T(8,128)(2,1)S(1)}, u32[]{:S(2)}, u32[]{:S(2)}) collective-permute-start(bf16[16,896]{1,0:T(8,128)(2,1)S(1)} %get-tuple-element.13), channel_id=1, source_target_pairs={{0,64},{64,128},{128,192},{192,256},{256,320},{320,384},{384,448},... | collective-permute-start | bytes 86024 | tf_op jit(solution)/shard_map/ppermute | solution.py:14
  157.6 3.3 %collective-permute-start.16 = (bf16[16,896]{1,0:T(8,128)(2,1)S(1)}, bf16[16,896]{1,0:T(8,128)(2,1)S(1)}, u32[]{:S(2)}, u32[]{:S(2)}) collective-permute-start(bf16[16,896]{1,0:T(8,128)(2,1)S(1)} %get-tuple-element.14), channel_id=1, source_target_pairs={{0,448},{64,0},{128,64},{192,128},{256,192},{320,256},{384,320},{4... | collective-permute-start | bytes 86024 | tf_op jit(solution)/shard_map/ppermute | solution.py:14
  160.9 4.3 %collective-permute-start.17 = (f32[2,16]{1,0:T(2,128)S(1)}, f32[2,16]{1,0:T(2,128)S(1)}, u32[]{:S(2)}, u32[]{:S(2)}) collective-permute-start(f32[2,16]{1,0:T(2,128)S(1)} %fusion.14), channel_id=1, source_target_pairs={{0,1},{1,0},{2,3},{3,2},{4,5},{5,4},{6,7},{7,6},{8,9},{9,8},{10,11... | collective-permute-start | bytes 392 | tf_op jit(solution)/shard_map/ppermute | solution.py:8
  165.3 6.1 %collective-permute-start.18 = (f32[2,16]{1,0:T(2,128)S(1)}, f32[2,16]{1,0:T(2,128)S(1)}, u32[]{:S(2)}, u32[]{:S(2)}) collective-permute-start(f32[2,16]{1,0:T(2,128)S(1)} %add.220), channel_id=1, source_target_pairs={{0,2},{1,3},{2,0},{3,1},{4,6},{5,7},{6,4},{7,5},{8,10},{9,11},{10,... | collective-permute-start | bytes 392 | tf_op jit(solution)/shard_map/ppermute | solution.py:8
  171.3 4.3 %collective-permute-start.19 = (f32[2,16]{1,0:T(2,128)S(1)}, f32[2,16]{1,0:T(2,128)S(1)}, u32[]{:S(2)}, u32[]{:S(2)}) collective-permute-start(f32[2,16]{1,0:T(2,128)S(1)} %add.221), channel_id=1, source_target_pairs={{0,4},{1,5},{2,6},{3,7},{4,0},{5,1},{6,2},{7,3},{8,12},{9,13},{10,... | collective-permute-start | bytes 392 | tf_op jit(solution)/shard_map/ppermute | solution.py:8
  175.9 7.7 %collective-permute-start.20 = (bf16[2,4,1,8,896]{4,3,1,0,2:T(8,128)(2,1)S(1)}, bf16[2,4,1,8,896]{4,3,1,0,2:T(8,128)(2,1)S(1)}, u32[]{:S(2)}, u32[]{:S(2)}) collective-permute-start(bf16[2,4,1,8,896]{4,3,1,0,2:T(8,128)(2,1)S(1)} %dynamic-slice_bitcast_fusion.5), channel_id=1, source_target_pairs={{0,8},{1,9},{2,10},{3,11},{4,12},{5,13},{6,14},{7,15},{8,0},{9,1},... | collective-permute-start | bytes 344072 | tf_op jit(solution)/shard_map/ppermute | solution.py:8
  183.6 16.6 %collective-permute-start.21 = (bf16[2,2,2,8,896]{4,3,2,1,0:T(8,128)(2,1)S(1)}, bf16[2,2,2,8,896]{4,3,2,1,0:T(8,128)(2,1)S(1)}, u32[]{:S(2)}, u32[]{:S(2)}) collective-permute-start(bf16[2,2,2,8,896]{4,3,2,1,0:T(8,128)(2,1)S(1)} %dynamic-slice_bitcast_fusion.4), channel_id=1, source_target_pairs={{0,16},{1,17},{2,18},{3,19},{4,20},{5,21},{6,22},{7,23},{8,24},{9,... | collective-permute-start | bytes 344072 | tf_op jit(solution)/shard_map/ppermute | solution.py:8
  200.3 22.3 %collective-permute-start.22 = (bf16[2,1,4,8,896]{4,3,2,0,1:T(8,128)(2,1)S(1)}, bf16[2,1,4,8,896]{4,3,2,0,1:T(8,128)(2,1)S(1)}, u32[]{:S(2)}, u32[]{:S(2)}) collective-permute-start(bf16[2,1,4,8,896]{4,3,2,0,1:T(8,128)(2,1)S(1)} %dynamic-slice_bitcast_fusion.3), channel_id=1, source_target_pairs={{0,32},{1,33},{2,34},{3,35},{4,36},{5,37},{6,38},{7,39},{8,40},{9,... | collective-permute-start | bytes 344072 | tf_op jit(solution)/shard_map/ppermute | solution.py:8
  223.0 39.1 %copy-start.1 = (bf16[1,1,1024,896]{3,2,1,0:T(8,128)(2,1)S(1)}, bf16[1,1,1024,896]{3,2,1,0:T(8,128)(2,1)}, u32[]{:S(2)}) copy-start(bf16[1,1,1024,896]{3,2,1,0:T(8,128)(2,1)} %param.12) | copy-start | bytes 5505028
  223.1 9.4 %collective-permute-start.23 = (f32[128,512]{1,0:T(8,128)S(1)}, f32[128,512]{1,0:T(8,128)S(1)}, u32[]{:S(2)}, u32[]{:S(2)}) collective-permute-start(f32[128,512]{1,0:T(8,128)S(1)} %constant_dynamic-slice_fusion.2), channel_id=1, source_target_pairs={{0,1},{1,0},{2,3},{3,2},{4,5},{5,4},{6,7},{7,6},{8,9},{9,8},{10,11... | collective-permute-start | bytes 786440 | tf_op jit(solution)/shard_map/ppermute | solution.py:8
  232.6 7.2 %collective-permute-start.24 = (f32[128,256]{1,0:T(8,128)S(1)}, f32[128,256]{1,0:T(8,128)S(1)}, u32[]{:S(2)}, u32[]{:S(2)}) collective-permute-start(f32[128,256]{1,0:T(8,128)S(1)} %constant_dynamic-slice_fusion.1), channel_id=1, source_target_pairs={{0,2},{1,3},{2,0},{3,1},{4,6},{5,7},{6,4},{7,5},{8,10},{9,11},{10,... | collective-permute-start | bytes 393224 | tf_op jit(solution)/shard_map/ppermute | solution.py:8
  239.8 5.0 %collective-permute-start.25 = (f32[128,128]{1,0:T(8,128)S(1)}, f32[128,128]{1,0:T(8,128)S(1)}, u32[]{:S(2)}, u32[]{:S(2)}) collective-permute-start(f32[128,128]{1,0:T(8,128)S(1)} %constant_dynamic-slice_fusion), channel_id=1, source_target_pairs={{0,4},{1,5},{2,6},{3,7},{4,0},{5,1},{6,2},{7,3},{8,12},{9,13},{10,... | collective-permute-start | bytes 196616 | tf_op jit(solution)/shard_map/ppermute | solution.py:8
  244.9 4.7 %collective-permute-start.26 = (bf16[128,128]{1,0:T(8,128)(2,1)S(1)}, bf16[128,128]{1,0:T(8,128)(2,1)S(1)}, u32[]{:S(2)}, u32[]{:S(2)}) collective-permute-start(bf16[128,128]{1,0:T(8,128)(2,1)S(1)} %multiply_convert_fusion), channel_id=1, source_target_pairs={{0,4},{1,5},{2,6},{3,7},{4,0},{5,1},{6,2},{7,3},{8,12},{9,13},{10,... | collective-permute-start | bytes 98312 | tf_op jit(solution)/shard_map/ppermute | solution.py:8
  249.6 6.5 %collective-permute-start.27 = (bf16[128,256]{1,0:T(8,128)(2,1)S(1)}, bf16[128,256]{1,0:T(8,128)(2,1)S(1)}, u32[]{:S(2)}, u32[]{:S(2)}) collective-permute-start(bf16[128,256]{1,0:T(8,128)(2,1)S(1)} %constant_dynamic-update-slice_fusion.2), channel_id=1, source_target_pairs={{0,2},{1,3},{2,0},{3,1},{4,6},{5,7},{6,4},{7,5},{8,10},{9,11},{10,... | collective-permute-start | bytes 196616 | tf_op jit(solution)/shard_map/ppermute | solution.py:8
  256.1 6.0 %collective-permute-start.28 = (bf16[128,512]{1,0:T(8,128)(2,1)S(1)}, bf16[128,512]{1,0:T(8,128)(2,1)S(1)}, u32[]{:S(2)}, u32[]{:S(2)}) collective-permute-start(bf16[128,512]{1,0:T(8,128)(2,1)S(1)} %constant_dynamic-update-slice_fusion.1), channel_id=1, source_target_pairs={{0,1},{1,0},{2,3},{3,2},{4,5},{5,4},{6,7},{7,6},{8,9},{9,8},{10,11... | collective-permute-start | bytes 393224 | tf_op jit(solution)/shard_map/ppermute | solution.py:8
  262.7 7.3 %collective-permute-start.29 = (bf16[2,4,1,8,896]{4,3,1,0,2:T(8,128)(2,1)S(1)}, bf16[2,4,1,8,896]{4,3,1,0,2:T(8,128)(2,1)S(1)}, u32[]{:S(2)}, u32[]{:S(2)}) collective-permute-start(bf16[2,4,1,8,896]{4,3,1,0,2:T(8,128)(2,1)S(1)} %dynamic-slice_bitcast_fusion.2), channel_id=1, source_target_pairs={{0,8},{1,9},{2,10},{3,11},{4,12},{5,13},{6,14},{7,15},{8,0},{9,1},... | collective-permute-start | bytes 344072 | tf_op jit(solution)/shard_map/ppermute | solution.py:8
  270.0 11.6 %collective-permute-start.30 = (bf16[2,2,2,8,896]{4,3,2,1,0:T(8,128)(2,1)S(1)}, bf16[2,2,2,8,896]{4,3,2,1,0:T(8,128)(2,1)S(1)}, u32[]{:S(2)}, u32[]{:S(2)}) collective-permute-start(bf16[2,2,2,8,896]{4,3,2,1,0:T(8,128)(2,1)S(1)} %dynamic-slice_bitcast_fusion.1), channel_id=1, source_target_pairs={{0,16},{1,17},{2,18},{3,19},{4,20},{5,21},{6,22},{7,23},{8,24},{9,... | collective-permute-start | bytes 344072 | tf_op jit(solution)/shard_map/ppermute | solution.py:8
  281.7 16.3 %collective-permute-start.31 = (bf16[2,1,4,8,896]{4,3,2,0,1:T(8,128)(2,1)S(1)}, bf16[2,1,4,8,896]{4,3,2,0,1:T(8,128)(2,1)S(1)}, u32[]{:S(2)}, u32[]{:S(2)}) collective-permute-start(bf16[2,1,4,8,896]{4,3,2,0,1:T(8,128)(2,1)S(1)} %dynamic-slice_bitcast_fusion), channel_id=1, source_target_pairs={{0,32},{1,33},{2,34},{3,35},{4,36},{5,37},{6,38},{7,39},{8,40},{9,... | collective-permute-start | bytes 344072 | tf_op jit(solution)/shard_map/ppermute | solution.py:8
  299.7 13.6 %collective-permute-start.32 = (bf16[16,896]{1,0:T(8,128)(2,1)S(1)}, bf16[16,896]{1,0:T(8,128)(2,1)S(1)}, u32[]{:S(2)}, u32[]{:S(2)}) collective-permute-start(bf16[16,896]{1,0:T(8,128)(2,1)S(1)} %get-tuple-element.11), channel_id=1, source_target_pairs={{0,64},{64,128},{128,192},{192,256},{256,320},{320,384},{384,448},... | collective-permute-start | bytes 86024 | tf_op jit(solution)/shard_map/ppermute | solution.py:14
  311.8 3.3 %collective-permute-start.33 = (bf16[16,896]{1,0:T(8,128)(2,1)S(1)}, bf16[16,896]{1,0:T(8,128)(2,1)S(1)}, u32[]{:S(2)}, u32[]{:S(2)}) collective-permute-start(bf16[16,896]{1,0:T(8,128)(2,1)S(1)} %get-tuple-element.12), channel_id=1, source_target_pairs={{0,448},{64,0},{128,64},{192,128},{256,192},{320,256},{384,320},{4... | collective-permute-start | bytes 86024 | tf_op jit(solution)/shard_map/ppermute | solution.py:14
where the time goes:
time: 318 us; the launch traced here: 316 us
  starting transfers between devices  174 us (55%)
  waiting for transfers between devices  125 us (39%)
  local copies, waits for them, and re-layouts  8.14 us (3%)
  matrix products  4.66 us (1%)
  other arithmetic  3.24 us (1%)
    ppermute x30, starting transfers between devices, swapped(): lax.ppermute(value, axis, [(i, i ^ 1 << stride) for i in range(lax.axis_s...  137 us
    ppermute x30, waiting for transfers between devices, swapped(): lax.ppermute(value, axis, [(i, i ^ 1 << stride) for i in range(lax.axis_s...  119 us
    ppermute x4, starting transfers between devices, from_behind(): return lax.ppermute(value, axis, pairs)  36.4 us
  transfers between devices with their start and end apart: 34, of which 32 were waited for; matrix products, arithmetic and copies ran while one was open for 2% of the time, Pallas kernels for 0%

commit v1 on v0

v1 whole, which is shorter than its diff:
```python
import jax
import jax.numpy as jnp
from jax import lax
from jax.sharding import PartitionSpec as P

GROUPS = 8
SLICES = 8
CAP = 8


def over_groups(value):
    members = [[g * SLICES + s for g in range(GROUPS)] for s in range(SLICES)]
    return lax.all_to_all(value, "expert", 0, 0, axis_index_groups=members, tiled=True)


def over_slices(value):
    members = [[g * SLICES + s for s in range(SLICES)] for g in range(GROUPS)]
    return lax.all_to_all(value, "expert", 0, 0, axis_index_groups=members, tiled=True)


def shifted(value, steps):
    count = lax.axis_size("pipe")
    return lax.ppermute(value, "pipe", [(i, (i + steps) % count) for i in range(count)])


def slot_matrices(chosen, weights):
    streams, tokens, _ = chosen.shape
    expert_ids = jnp.arange(GROUPS, dtype=jnp.int32)
    matches = chosen[:, :, :, None] == expert_ids
    hits = jnp.sum(matches.astype(jnp.int32), axis=2)
    ranks = jnp.cumsum(hits, axis=1) - hits
    mixw = jnp.sum(jnp.where(matches, weights[..., None], 0.0), axis=2)
    slot_ids = jnp.arange(CAP, dtype=jnp.int32)
    placed = (hits[..., None] == 1) & (ranks[..., None] == slot_ids)
    same = jnp.eye(streams, dtype=jnp.bool_)
    full = placed[:, :, :, None, :] & same[:, None, None, :, None]
    full = full.reshape(streams * tokens, GROUPS * streams * CAP)
    mixed = jnp.broadcast_to(
        mixw[:, :, :, None, None], (streams, tokens, GROUPS, streams, CAP)
    ).reshape(full.shape)
    return full.astype(jnp.bfloat16), jnp.where(full, mixed, 0.0)


def shards(state, up_weight, down_weight, norm_gain, routes, route_weight):
    expert_index = lax.axis_index("expert")
    group_id = expert_index // SLICES
    slice_id = expert_index % SLICES
    streams, tokens, width = state.shape[1], state.shape[3], state.shape[4]
    features = width * SLICES
    up, down = up_weight[0, 0], down_weight[0, 0]
    hidden_width = up.shape[1]
    gain = lax.dynamic_slice_in_dim(norm_gain[0], slice_id * width, width, 0)
    lane = jnp.arange(128)
    current = state[0, :, 0].reshape(streams * tokens, width)
    slots = streams * CAP
    for step in range(routes.shape[0]):
        chosen = lax.dynamic_slice_in_dim(routes[step, :, 0], group_id * tokens, tokens, 1)
        weights = lax.dynamic_slice_in_dim(route_weight[step, :, 0], group_id * tokens, tokens, 1)
        placed, mix = slot_matrices(chosen, weights)
        outgoing = lax.dot_general(
            placed, current, (((0,), (0,)), ((), ())), preferred_element_type=jnp.float32
        ).astype(jnp.bfloat16)
        rows = over_groups(outgoing.reshape(GROUPS, slots, width)).reshape(GROUPS * slots, width)
        rows_f = rows.astype(jnp.float32)
        squares = jnp.sum(rows_f * rows_f, axis=1, keepdims=True)
        scaled = (rows_f * gain).astype(jnp.bfloat16)
        partial = jnp.dot(scaled, up, preferred_element_type=jnp.float32).astype(jnp.bfloat16)
        high = lax.reduce_precision(squares, 8, 7)
        tail = jnp.where(lane == 0, high, jnp.where(lane == 1, squares - high, 0.0))
        sent = jnp.concatenate([partial, tail.astype(jnp.bfloat16)], axis=1)
        parts = over_slices(sent.reshape(SLICES, slots, hidden_width + 128)).astype(jnp.float32)
        total = jnp.sum(parts, axis=0)
        summed = total[:, hidden_width : hidden_width + 1] + total[:, hidden_width + 1 : hidden_width + 2]
        value = total[:, :hidden_width] * lax.rsqrt(summed / features + 1e-06)
        active = jax.nn.silu(value).astype(jnp.bfloat16)
        hidden = over_slices(jnp.broadcast_to(active, (SLICES, slots, hidden_width)))
        produced = jnp.dot(
            hidden.reshape(GROUPS * slots, hidden_width), down, preferred_element_type=jnp.float32
        ).astype(jnp.bfloat16)
        returned = over_groups(produced.reshape(GROUPS, slots, width)).reshape(GROUPS * slots, width)
        added = jnp.dot(
            mix,
            returned.astype(jnp.float32),
            precision=lax.Precision.HIGHEST,
            preferred_element_type=jnp.float32,
        )
        result = (current.astype(jnp.float32) + added).astype(jnp.bfloat16)
        forward = shifted(result[:tokens], 1)
        backward = shifted(result[tokens:], -1)
        current = jnp.concatenate([forward, backward], axis=0)
    return current.reshape(1, streams, 1, tokens, width)


def solution(mesh):
    return jax.shard_map(
        shards,
        mesh=mesh,
        in_specs=(
            P("pipe", None, "expert", None, None),
            P("pipe", "expert", None, None),
            P("pipe", "expert", None, None),
            P("pipe", None),
            P(None, None, "pipe", None, None),
            P(None, None, "pipe", None, None),
        ),
        out_specs=P("pipe", None, "expert", None, None),
        check_vma=False,
    )
```

time: 318 us -> 164 us (0.52)
  starting transfers between devices: 174 us -> 37.7 us
  waiting for transfers between devices: 125 us -> 53.2 us
  blocking collectives: 0 us -> 60.9 us
  local copies, waits for them, and re-layouts: 8.14 us -> 2.73 us
    ppermute x34 -> x4, starting transfers between devices: 174 us -> 10.9 us  [shifted(): lax.ppermute(value, 'pipe', [(i, (i + steps) % count) for i in range(coun...]
    ppermute x34 -> x4, waiting for transfers between devices: 125 us -> 6.86 us  [shifted(): lax.ppermute(value, 'pipe', [(i, (i + steps) % count) for i in range(coun...]
    all_to_all x0 -> x5, blocking collectives: none -> 60.9 us  [the longest x4 38.2 us: over_slices(): lax.all_to_all(value, 'expert', 0, 0, axis_index_groups=members, tiled=True)]
    all_to_all x0 -> x3, waiting for transfers between devices: none -> 46.3 us  [over_groups(): lax.all_to_all(value, 'expert', 0, 0, axis_index_groups=members, tiled=True)]
    all_to_all x0 -> x3, starting transfers between devices: none -> 26.8 us  [over_groups(): lax.all_to_all(value, 'expert', 0, 0, axis_index_groups=members, tiled=True)]
    gather x14 -> x0, local copies, waits for them, and re-layouts: 4.92 us -> none  [the longest x10 2.6 us: section_layer(): choice_rank = jnp.take_along_axis(ranks, chosen, axis=2)]
  transfers between devices with their start and end apart: 34 -> 7, of which waited for: 32 -> 7; matrix products, arithmetic and copies ran while one was open for 2% -> 1% of each run, Pallas kernels for 0% -> 0%
where the time goes in v1:
time: 164 us; the launch traced here: 163 us
  blocking collectives  60.9 us (37%)
  waiting for transfers between devices  53.2 us (32%)
  starting transfers between devices  37.7 us (23%)
  matrix products  5.61 us (3%)
  local copies, waits for them, and re-layouts  2.73 us (2%)
  other arithmetic  2.48 us (2%)
    all_to_all x3, waiting for transfers between devices, over_groups(): lax.all_to_all(value, 'expert', 0, 0, axis_index_groups=members, tiled=True)  46.3 us
    all_to_all x4, blocking collectives, over_slices(): lax.all_to_all(value, 'expert', 0, 0, axis_index_groups=members, tiled=True)  38.2 us
    all_to_all x3, starting transfers between devices, over_groups(): lax.all_to_all(value, 'expert', 0, 0, axis_index_groups=members, tiled=True)  26.8 us
    all_to_all x1, blocking collectives, over_groups(): lax.all_to_all(value, 'expert', 0, 0, axis_index_groups=members, tiled=True)  22.6 us
    ppermute x4, starting transfers between devices, shifted(): lax.ppermute(value, 'pipe', [(i, (i + steps) % count) for i in range(coun...  10.9 us
    ppermute x4, waiting for transfers between devices, shifted(): lax.ppermute(value, 'pipe', [(i, (i + steps) % count) for i in range(coun...  6.86 us
  transfers between devices with their start and end apart: 7, of which 7 were waited for; matrix products, arithmetic and copies ran while one was open for 1% of the time, Pallas kernels for 0%

profile of v1, /device:TPU:1, one launch (start us, length us, event | category | flops | bytes accessed | tf_op | source)
XLA Modules:
  0.0 162.9 jit_solution(8178342435347853891)
XLA Ops:
  0.0 0.8 fusion.35
  0.9 0.1 dynamic-slice_bitcast_fusion.1
  1.2 0.1 copy.46
  1.3 0.1 copy.51
  1.5 0.2 broadcast_and_fusion.1
  1.7 0.1 and.95
  1.8 1.7 %convolution_convert_fusion.1 = bf16[128,896]{1,0:T(8,128)(2,1)} fusion(pred[32,128]{0,1:T(32,128)(4,1)S(1)} %and.95, bf16[32,896]{1,0:T(8,128)(2,1)} %bitcast.71), kind=kOutput, calls=%fused_computation.13 | convolution fusion | flops 7454720 | bytes 290816 | tf_op jit(solution)/shard_map/dot_general | solution.py:60
  3.5 15.6 %all-to-all-start = ((bf16[8,16,896]{2,1,0:T(8,128)(2,1)}), bf16[8,16,896]{2,1,0:T(8,128)(2,1)S(1)}, u32[]{:S(2)}, u32[]{:S(2)}) async-start(bf16[8,16,896]{2,1,0:T(8,128)(2,1)} %bitcast.3), calls=%async_computation | async-start | bytes 458752 | tf_op jit(solution)/shard_map/all_to_all | solution.py:13
  19.1 0.7 dynamic-slice_reduce_fusion
  19.9 15.0 %all-to-all-done = bf16[8,16,896]{2,1,0:T(8,128)(2,1)S(1)} async-done(((bf16[8,16,896]{2,1,0:T(8,128)(2,1)}), bf16[8,16,896]{2,1,0:T(8,128)(2,1)S(1)}, u32[]{:S(2)}, u32[]{:S(2)}) %all-to-all-start) | async-done | bytes 229408 | tf_op jit(solution)/shard_map/all_to_all | solution.py:13
  34.8 0.1 fusion.21
  35.0 0.1 reduce_sum.79
  35.1 0.4 fusion.8
  35.5 0.1 select_convert_fusion.1
  35.7 11.2 %all_to_all.40 = bf16[8,16,1152]{2,1,0:T(8,128)(2,1)S(1)} all-to-all(bf16[8,16,1152]{2,1,0:T(8,128)(2,1)S(1)} %bitcast.62), channel_id=1, replica_groups={{0,1,2,3,4,5,6,7},{8,9,10,11,12,13,14,15},{16,17,18,19,20,21,22,23},{24..., dimensions={0} | all-to-all | bytes 589824 | tf_op jit(solution)/shard_map/all_to_all | solution.py:18
  46.9 0.2 fusion.32
  47.1 0.1 multiply_convert_fusion.1
  47.2 8.5 %all_to_all.41 = bf16[8,16,1024]{2,1,0:T(8,128)(2,1)S(1)} all-to-all(bf16[8,16,1024]{2,1,0:T(8,128)(2,1)S(1)} %broadcast_in_dim.120), channel_id=1, replica_groups={{0,1,2,3,4,5,6,7},{8,9,10,11,12,13,14,15},{16,17,18,19,20,21,22,23},{24..., dimensions={0} | all-to-all | bytes 524288 | tf_op jit(solution)/shard_map/all_to_all | solution.py:18
  55.7 1.1 fusion.14
  56.9 7.8 %all-to-all-start.3 = ((bf16[8,16,896]{2,1,0:T(8,128)(2,1)}), bf16[8,16,896]{2,1,0:T(8,128)(2,1)S(1)}, u32[]{:S(2)}, u32[]{:S(2)}) async-start(bf16[8,16,896]{2,1,0:T(8,128)(2,1)} %bitcast.9), calls=%async_computation.3 | async-start | bytes 458752 | tf_op jit(solution)/shard_map/all_to_all | solution.py:13
  64.7 0.1 dynamic-slice_bitcast_fusion
  64.8 0.2 broadcast_select_fusion.1
  65.0 0.1 select_n.70
  65.1 14.7 %all-to-all-done.3 = bf16[8,16,896]{2,1,0:T(8,128)(2,1)S(1)} async-done(((bf16[8,16,896]{2,1,0:T(8,128)(2,1)}), bf16[8,16,896]{2,1,0:T(8,128)(2,1)S(1)}, u32[]{:S(2)}, u32[]{:S(2)}) %all-to-all-start.3) | async-done | bytes 229408 | tf_op jit(solution)/shard_map/all_to_all | solution.py:13
  79.8 0.3 fusion.20
  80.1 6.6 %collective-permute-start = (bf16[16,896]{1,0:T(8,128)(2,1)S(1)}, bf16[16,896]{1,0:T(8,128)(2,1)S(1)}, u32[]{:S(2)}, u32[]{:S(2)}) collective-permute-start(bf16[16,896]{1,0:T(8,128)(2,1)S(1)} %get-tuple-element.12), channel_id=1, source_target_pairs={{0,64},{64,128},{128,192},{192,256},{256,320},{320,384},{384,448},... | collective-permute-start | bytes 86024 | tf_op jit(solution)/shard_map/ppermute | solution.py:23
  86.8 0.1 and.101
  86.9 0.9 collective-permute-done
  87.7 2.4 %collective-permute-done.1 = bf16[16,896]{1,0:T(8,128)(2,1)S(1)} collective-permute-done((bf16[16,896]{1,0:T(8,128)(2,1)S(1)}, bf16[16,896]{1,0:T(8,128)(2,1)S(1)}, u32[]{:S(2)}, u32[]{:S(2)}) %collective-permute-start.1) | collective-permute-done | bytes 28704 | tf_op jit(solution)/shard_map/ppermute | solution.py:23
  90.2 0.2 convolution_convert_fusion
  90.4 22.6 %all_to_all.42 = bf16[8,16,896]{2,1,0:T(8,128)(2,1)S(1)} all-to-all(bf16[8,16,896]{2,1,0:T(8,128)(2,1)S(1)} %bitcast.70), channel_id=1, replica_groups={{0,8,16,24,32,40,48,56},{1,9,17,25,33,41,49,57},{2,10,18,26,34,42,50,58..., dimensions={0} | all-to-all | bytes 458752 | tf_op jit(solution)/shard_map/all_to_all | solution.py:13
  113.0 0.1 fusion.23
  113.1 0.1 reduce_sum.84
  113.2 0.5 fusion.11
  113.7 0.1 select_convert_fusion
  113.8 9.7 %all_to_all.43 = bf16[8,16,1152]{2,1,0:T(8,128)(2,1)S(1)} all-to-all(bf16[8,16,1152]{2,1,0:T(8,128)(2,1)S(1)} %bitcast.63), channel_id=1, replica_groups={{0,1,2,3,4,5,6,7},{8,9,10,11,12,13,14,15},{16,17,18,19,20,21,22,23},{24..., dimensions={0} | all-to-all | bytes 589824 | tf_op jit(solution)/shard_map/all_to_all | solution.py:18
  123.6 0.2 fusion.28
  123.8 0.1 multiply_convert_fusion
  123.9 8.8 %all_to_all.44 = bf16[8,16,1024]{2,1,0:T(8,128)(2,1)S(1)} all-to-all(bf16[8,16,1024]{2,1,0:T(8,128)(2,1)S(1)} %broadcast_in_dim.126), channel_id=1, replica_groups={{0,1,2,3,4,5,6,7},{8,9,10,11,12,13,14,15},{16,17,18,19,20,21,22,23},{24..., dimensions={0} | all-to-all | bytes 524288 | tf_op jit(solution)/shard_map/all_to_all | solution.py:18
  132.8 1.1 fusion.17
  133.9 3.4 %all-to-all-start.7 = ((bf16[8,16,896]{2,1,0:T(8,128)(2,1)}), bf16[8,16,896]{2,1,0:T(8,128)(2,1)S(1)}, u32[]{:S(2)}, u32[]{:S(2)}) async-start(bf16[8,16,896]{2,1,0:T(8,128)(2,1)} %bitcast.17), calls=%async_computation.7 | async-start | bytes 458752 | tf_op jit(solution)/shard_map/all_to_all | solution.py:13
  137.3 0.1 select_n.77
  137.5 16.7 %all-to-all-done.7 = bf16[8,16,896]{2,1,0:T(8,128)(2,1)S(1)} async-done(((bf16[8,16,896]{2,1,0:T(8,128)(2,1)}), bf16[8,16,896]{2,1,0:T(8,128)(2,1)S(1)}, u32[]{:S(2)}, u32[]{:S(2)}) %all-to-all-start.7) | async-done | bytes 229408 | tf_op jit(solution)/shard_map/all_to_all | solution.py:13
  154.2 0.3 add_convert_fusion
  154.5 4.2 %collective-permute-start.2 = (bf16[16,896]{1,0:T(8,128)(2,1)S(1)}, bf16[16,896]{1,0:T(8,128)(2,1)S(1)}, u32[]{:S(2)}, u32[]{:S(2)}) collective-permute-start(bf16[16,896]{1,0:T(8,128)(2,1)S(1)} %get-tuple-element.9), channel_id=1, source_target_pairs={{0,64},{64,128},{128,192},{192,256},{256,320},{320,384},{384,448},... | collective-permute-start | bytes 86024 | tf_op jit(solution)/shard_map/ppermute | solution.py:23
  158.7 1.0 collective-permute-done.2
  159.7 2.6 %collective-permute-done.3 = bf16[16,896]{1,0:T(8,128)(2,1)S(1)} collective-permute-done((bf16[16,896]{1,0:T(8,128)(2,1)S(1)}, bf16[16,896]{1,0:T(8,128)(2,1)S(1)}, u32[]{:S(2)}, u32[]{:S(2)}) %collective-permute-start.3) | collective-permute-done | bytes 28704 | tf_op jit(solution)/shard_map/ppermute | solution.py:23
  162.3 0.6 pad_maximum_fusion.2
  (45 shorter events, 0.7 us)
Async XLA Ops:
  0.0 35.1 %copy-start = (bf16[1,1,896,1024]{3,2,1,0:T(8,128)(2,1)S(1)}, bf16[1,1,896,1024]{3,2,1,0:T(8,128)(2,1)}, u32[]{:S(2)}) copy-start(bf16[1,1,896,1024]{3,2,1,0:T(8,128)(2,1)} %param.7) | copy-start | bytes 5505028
  3.5 31.3 %all-to-all-start = ((bf16[8,16,896]{2,1,0:T(8,128)(2,1)}), bf16[8,16,896]{2,1,0:T(8,128)(2,1)S(1)}, u32[]{:S(2)}, u32[]{:S(2)}) async-start(bf16[8,16,896]{2,1,0:T(8,128)(2,1)} %bitcast.3), calls=%async_computation | async-start | bytes 458752 | tf_op jit(solution)/shard_map/all_to_all | solution.py:13
  35.5 20.2 %copy-start.1 = (bf16[1,1,1024,896]{3,2,1,0:T(8,128)(2,1)S(1)}, bf16[1,1,1024,896]{3,2,1,0:T(8,128)(2,1)}, u32[]{:S(2)}) copy-start(bf16[1,1,1024,896]{3,2,1,0:T(8,128)(2,1)} %param.8) | copy-start | bytes 5505028
  47.1 17.5 %copy-start.4 = (f32[2,2,1,128,2]{3,4,2,1,0:T(2,128)S(1)}, f32[2,2,1,128,2]{3,4,2,1,0:T(2,128)}, u32[]{:S(2)}) copy-start(f32[2,2,1,128,2]{3,4,2,1,0:T(2,128)} %param.11) | copy-start | bytes 12292
  55.7 24.1 %copy-start.3 = (bf16[1,2,1,16,896]{4,3,2,1,0:T(8,128)(2,1)S(1)}, bf16[1,2,1,16,896]{4,3,2,1,0:T(8,128)(2,1)}, u32[]{:S(2)}) copy-start(bf16[1,2,1,16,896]{4,3,2,1,0:T(8,128)(2,1)} %param.6) | copy-start | bytes 172036
  56.9 23.0 %all-to-all-start.3 = ((bf16[8,16,896]{2,1,0:T(8,128)(2,1)}), bf16[8,16,896]{2,1,0:T(8,128)(2,1)S(1)}, u32[]{:S(2)}, u32[]{:S(2)}) async-start(bf16[8,16,896]{2,1,0:T(8,128)(2,1)} %bitcast.9), calls=%async_computation.3 | async-start | bytes 458752 | tf_op jit(solution)/shard_map/all_to_all | solution.py:13
  80.1 7.6 %collective-permute-start = (bf16[16,896]{1,0:T(8,128)(2,1)S(1)}, bf16[16,896]{1,0:T(8,128)(2,1)S(1)}, u32[]{:S(2)}, u32[]{:S(2)}) collective-permute-start(bf16[16,896]{1,0:T(8,128)(2,1)S(1)} %get-tuple-element.12), channel_id=1, source_target_pairs={{0,64},{64,128},{128,192},{192,256},{256,320},{320,384},{384,448},... | collective-permute-start | bytes 86024 | tf_op jit(solution)/shard_map/ppermute | solution.py:23
  86.9 3.3 %collective-permute-start.1 = (bf16[16,896]{1,0:T(8,128)(2,1)S(1)}, bf16[16,896]{1,0:T(8,128)(2,1)S(1)}, u32[]{:S(2)}, u32[]{:S(2)}) collective-permute-start(bf16[16,896]{1,0:T(8,128)(2,1)S(1)} %get-tuple-element.11), channel_id=1, source_target_pairs={{0,448},{64,0},{128,64},{192,128},{256,192},{320,256},{384,320},{4... | collective-permute-start | bytes 86024 | tf_op jit(solution)/shard_map/ppermute | solution.py:23
  113.7 19.1 %copy-start.2 = (bf16[1,1,1024,896]{3,2,1,0:T(8,128)(2,1)S(1)}, bf16[1,1,1024,896]{3,2,1,0:T(8,128)(2,1)}, u32[]{:S(2)}) copy-start(bf16[1,1,1024,896]{3,2,1,0:T(8,128)(2,1)} %param.8) | copy-start | bytes 5505028
  133.9 20.2 %all-to-all-start.7 = ((bf16[8,16,896]{2,1,0:T(8,128)(2,1)}), bf16[8,16,896]{2,1,0:T(8,128)(2,1)S(1)}, u32[]{:S(2)}, u32[]{:S(2)}) async-start(bf16[8,16,896]{2,1,0:T(8,128)(2,1)} %bitcast.17), calls=%async_computation.7 | async-start | bytes 458752 | tf_op jit(solution)/shard_map/all_to_all | solution.py:13
  154.5 5.2 %collective-permute-start.2 = (bf16[16,896]{1,0:T(8,128)(2,1)S(1)}, bf16[16,896]{1,0:T(8,128)(2,1)S(1)}, u32[]{:S(2)}, u32[]{:S(2)}) collective-permute-start(bf16[16,896]{1,0:T(8,128)(2,1)S(1)} %get-tuple-element.9), channel_id=1, source_target_pairs={{0,64},{64,128},{128,192},{192,256},{256,320},{320,384},{384,448},... | collective-permute-start | bytes 86024 | tf_op jit(solution)/shard_map/ppermute | solution.py:23
  158.7 3.6 %collective-permute-start.3 = (bf16[16,896]{1,0:T(8,128)(2,1)S(1)}, bf16[16,896]{1,0:T(8,128)(2,1)S(1)}, u32[]{:S(2)}, u32[]{:S(2)}) collective-permute-start(bf16[16,896]{1,0:T(8,128)(2,1)S(1)} %get-tuple-element.10), channel_id=1, source_target_pairs={{0,448},{64,0},{128,64},{192,128},{256,192},{320,256},{384,320},{4... | collective-permute-start | bytes 86024 | tf_op jit(solution)/shard_map/ppermute | solution.py:23

commit v2 on v1

v2 whole, which is shorter than its diff:
```python
import jax
import jax.numpy as jnp
from jax import lax
from jax.experimental import pallas as pl
from jax.experimental.pallas import tpu as pltpu
from jax.sharding import PartitionSpec as P

GROUPS = 8
SLICES = 8
CAP = 8
LANES = 128
VMEM = pl.BlockSpec(memory_space=pltpu.VMEM)
HBM = pl.BlockSpec(memory_space=pltpu.HBM)


def over_groups(value):
    members = [[g * SLICES + s for g in range(GROUPS)] for s in range(SLICES)]
    return lax.all_to_all(value, "expert", 0, 0, axis_index_groups=members, tiled=True)


def over_slices(value):
    members = [[g * SLICES + s for s in range(SLICES)] for g in range(GROUPS)]
    return lax.all_to_all(value, "expert", 0, 0, axis_index_groups=members, tiled=True)


def shifted(value, steps):
    count = lax.axis_size("pipe")
    return lax.ppermute(value, "pipe", [(i, (i + steps) % count) for i in range(count)])


def prepare(
    state_hbm, routes_hbm, weights_hbm, gain_hbm,
    rows_ref, place_ref, mix_ref, gain_ref,
    state_ref, routes_ref, weights_ref, arrived,
):
    expert_index = lax.axis_index("expert")
    group, part = expert_index // SLICES, expert_index % SLICES
    steps, streams, topk, every = routes_ref.shape
    tokens = every // GROUPS
    slots = GROUPS * streams * CAP
    width = state_ref.shape[1]
    own_gain = gain_hbm.at[:, pl.ds(pl.multiple_of(part * width, LANES), width)]
    copies = [
        pltpu.make_async_copy(source, target, arrived.at[i])
        for i, (source, target) in enumerate(
            [
                (routes_hbm, routes_ref),
                (weights_hbm, weights_ref),
                (state_hbm, state_ref),
                (own_gain, gain_ref),
            ]
        )
    ]
    for copy in copies:
        copy.start()

    def own(ref, step, choice):
        lane = lax.broadcasted_iota(jnp.int32, (1, every), 1)
        out = jnp.zeros((1, every), ref.dtype)
        for m in range(streams):
            line = ref[step, m, choice : choice + 1, :]
            line = pltpu.roll(line, (every - group * tokens + m * tokens) % every, 1)
            out = jnp.where(lane // tokens == m, line, out)
        return out

    row = lax.broadcasted_iota(jnp.int32, (slots, every), 0)
    lane = lax.broadcasted_iota(jnp.int32, (slots, every), 1)
    expert, stream, slot = row // (streams * CAP), row // CAP % streams, row % CAP
    mine = lane // tokens == stream
    earlier_row = lax.broadcasted_iota(jnp.int32, (every, every), 0)
    earlier_lane = lax.broadcasted_iota(jnp.int32, (every, every), 1)
    earlier = (earlier_row // tokens == earlier_lane // tokens) & (earlier_row < earlier_lane)
    earlier = jnp.where(earlier, 1.0, 0.0).astype(jnp.bfloat16)
    for copy in copies:
        copy.wait()
    for step in range(steps):
        named = [mine & (own(routes_ref, step, k) == expert) for k in range(topk)]
        hit = named[0]
        for k in range(1, topk):
            hit = hit | named[k]
        hit = jnp.where(hit, 1.0, 0.0)
        rank = jnp.dot(hit.astype(jnp.bfloat16), earlier, preferred_element_type=jnp.float32)
        placed = jnp.where(rank == slot.astype(jnp.float32), hit, 0.0)
        weight = jnp.zeros((slots, every), jnp.float32)
        for k in range(topk):
            weight = jnp.where(named[k], own(weights_ref, step, k), weight)
        mix = jnp.transpose(placed * weight)
        mix_ref[step] = mix[: streams * tokens]
        narrow = placed[:, : streams * tokens].astype(jnp.bfloat16)
        if step == 0:
            rows_ref[...] = jnp.dot(
                narrow, state_ref[...], preferred_element_type=jnp.float32
            ).astype(jnp.bfloat16)
        else:
            place_ref[step - 1] = narrow


def shards(state, up_weight, down_weight, norm_gain, routes, route_weight):
    streams, tokens, width = state.shape[1], state.shape[3], state.shape[4]
    steps = routes.shape[0]
    features = width * SLICES
    up, down = up_weight[0, 0], down_weight[0, 0]
    hidden_width = up.shape[1]
    slots = streams * CAP
    current = state[0, :, 0].reshape(streams * tokens, width)
    outgoing, place, mix, gain = pl.pallas_call(
        prepare,
        out_shape=(
            jax.ShapeDtypeStruct((GROUPS * slots, width), jnp.bfloat16),
            jax.ShapeDtypeStruct((steps - 1, GROUPS * slots, streams * tokens), jnp.bfloat16),
            jax.ShapeDtypeStruct((steps, streams * tokens, GROUPS * slots), jnp.float32),
            jax.ShapeDtypeStruct((1, width), jnp.float32),
        ),
        in_specs=[HBM, HBM, HBM, HBM],
        out_specs=(VMEM, VMEM, VMEM, VMEM),
        scratch_shapes=[
            pltpu.VMEM(current.shape, current.dtype),
            pltpu.VMEM((steps, streams, routes.shape[4], routes.shape[3]), routes.dtype),
            pltpu.VMEM((steps, streams, routes.shape[4], routes.shape[3]), route_weight.dtype),
            pltpu.SemaphoreType.DMA((4,)),
        ],
        name="prepare",
    )(
        current,
        jnp.swapaxes(routes[:, :, 0], 2, 3),
        jnp.swapaxes(route_weight[:, :, 0], 2, 3),
        norm_gain,
    )
    lane = jnp.arange(LANES)
    for step in range(steps):
        if step > 0:
            outgoing = jnp.dot(
                place[step - 1], current, preferred_element_type=jnp.float32
            ).astype(jnp.bfloat16)
        rows = over_groups(outgoing.reshape(GROUPS, slots, width)).reshape(GROUPS * slots, width)
        rows_f = rows.astype(jnp.float32)
        squares = jnp.sum(rows_f * rows_f, axis=1, keepdims=True)
        scaled = (rows_f * gain).astype(jnp.bfloat16)
        partial = jnp.dot(scaled, up, preferred_element_type=jnp.float32).astype(jnp.bfloat16)
        high = lax.reduce_precision(squares, 8, 7)
        tail = jnp.where(lane == 0, high, jnp.where(lane == 1, squares - high, 0.0))
        sent = jnp.concatenate([partial, tail.astype(jnp.bfloat16)], axis=1)
        parts = over_slices(sent.reshape(SLICES, slots, hidden_width + LANES)).astype(jnp.float32)
        total = jnp.sum(parts, axis=0)
        summed = total[:, hidden_width : hidden_width + 1] + total[:, hidden_width + 1 : hidden_width + 2]
        value = total[:, :hidden_width] * lax.rsqrt(summed / features + 1e-06)
        active = jax.nn.silu(value).astype(jnp.bfloat16)
        hidden = over_slices(jnp.broadcast_to(active, (SLICES, slots, hidden_width)))
        produced = jnp.dot(
            hidden.reshape(GROUPS * slots, hidden_width), down, preferred_element_type=jnp.float32
        ).astype(jnp.bfloat16)
        returned = over_groups(produced.reshape(GROUPS, slots, width)).reshape(GROUPS * slots, width)
        added = jnp.dot(
            mix[step],
            returned.astype(jnp.float32),
            precision=lax.Precision.HIGHEST,
            preferred_element_type=jnp.float32,
        )
        result = (current.astype(jnp.float32) + added).astype(jnp.bfloat16)
        forward = shifted(result[:tokens], 1)
        backward = shifted(result[tokens:], -1)
        current = jnp.concatenate([forward, backward], axis=0)
    return current.reshape(1, streams, 1, tokens, width)


def solution(mesh):
    return jax.shard_map(
        shards,
        mesh=mesh,
        in_specs=(
            P("pipe", None, "expert", None, None),
            P("pipe", "expert", None, None),
            P("pipe", "expert", None, None),
            P("pipe", None),
            P(None, None, "pipe", None, None),
            P(None, None, "pipe", None, None),
        ),
        out_specs=P("pipe", None, "expert", None, None),
        check_vma=False,
    )
```

time: 164 us -> 160 us (0.976)
  blocking collectives: 60.9 us -> 101 us
  waiting for transfers between devices: 53.2 us -> 21.6 us
  starting transfers between devices: 37.7 us -> 28.9 us
  matrix products: 5.61 us -> 2.46 us
  local copies, waits for them, and re-layouts: 2.73 us -> 0.26 us
  Pallas kernels: 0 us -> 2.12 us
    all_to_all x1 -> x3, blocking collectives: 22.6 us -> 63.3 us  [over_groups(): lax.all_to_all(value, 'expert', 0, 0, axis_index_groups=members, tiled=True)]
    all_to_all x3 -> x1, waiting for transfers between devices: 46.3 us -> 15 us  [over_groups(): lax.all_to_all(value, 'expert', 0, 0, axis_index_groups=members, tiled=True)]
    all_to_all x3 -> x1, starting transfers between devices: 26.8 us -> 15.7 us  [over_groups(): lax.all_to_all(value, 'expert', 0, 0, axis_index_groups=members, tiled=True)]
    ppermute x4, starting transfers between devices: 10.9 us -> 13.2 us  [shifted(): lax.ppermute(value, 'pipe', [(i, (i + steps) % count) for i in range(coun...]
    pallas_call x0 -> x1, Pallas kernels: none -> 2.12 us  [shards(): pl.pallas_call(prepare, out_shape=(jax.ShapeDtypeStruct((GROUPS * slots,...]
    dot_general x4 -> x3, matrix products: 2.45 us -> 0.65 us  [the longest x2 0.46 us: shards(): jnp.dot(mix[step], returned.astype(jnp.float32), precision=lax.Precision....]
  transfers between devices with their start and end apart: 7 -> 5, of which waited for: 7 -> 5; matrix products, arithmetic and copies ran while one was open for 1% -> 0% of each run, Pallas kernels for 0% -> 0%
where the time goes in v2:
time: 160 us; the launch traced here: 159 us
  blocking collectives  101 us (63%)
  starting transfers between devices  28.9 us (18%)
  waiting for transfers between devices  21.6 us (14%)
  other arithmetic  2.51 us (2%)
  matrix products  2.46 us (2%)
  Pallas kernels  2.12 us (1%)
    all_to_all x3, blocking collectives, over_groups(): lax.all_to_all(value, 'expert', 0, 0, axis_index_groups=members, tiled=True)  63.3 us
    all_to_all x4, blocking collectives, over_slices(): lax.all_to_all(value, 'expert', 0, 0, axis_index_groups=members, tiled=True)  38 us
    all_to_all x1, starting transfers between devices, over_groups(): lax.all_to_all(value, 'expert', 0, 0, axis_index_groups=members, tiled=True)  15.7 us
    all_to_all x1, waiting for transfers between devices, over_groups(): lax.all_to_all(value, 'expert', 0, 0, axis_index_groups=members, tiled=True)  15 us
    ppermute x4, starting transfers between devices, shifted(): lax.ppermute(value, 'pipe', [(i, (i + steps) % count) for i in range(coun...  13.2 us
    ppermute x4, waiting for transfers between devices, shifted(): lax.ppermute(value, 'pipe', [(i, (i + steps) % count) for i in range(coun...  6.58 us
  transfers between devices with their start and end apart: 5, of which 5 were waited for; matrix products, arithmetic and copies ran while one was open for 0% of the time, Pallas kernels for 0%

profile of v2, /device:TPU:1, one launch (start us, length us, event | category | flops | bytes accessed | tf_op | source)
XLA Modules:
  0.0 159.3 jit_solution(15189634331421908524)
XLA Ops:
  0.0 0.0 copy-start
  0.0 2.1 %prepare.1 = (bf16[128,896]{1,0:T(8,128)(2,1)}, bf16[1,128,32]{2,1,0:T(8,128)(2,1)}, f32[2,32,128]{2,1,0:T(8,128)}, f32[1,896]{1,0:T(1,128)}) custom-call(bf16[32,896]{1,0:T(8,128)(2,1)} %bitcast.70, s32[2,2,2,128]{3,2,1,0:T(2,128)} %bitcast.72, f32[2,2,2,128]{3,2,1,0:T(2,128)} %bitcast.73, f32[1,7168]{1,0:T(1,128)} %gain_hbm.1), custom_call_target="tpu_custom_call" | custom-call | tf_op jit(solution)/shard_map/prepare/pallas_call | solution.py:106
  2.1 15.7 %all-to-all-start = ((bf16[8,16,896]{2,1,0:T(8,128)(2,1)}), bf16[8,16,896]{2,1,0:T(8,128)(2,1)S(1)}, u32[]{:S(2)}, u32[]{:S(2)}) async-start(bf16[8,16,896]{2,1,0:T(8,128)(2,1)} %bitcast.69), calls=%async_computation | async-start | bytes 458752 | tf_op jit(solution)/shard_map/all_to_all | solution.py:18
  17.8 0.7 reduce.2
  18.5 15.0 %all-to-all-done = bf16[8,16,896]{2,1,0:T(8,128)(2,1)S(1)} async-done(((bf16[8,16,896]{2,1,0:T(8,128)(2,1)}), bf16[8,16,896]{2,1,0:T(8,128)(2,1)S(1)}, u32[]{:S(2)}, u32[]{:S(2)}) %all-to-all-start) | async-done | bytes 229408 | tf_op jit(solution)/shard_map/all_to_all | solution.py:18
  33.5 0.1 fusion.21
  33.6 0.1 reduce_sum.41
  33.7 0.0 copy-done
  33.7 0.4 fusion.8
  34.2 0.0 copy-start.1
  34.2 0.1 select_convert_fusion.1
  34.3 11.2 %all_to_all.40 = bf16[8,16,1152]{2,1,0:T(8,128)(2,1)S(1)} all-to-all(bf16[8,16,1152]{2,1,0:T(8,128)(2,1)S(1)} %bitcast.58), channel_id=1, replica_groups={{0,1,2,3,4,5,6,7},{8,9,10,11,12,13,14,15},{16,17,18,19,20,21,22,23},{24..., dimensions={0} | all-to-all | bytes 589824 | tf_op jit(solution)/shard_map/all_to_all | solution.py:23
  45.5 0.2 fusion.40
  45.7 0.0 copy-start.4
  45.7 0.1 multiply_convert_fusion.1
  45.9 0.0 copy-start.5
  45.9 8.5 %all_to_all.41 = bf16[8,16,1024]{2,1,0:T(8,128)(2,1)S(1)} all-to-all(bf16[8,16,1024]{2,1,0:T(8,128)(2,1)S(1)} %broadcast_in_dim.58), channel_id=1, replica_groups={{0,1,2,3,4,5,6,7},{8,9,10,11,12,13,14,15},{16,17,18,19,20,21,22,23},{24..., dimensions={0} | all-to-all | bytes 524288 | tf_op jit(solution)/shard_map/all_to_all | solution.py:23
  54.4 0.0 copy-done.1
  54.4 0.5 fusion.14
  54.8 22.7 %all_to_all.42 = bf16[8,16,896]{2,1,0:T(8,128)(2,1)S(1)} all-to-all(bf16[8,16,896]{2,1,0:T(8,128)(2,1)S(1)} %bitcast.64), channel_id=1, replica_groups={{0,8,16,24,32,40,48,56},{1,9,17,25,33,41,49,57},{2,10,18,26,34,42,50,58..., dimensions={0} | all-to-all | bytes 458752 | tf_op jit(solution)/shard_map/all_to_all | solution.py:18
  77.6 0.0 copy-done.3
  77.6 0.0 copy-done.4
  77.6 0.2 fusion.20
  77.8 6.7 %collective-permute-start = (bf16[16,896]{1,0:T(8,128)(2,1)S(1)}, bf16[16,896]{1,0:T(8,128)(2,1)S(1)}, u32[]{:S(2)}, u32[]{:S(2)}) collective-permute-start(bf16[16,896]{1,0:T(8,128)(2,1)S(1)} %get-tuple-element.20), channel_id=1, source_target_pairs={{0,64},{64,128},{128,192},{192,256},{256,320},{320,384},{384,448},... | collective-permute-start | bytes 86024 | tf_op jit(solution)/shard_map/ppermute | solution.py:28
  84.5 0.0 collective-permute-start.1
  84.5 1.0 collective-permute-done
  85.5 2.3 %collective-permute-done.1 = bf16[16,896]{1,0:T(8,128)(2,1)S(1)} collective-permute-done((bf16[16,896]{1,0:T(8,128)(2,1)S(1)}, bf16[16,896]{1,0:T(8,128)(2,1)S(1)}, u32[]{:S(2)}, u32[]{:S(2)}) %collective-permute-start.1) | collective-permute-done | bytes 28704 | tf_op jit(solution)/shard_map/ppermute | solution.py:28
  87.8 0.0 copy-done.5
  87.8 0.2 convolution_convert_fusion
  88.0 22.5 %all_to_all.43 = bf16[8,16,896]{2,1,0:T(8,128)(2,1)S(1)} all-to-all(bf16[8,16,896]{2,1,0:T(8,128)(2,1)S(1)} %bitcast.66), channel_id=1, replica_groups={{0,8,16,24,32,40,48,56},{1,9,17,25,33,41,49,57},{2,10,18,26,34,42,50,58..., dimensions={0} | all-to-all | bytes 458752 | tf_op jit(solution)/shard_map/all_to_all | solution.py:18
  110.5 0.1 fusion.23
  110.6 0.1 reduce_sum.44
  110.7 0.5 fusion.11
  111.2 0.0 copy-start.2
  111.2 0.1 select_convert_fusion
  111.3 9.3 %all_to_all.44 = bf16[8,16,1152]{2,1,0:T(8,128)(2,1)S(1)} all-to-all(bf16[8,16,1152]{2,1,0:T(8,128)(2,1)S(1)} %bitcast.59), channel_id=1, replica_groups={{0,1,2,3,4,5,6,7},{8,9,10,11,12,13,14,15},{16,17,18,19,20,21,22,23},{24..., dimensions={0} | all-to-all | bytes 589824 | tf_op jit(solution)/shard_map/all_to_all | solution.py:23
  120.7 0.2 fusion.36
  120.9 0.1 multiply_convert_fusion
  121.0 9.0 %all_to_all.45 = bf16[8,16,1024]{2,1,0:T(8,128)(2,1)S(1)} all-to-all(bf16[8,16,1024]{2,1,0:T(8,128)(2,1)S(1)} %broadcast_in_dim.61), channel_id=1, replica_groups={{0,1,2,3,4,5,6,7},{8,9,10,11,12,13,14,15},{16,17,18,19,20,21,22,23},{24..., dimensions={0} | all-to-all | bytes 524288 | tf_op jit(solution)/shard_map/all_to_all | solution.py:23
  130.0 0.0 copy-done.2
  130.0 0.5 fusion.17
  130.5 18.1 %all_to_all.46 = bf16[8,16,896]{2,1,0:T(8,128)(2,1)S(1)} all-to-all(bf16[8,16,896]{2,1,0:T(8,128)(2,1)S(1)} %bitcast.65), channel_id=1, replica_groups={{0,8,16,24,32,40,48,56},{1,9,17,25,33,41,49,57},{2,10,18,26,34,42,50,58..., dimensions={0} | all-to-all | bytes 458752 | tf_op jit(solution)/shard_map/all_to_all | solution.py:18
  148.6 0.2 add_convert_fusion
  148.9 6.5 %collective-permute-start.2 = (bf16[16,896]{1,0:T(8,128)(2,1)S(1)}, bf16[16,896]{1,0:T(8,128)(2,1)S(1)}, u32[]{:S(2)}, u32[]{:S(2)}) collective-permute-start(bf16[16,896]{1,0:T(8,128)(2,1)S(1)} %get-tuple-element.17), channel_id=1, source_target_pairs={{0,64},{64,128},{128,192},{192,256},{256,320},{320,384},{384,448},... | collective-permute-start | bytes 86024 | tf_op jit(solution)/shard_map/ppermute | solution.py:28
  155.4 0.0 collective-permute-start.3
  155.4 1.0 collective-permute-done.2
  156.4 2.3 %collective-permute-done.3 = bf16[16,896]{1,0:T(8,128)(2,1)S(1)} collective-permute-done((bf16[16,896]{1,0:T(8,128)(2,1)S(1)}, bf16[16,896]{1,0:T(8,128)(2,1)S(1)}, u32[]{:S(2)}, u32[]{:S(2)}) %collective-permute-start.3) | collective-permute-done | bytes 28704 | tf_op jit(solution)/shard_map/ppermute | solution.py:28
  158.7 0.6 pad_maximum_fusion.2
  (14 shorter events, 0.2 us)
Async XLA Ops:
  0.0 33.7 %copy-start = (bf16[1,1,896,1024]{3,2,1,0:T(8,128)(2,1)S(1)}, bf16[1,1,896,1024]{3,2,1,0:T(8,128)(2,1)}, u32[]{:S(2)}) copy-start(bf16[1,1,896,1024]{3,2,1,0:T(8,128)(2,1)} %param.7) | copy-start | bytes 5505028
  2.1 31.3 %all-to-all-start = ((bf16[8,16,896]{2,1,0:T(8,128)(2,1)}), bf16[8,16,896]{2,1,0:T(8,128)(2,1)S(1)}, u32[]{:S(2)}, u32[]{:S(2)}) async-start(bf16[8,16,896]{2,1,0:T(8,128)(2,1)} %bitcast.69), calls=%async_computation | async-start | bytes 458752 | tf_op jit(solution)/shard_map/all_to_all | solution.py:18
  34.2 20.2 %copy-start.1 = (bf16[1,1,1024,896]{3,2,1,0:T(8,128)(2,1)S(1)}, bf16[1,1,1024,896]{3,2,1,0:T(8,128)(2,1)}, u32[]{:S(2)}) copy-start(bf16[1,1,1024,896]{3,2,1,0:T(8,128)(2,1)} %param.8) | copy-start | bytes 5505028
  45.7 31.8 %copy-start.3 = (bf16[1,2,1,16,896]{4,3,2,1,0:T(8,128)(2,1)S(1)}, bf16[1,2,1,16,896]{4,3,2,1,0:T(8,128)(2,1)}, u32[]{:S(2)}) copy-start(bf16[1,2,1,16,896]{4,3,2,1,0:T(8,128)(2,1)} %param.6) | copy-start | bytes 172036
  45.7 31.8 %copy-start.4 = (f32[2,32,128]{2,1,0:T(8,128)S(1)}, f32[2,32,128]{2,1,0:T(8,128)}, u32[]{:S(2)}) copy-start(f32[2,32,128]{2,1,0:T(8,128)} %get-tuple-element.9) | copy-start | bytes 98308
  45.9 41.9 %copy-start.5 = (bf16[1,128,32]{2,1,0:T(8,128)(2,1)S(1)}, bf16[1,128,32]{2,1,0:T(8,128)(2,1)}, u32[]{:S(2)}) copy-start(bf16[1,128,32]{2,1,0:T(8,128)(2,1)} %get-tuple-element.12) | copy-start | bytes 24580
  77.8 7.7 %collective-permute-start = (bf16[16,896]{1,0:T(8,128)(2,1)S(1)}, bf16[16,896]{1,0:T(8,128)(2,1)S(1)}, u32[]{:S(2)}, u32[]{:S(2)}) collective-permute-start(bf16[16,896]{1,0:T(8,128)(2,1)S(1)} %get-tuple-element.20), channel_id=1, source_target_pairs={{0,64},{64,128},{128,192},{192,256},{256,320},{320,384},{384,448},... | collective-permute-start | bytes 86024 | tf_op jit(solution)/shard_map/ppermute | solution.py:28
  84.5 3.3 %collective-permute-start.1 = (bf16[16,896]{1,0:T(8,128)(2,1)S(1)}, bf16[16,896]{1,0:T(8,128)(2,1)S(1)}, u32[]{:S(2)}, u32[]{:S(2)}) collective-permute-start(bf16[16,896]{1,0:T(8,128)(2,1)S(1)} %get-tuple-element.19), channel_id=1, source_target_pairs={{0,448},{64,0},{128,64},{192,128},{256,192},{320,256},{384,320},{4... | collective-permute-start | bytes 86024 | tf_op jit(solution)/shard_map/ppermute | solution.py:28
  111.2 18.9 %copy-start.2 = (bf16[1,1,1024,896]{3,2,1,0:T(8,128)(2,1)S(1)}, bf16[1,1,1024,896]{3,2,1,0:T(8,128)(2,1)}, u32[]{:S(2)}) copy-start(bf16[1,1,1024,896]{3,2,1,0:T(8,128)(2,1)} %param.8) | copy-start | bytes 5505028
  148.9 7.5 %collective-permute-start.2 = (bf16[16,896]{1,0:T(8,128)(2,1)S(1)}, bf16[16,896]{1,0:T(8,128)(2,1)S(1)}, u32[]{:S(2)}, u32[]{:S(2)}) collective-permute-start(bf16[16,896]{1,0:T(8,128)(2,1)S(1)} %get-tuple-element.17), channel_id=1, source_target_pairs={{0,64},{64,128},{128,192},{192,256},{256,320},{320,384},{384,448},... | collective-permute-start | bytes 86024 | tf_op jit(solution)/shard_map/ppermute | solution.py:28
  155.4 3.3 %collective-permute-start.3 = (bf16[16,896]{1,0:T(8,128)(2,1)S(1)}, bf16[16,896]{1,0:T(8,128)(2,1)S(1)}, u32[]{:S(2)}, u32[]{:S(2)}) collective-permute-start(bf16[16,896]{1,0:T(8,128)(2,1)S(1)} %get-tuple-element.18), channel_id=1, source_target_pairs={{0,448},{64,0},{128,64},{192,128},{256,192},{320,256},{384,320},{4... | collective-permute-start | bytes 86024 | tf_op jit(solution)/shard_map/ppermute | solution.py:28

commit v3 on v2

--- a/solution.py
+++ b/solution.py
@@ -23,33 +23,34 @@
     return lax.all_to_all(value, "expert", 0, 0, axis_index_groups=members, tiled=True)
 
 
-def shifted(value, steps):
+def swapped(value, off_chip):
     count = lax.axis_size("pipe")
-    return lax.ppermute(value, "pipe", [(i, (i + steps) % count) for i in range(count)])
+    pairs = [(i, i ^ 1) for i in range(count)]
+    if off_chip:
+        pairs = [(i, (i + 1 if i % 2 else i - 1) % count) for i in range(count)]
+    return lax.ppermute(value, "pipe", pairs)
 
 
 def prepare(
     state_hbm, routes_hbm, weights_hbm, gain_hbm,
-    rows_ref, place_ref, mix_ref, gain_ref,
-    state_ref, routes_ref, weights_ref, arrived,
+    rows_ref, state_ref, place_ref, mix_ref, gain_ref,
+    routes_ref, weights_ref, gain_line, arrived,
 ):
     expert_index = lax.axis_index("expert")
+    odd = lax.axis_index("pipe") % 2
     group, part = expert_index // SLICES, expert_index % SLICES
     steps, streams, topk, every = routes_ref.shape
     tokens = every // GROUPS
     slots = GROUPS * streams * CAP
     width = state_ref.shape[1]
+    stream_at = [odd, 1 - odd]
     own_gain = gain_hbm.at[:, pl.ds(pl.multiple_of(part * width, LANES), width)]
+    moves = [(routes_hbm, routes_ref), (weights_hbm, weights_ref), (own_gain, gain_line)]
+    for q in range(streams):
+        moves.append((state_hbm.at[stream_at[q]], state_ref.at[pl.ds(q * tokens, tokens)]))
     copies = [
         pltpu.make_async_copy(source, target, arrived.at[i])
-        for i, (source, target) in enumerate(
-            [
-                (routes_hbm, routes_ref),
-                (weights_hbm, weights_ref),
-                (state_hbm, state_ref),
-                (own_gain, gain_ref),
-            ]
-        )
+        for i, (source, target) in enumerate(moves)
     ]
     for copy in copies:
         copy.start()
@@ -57,22 +58,23 @@
     def own(ref, step, choice):
         lane = lax.broadcasted_iota(jnp.int32, (1, every), 1)
         out = jnp.zeros((1, every), ref.dtype)
-        for m in range(streams):
-            line = ref[step, m, choice : choice + 1, :]
-            line = pltpu.roll(line, (every - group * tokens + m * tokens) % every, 1)
-            out = jnp.where(lane // tokens == m, line, out)
+        for q in range(streams):
+            line = ref[step, stream_at[q], choice : choice + 1, :]
+            line = pltpu.roll(line, (every - group * tokens + q * tokens) % every, 1)
+            out = jnp.where(lane // tokens == q, line, out)
         return out
 
     row = lax.broadcasted_iota(jnp.int32, (slots, every), 0)
     lane = lax.broadcasted_iota(jnp.int32, (slots, every), 1)
-    expert, stream, slot = row // (streams * CAP), row // CAP % streams, row % CAP
-    mine = lane // tokens == stream
+    expert, position, slot = row // (streams * CAP), row // CAP % streams, row % CAP
+    mine = lane // tokens == position
     earlier_row = lax.broadcasted_iota(jnp.int32, (every, every), 0)
     earlier_lane = lax.broadcasted_iota(jnp.int32, (every, every), 1)
     earlier = (earlier_row // tokens == earlier_lane // tokens) & (earlier_row < earlier_lane)
     earlier = jnp.where(earlier, 1.0, 0.0).astype(jnp.bfloat16)
     for copy in copies:
         copy.wait()
+    gain_ref[...] = jnp.broadcast_to(gain_line[...], gain_ref.shape)
     for step in range(steps):
         named = [mine & (own(routes_ref, step, k) == expert) for k in range(topk)]
         hit = named[0]
@@ -102,26 +104,26 @@
     up, down = up_weight[0, 0], down_weight[0, 0]
     hidden_width = up.shape[1]
     slots = streams * CAP
-    current = state[0, :, 0].reshape(streams * tokens, width)
-    outgoing, place, mix, gain = pl.pallas_call(
+    outgoing, current, place, mix, gain = pl.pallas_call(
         prepare,
         out_shape=(
             jax.ShapeDtypeStruct((GROUPS * slots, width), jnp.bfloat16),
+            jax.ShapeDtypeStruct((streams * tokens, width), state.dtype),
             jax.ShapeDtypeStruct((steps - 1, GROUPS * slots, streams * tokens), jnp.bfloat16),
             jax.ShapeDtypeStruct((steps, streams * tokens, GROUPS * slots), jnp.float32),
-            jax.ShapeDtypeStruct((1, width), jnp.float32),
+            jax.ShapeDtypeStruct((slots, width), jnp.float32),
         ),
         in_specs=[HBM, HBM, HBM, HBM],
-        out_specs=(VMEM, VMEM, VMEM, VMEM),
+        out_specs=(VMEM, VMEM, VMEM, VMEM, VMEM),
         scratch_shapes=[
-            pltpu.VMEM(current.shape, current.dtype),
             pltpu.VMEM((steps, streams, routes.shape[4], routes.shape[3]), routes.dtype),
             pltpu.VMEM((steps, streams, routes.shape[4], routes.shape[3]), route_weight.dtype),
-            pltpu.SemaphoreType.DMA((4,)),
+            pltpu.VMEM((1, width), jnp.float32),
+            pltpu.SemaphoreType.DMA((5,)),
         ],
         name="prepare",
     )(
-        current,
+        state[0, :, 0],
         jnp.swapaxes(routes[:, :, 0], 2, 3),
         jnp.swapaxes(route_weight[:, :, 0], 2, 3),
         norm_gain,
@@ -132,10 +134,9 @@
             outgoing = jnp.dot(
                 place[step - 1], current, preferred_element_type=jnp.float32
             ).astype(jnp.bfloat16)
-        rows = over_groups(outgoing.reshape(GROUPS, slots, width)).reshape(GROUPS * slots, width)
-        rows_f = rows.astype(jnp.float32)
-        squares = jnp.sum(rows_f * rows_f, axis=1, keepdims=True)
-        scaled = (rows_f * gain).astype(jnp.bfloat16)
+        rows_f = over_groups(outgoing.reshape(GROUPS, slots, width)).astype(jnp.float32)
+        squares = jnp.sum(rows_f * rows_f, axis=2).reshape(GROUPS * slots, 1)
+        scaled = (rows_f * gain).astype(jnp.bfloat16).reshape(GROUPS * slots, width)
         partial = jnp.dot(scaled, up, preferred_element_type=jnp.float32).astype(jnp.bfloat16)
         high = lax.reduce_precision(squares, 8, 7)
         tail = jnp.where(lane == 0, high, jnp.where(lane == 1, squares - high, 0.0))
@@ -157,10 +158,12 @@
             preferred_element_type=jnp.float32,
         )
         result = (current.astype(jnp.float32) + added).astype(jnp.bfloat16)
-        forward = shifted(result[:tokens], 1)
-        backward = shifted(result[tokens:], -1)
-        current = jnp.concatenate([forward, backward], axis=0)
-    return current.reshape(1, streams, 1, tokens, width)
+        far = swapped(result[tokens:], True)
+        near = swapped(result[:tokens], False)
+        current = jnp.concatenate([far, near], axis=0)
+    odd = lax.axis_index("pipe") % 2 == 1
+    ordered = jnp.stack([jnp.where(odd, near, far), jnp.where(odd, far, near)])
+    return ordered[None, :, None]
 
 
 def solution(mesh):

time: 160 us -> 165 us (1.031)
  starting transfers between devices: 28.9 us -> 37.5 us
  waiting for transfers between devices: 21.6 us -> 19.4 us
    ppermute x4, starting transfers between devices: 13.2 us -> 21.9 us  [swapped(): return lax.ppermute(value, 'pipe', pairs)]
    ppermute x4, waiting for transfers between devices: 6.58 us -> 2.96 us  [swapped(): return lax.ppermute(value, 'pipe', pairs)]
    all_to_all x4, blocking collectives: 38 us -> 35.9 us  [over_slices(): lax.all_to_all(value, 'expert', 0, 0, axis_index_groups=members, tiled=True)]
  transfers between devices with their start and end apart: 5 -> 5, of which waited for: 5 -> 3; matrix products, arithmetic and copies ran while one was open for 0% -> 0% of each run, Pallas kernels for 0% -> 0%
where the time goes in v3:
time: 165 us; the launch traced here: 164 us
  blocking collectives  99.5 us (60%)
  starting transfers between devices  37.5 us (23%)
  waiting for transfers between devices  19.4 us (12%)
  other arithmetic  2.65 us (2%)
  matrix products  2.46 us (1%)
  Pallas kernels  2.12 us (1%)
    all_to_all x3, blocking collectives, over_groups(): lax.all_to_all(value, 'expert', 0, 0, axis_index_groups=members, tiled=True)  63.6 us
    all_to_all x4, blocking collectives, over_slices(): lax.all_to_all(value, 'expert', 0, 0, axis_index_groups=members, tiled=True)  35.9 us
    ppermute x4, starting transfers between devices, swapped(): return lax.ppermute(value, 'pipe', pairs)  21.9 us
    all_to_all x1, waiting for transfers between devices, over_groups(): lax.all_to_all(value, 'expert', 0, 0, axis_index_groups=members, tiled=True)  16.4 us
    all_to_all x1, starting transfers between devices, over_groups(): lax.all_to_all(value, 'expert', 0, 0, axis_index_groups=members, tiled=True)  15.7 us
  transfers between devices with their start and end apart: 5, of which 3 were waited for; matrix products, arithmetic and copies ran while one was open for 0% of the time, Pallas kernels for 0%

profile of v3, /device:TPU:1, one launch (start us, length us, event | category | flops | bytes accessed | tf_op | source)
XLA Modules:
  0.0 164.2 jit_solution(14153039866933150040)
XLA Ops:
  0.0 0.0 copy-start
  0.0 2.1 %prepare.1 = (bf16[128,896]{1,0:T(8,128)(2,1)}, bf16[32,896]{1,0:T(8,128)(2,1)}, bf16[1,128,32]{2,1,0:T(8,128)(2,1)}, f32[2,32,128]{2,1,0:T(8,128)}, f32[16,896]{1,0:T(8,128)}) custom-call(bf16[2,16,896]{2,1,0:T(8,128)(2,1)} %bitcast.75, s32[2,2,2,128]{3,2,1,0:T(2,128)} %bitcast.76, f32[2,2,2,128]{3,2,1,0:T(2,128)} %bitcast.77, f32[1,7168]{1,0:T(1,128)} %gain_hbm.1), custom_call_target="tpu_custom_call" | custom-call | tf_op jit(solution)/shard_map/prepare/pallas_call | solution.py:107
  2.1 15.7 %all-to-all-start = ((bf16[8,16,896]{2,1,0:T(8,128)(2,1)}), bf16[8,16,896]{2,1,0:T(8,128)(2,1)S(1)}, u32[]{:S(2)}, u32[]{:S(2)}) async-start(bf16[8,16,896]{2,1,0:T(8,128)(2,1)} %bitcast.74), calls=%async_computation | async-start | bytes 458752 | tf_op jit(solution)/shard_map/all_to_all | solution.py:18
  17.8 16.4 %all-to-all-done = bf16[8,16,896]{2,1,0:T(8,128)(2,1)S(1)} async-done(((bf16[8,16,896]{2,1,0:T(8,128)(2,1)}), bf16[8,16,896]{2,1,0:T(8,128)(2,1)S(1)}, u32[]{:S(2)}, u32[]{:S(2)}) %all-to-all-start) | async-done | bytes 229408 | tf_op jit(solution)/shard_map/all_to_all | solution.py:18
  34.2 0.9 fusion.21
  35.1 0.1 reshape.79
  35.2 0.0 copy-done
  35.3 0.4 fusion.8
  35.7 0.0 copy-start.1
  35.7 0.1 select_convert_fusion.1
  35.9 9.9 %all_to_all.40 = bf16[8,16,1152]{2,1,0:T(8,128)(2,1)S(1)} all-to-all(bf16[8,16,1152]{2,1,0:T(8,128)(2,1)S(1)} %bitcast.63), channel_id=1, replica_groups={{0,1,2,3,4,5,6,7},{8,9,10,11,12,13,14,15},{16,17,18,19,20,21,22,23},{24..., dimensions={0} | all-to-all | bytes 589824 | tf_op jit(solution)/shard_map/all_to_all | solution.py:23
  45.8 0.2 fusion.40
  46.0 0.0 copy-start.4
  46.0 0.0 copy-start.5
  46.0 0.1 multiply_convert_fusion.1
  46.1 0.0 copy-start.6
  46.1 8.5 %all_to_all.41 = bf16[8,16,1024]{2,1,0:T(8,128)(2,1)S(1)} all-to-all(bf16[8,16,1024]{2,1,0:T(8,128)(2,1)S(1)} %broadcast_in_dim.61), channel_id=1, replica_groups={{0,1,2,3,4,5,6,7},{8,9,10,11,12,13,14,15},{16,17,18,19,20,21,22,23},{24..., dimensions={0} | all-to-all | bytes 524288 | tf_op jit(solution)/shard_map/all_to_all | solution.py:23
  54.6 0.0 copy-done.1
  54.6 0.5 fusion.14
  55.1 23.3 %all_to_all.42 = bf16[8,16,896]{2,1,0:T(8,128)(2,1)S(1)} all-to-all(bf16[8,16,896]{2,1,0:T(8,128)(2,1)S(1)} %bitcast.67), channel_id=1, replica_groups={{0,8,16,24,32,40,48,56},{1,9,17,25,33,41,49,57},{2,10,18,26,34,42,50,58..., dimensions={0} | all-to-all | bytes 458752 | tf_op jit(solution)/shard_map/all_to_all | solution.py:18
  78.4 0.0 copy-done.4
  78.4 0.0 copy-done.5
  78.4 0.2 fusion.20
  78.7 8.6 %collective-permute-start = (bf16[16,896]{1,0:T(8,128)(2,1)S(1)}, bf16[16,896]{1,0:T(8,128)(2,1)S(1)}, u32[]{:S(2)}, u32[]{:S(2)}) collective-permute-start(bf16[16,896]{1,0:T(8,128)(2,1)S(1)} %get-tuple-element.24), channel_id=1, source_target_pairs={{0,448},{64,128},{128,64},{192,256},{256,192},{320,384},{384,320},... | collective-permute-start | bytes 86024 | tf_op jit(solution)/shard_map/ppermute | solution.py:31
  87.2 1.9 %collective-permute-start.1 = (bf16[16,896]{1,0:T(8,128)(2,1)S(1)}, bf16[16,896]{1,0:T(8,128)(2,1)S(1)}, u32[]{:S(2)}, u32[]{:S(2)}) collective-permute-start(bf16[16,896]{1,0:T(8,128)(2,1)S(1)} %get-tuple-element.23), channel_id=1, source_target_pairs={{0,64},{64,0},{128,192},{192,128},{256,320},{320,256},{384,448},{4... | collective-permute-start | bytes 86024 | tf_op jit(solution)/shard_map/ppermute | solution.py:31
  89.2 0.0 collective-permute-done
  89.2 1.1 collective-permute-done.1
  90.3 0.0 copy-done.6
  90.3 0.2 convolution_convert_fusion
  90.5 20.8 %all_to_all.43 = bf16[8,16,896]{2,1,0:T(8,128)(2,1)S(1)} all-to-all(bf16[8,16,896]{2,1,0:T(8,128)(2,1)S(1)} %bitcast.71), channel_id=1, replica_groups={{0,8,16,24,32,40,48,56},{1,9,17,25,33,41,49,57},{2,10,18,26,34,42,50,58..., dimensions={0} | all-to-all | bytes 458752 | tf_op jit(solution)/shard_map/all_to_all | solution.py:18
  111.3 0.0 copy-done.3
  111.4 0.1 fusion.23
  111.5 0.5 fusion.11
  112.0 0.1 reshape.86
  112.0 0.1 select_convert_fusion
  112.2 9.0 %all_to_all.44 = bf16[8,16,1152]{2,1,0:T(8,128)(2,1)S(1)} all-to-all(bf16[8,16,1152]{2,1,0:T(8,128)(2,1)S(1)} %bitcast.64), channel_id=1, replica_groups={{0,1,2,3,4,5,6,7},{8,9,10,11,12,13,14,15},{16,17,18,19,20,21,22,23},{24..., dimensions={0} | all-to-all | bytes 589824 | tf_op jit(solution)/shard_map/all_to_all | solution.py:23
  121.3 0.2 fusion.36
  121.4 0.1 multiply_convert_fusion
  121.6 8.5 %all_to_all.45 = bf16[8,16,1024]{2,1,0:T(8,128)(2,1)S(1)} all-to-all(bf16[8,16,1024]{2,1,0:T(8,128)(2,1)S(1)} %broadcast_in_dim.64), channel_id=1, replica_groups={{0,1,2,3,4,5,6,7},{8,9,10,11,12,13,14,15},{16,17,18,19,20,21,22,23},{24..., dimensions={0} | all-to-all | bytes 524288 | tf_op jit(solution)/shard_map/all_to_all | solution.py:23
  130.1 0.0 copy-done.2
  130.1 0.4 fusion.17
  130.5 19.5 %all_to_all.46 = bf16[8,16,896]{2,1,0:T(8,128)(2,1)S(1)} all-to-all(bf16[8,16,896]{2,1,0:T(8,128)(2,1)S(1)} %bitcast.68), channel_id=1, replica_groups={{0,8,16,24,32,40,48,56},{1,9,17,25,33,41,49,57},{2,10,18,26,34,42,50,58..., dimensions={0} | all-to-all | bytes 458752 | tf_op jit(solution)/shard_map/all_to_all | solution.py:18
  150.1 0.2 add_convert_fusion
  150.3 7.5 %collective-permute-start.2 = (bf16[16,896]{1,0:T(8,128)(2,1)S(1)}, bf16[16,896]{1,0:T(8,128)(2,1)S(1)}, u32[]{:S(2)}, u32[]{:S(2)}) collective-permute-start(bf16[16,896]{1,0:T(8,128)(2,1)S(1)} %get-tuple-element.21), channel_id=1, source_target_pairs={{0,64},{64,0},{128,192},{192,128},{256,320},{320,256},{384,448},{4... | collective-permute-start | bytes 86024 | tf_op jit(solution)/shard_map/ppermute | solution.py:31
  157.8 3.9 %collective-permute-start.3 = (bf16[16,896]{1,0:T(8,128)(2,1)S(1)}, bf16[16,896]{1,0:T(8,128)(2,1)S(1)}, u32[]{:S(2)}, u32[]{:S(2)}) collective-permute-start(bf16[16,896]{1,0:T(8,128)(2,1)S(1)} %get-tuple-element.22), channel_id=1, source_target_pairs={{0,448},{64,128},{128,64},{192,256},{256,192},{320,384},{384,320},... | collective-permute-start | bytes 86024 | tf_op jit(solution)/shard_map/ppermute | solution.py:31
  161.7 0.0 collective-permute-done.2
  161.7 1.8 %collective-permute-done.3 = bf16[16,896]{1,0:T(8,128)(2,1)S(1)} collective-permute-done((bf16[16,896]{1,0:T(8,128)(2,1)S(1)}, bf16[16,896]{1,0:T(8,128)(2,1)S(1)}, u32[]{:S(2)}, u32[]{:S(2)}) %collective-permute-start.3) | collective-permute-done | bytes 28704 | tf_op jit(solution)/shard_map/ppermute | solution.py:31
  163.6 0.6 maximum_bitcast_fusion
  (16 shorter events, 0.2 us)
Async XLA Ops:
  0.0 35.2 %copy-start = (bf16[1,1,896,1024]{3,2,1,0:T(8,128)(2,1)S(1)}, bf16[1,1,896,1024]{3,2,1,0:T(8,128)(2,1)}, u32[]{:S(2)}) copy-start(bf16[1,1,896,1024]{3,2,1,0:T(8,128)(2,1)} %param.7) | copy-start | bytes 5505028
  2.1 32.1 %all-to-all-start = ((bf16[8,16,896]{2,1,0:T(8,128)(2,1)}), bf16[8,16,896]{2,1,0:T(8,128)(2,1)S(1)}, u32[]{:S(2)}, u32[]{:S(2)}) async-start(bf16[8,16,896]{2,1,0:T(8,128)(2,1)} %bitcast.74), calls=%async_computation | async-start | bytes 458752 | tf_op jit(solution)/shard_map/all_to_all | solution.py:18
  35.7 18.9 %copy-start.1 = (bf16[1,1,1024,896]{3,2,1,0:T(8,128)(2,1)S(1)}, bf16[1,1,1024,896]{3,2,1,0:T(8,128)(2,1)}, u32[]{:S(2)}) copy-start(bf16[1,1,1024,896]{3,2,1,0:T(8,128)(2,1)} %param.8) | copy-start | bytes 5505028
  46.0 32.4 %copy-start.4 = (bf16[32,896]{1,0:T(8,128)(2,1)S(1)}, bf16[32,896]{1,0:T(8,128)(2,1)}, u32[]{:S(2)}) copy-start(bf16[32,896]{1,0:T(8,128)(2,1)} %get-tuple-element.10) | copy-start | bytes 172036
  46.0 32.4 %copy-start.5 = (f32[2,32,128]{2,1,0:T(8,128)S(1)}, f32[2,32,128]{2,1,0:T(8,128)}, u32[]{:S(2)}) copy-start(f32[2,32,128]{2,1,0:T(8,128)} %get-tuple-element.11) | copy-start | bytes 98308
  46.1 44.2 %copy-start.6 = (bf16[1,128,32]{2,1,0:T(8,128)(2,1)S(1)}, bf16[1,128,32]{2,1,0:T(8,128)(2,1)}, u32[]{:S(2)}) copy-start(bf16[1,128,32]{2,1,0:T(8,128)(2,1)} %get-tuple-element.14) | copy-start | bytes 24580
  54.6 56.7 %copy-start.3 = (f32[16,896]{1,0:T(8,128)S(1)}, f32[16,896]{1,0:T(8,128)}, u32[]{:S(2)}) copy-start(f32[16,896]{1,0:T(8,128)} %get-tuple-element.13) | copy-start | bytes 172036
  78.7 10.5 %collective-permute-start = (bf16[16,896]{1,0:T(8,128)(2,1)S(1)}, bf16[16,896]{1,0:T(8,128)(2,1)S(1)}, u32[]{:S(2)}, u32[]{:S(2)}) collective-permute-start(bf16[16,896]{1,0:T(8,128)(2,1)S(1)} %get-tuple-element.24), channel_id=1, source_target_pairs={{0,448},{64,128},{128,64},{192,256},{256,192},{320,384},{384,320},... | collective-permute-start | bytes 86024 | tf_op jit(solution)/shard_map/ppermute | solution.py:31
  87.2 3.1 %collective-permute-start.1 = (bf16[16,896]{1,0:T(8,128)(2,1)S(1)}, bf16[16,896]{1,0:T(8,128)(2,1)S(1)}, u32[]{:S(2)}, u32[]{:S(2)}) collective-permute-start(bf16[16,896]{1,0:T(8,128)(2,1)S(1)} %get-tuple-element.23), channel_id=1, source_target_pairs={{0,64},{64,0},{128,192},{192,128},{256,320},{320,256},{384,448},{4... | collective-permute-start | bytes 86024 | tf_op jit(solution)/shard_map/ppermute | solution.py:31
  112.0 18.0 %copy-start.2 = (bf16[1,1,1024,896]{3,2,1,0:T(8,128)(2,1)S(1)}, bf16[1,1,1024,896]{3,2,1,0:T(8,128)(2,1)}, u32[]{:S(2)}) copy-start(bf16[1,1,1024,896]{3,2,1,0:T(8,128)(2,1)} %param.8) | copy-start | bytes 5505028
  150.3 11.4 %collective-permute-start.2 = (bf16[16,896]{1,0:T(8,128)(2,1)S(1)}, bf16[16,896]{1,0:T(8,128)(2,1)S(1)}, u32[]{:S(2)}, u32[]{:S(2)}) collective-permute-start(bf16[16,896]{1,0:T(8,128)(2,1)S(1)} %get-tuple-element.21), channel_id=1, source_target_pairs={{0,64},{64,0},{128,192},{192,128},{256,320},{320,256},{384,448},{4... | collective-permute-start | bytes 86024 | tf_op jit(solution)/shard_map/ppermute | solution.py:31
  157.8 5.8 %collective-permute-start.3 = (bf16[16,896]{1,0:T(8,128)(2,1)S(1)}, bf16[16,896]{1,0:T(8,128)(2,1)S(1)}, u32[]{:S(2)}, u32[]{:S(2)}) collective-permute-start(bf16[16,896]{1,0:T(8,128)(2,1)S(1)} %get-tuple-element.22), channel_id=1, source_target_pairs={{0,448},{64,128},{128,64},{192,256},{256,192},{320,384},{384,320},... | collective-permute-start | bytes 86024 | tf_op jit(solution)/shard_map/ppermute | solution.py:31

commit v4 on v2

--- a/solution.py
+++ b/solution.py
@@ -9,12 +9,14 @@
 SLICES = 8
 CAP = 8
 LANES = 128
+FIRST = 5
 VMEM = pl.BlockSpec(memory_space=pltpu.VMEM)
 HBM = pl.BlockSpec(memory_space=pltpu.HBM)
 
 
 def over_groups(value):
-    members = [[g * SLICES + s for g in range(GROUPS)] for s in range(SLICES)]
+    order = [(i + FIRST) % GROUPS for i in range(GROUPS)]
+    members = [[g * SLICES + s for g in order] for s in range(SLICES)]
     return lax.all_to_all(value, "expert", 0, 0, axis_index_groups=members, tiled=True)
 
 
@@ -65,7 +67,8 @@
 
     row = lax.broadcasted_iota(jnp.int32, (slots, every), 0)
     lane = lax.broadcasted_iota(jnp.int32, (slots, every), 1)
-    expert, stream, slot = row // (streams * CAP), row // CAP % streams, row % CAP
+    expert = (row // (streams * CAP) + FIRST) % GROUPS
+    stream, slot = row // CAP % streams, row % CAP
     mine = lane // tokens == stream
     earlier_row = lax.broadcasted_iota(jnp.int32, (every, every), 0)
     earlier_lane = lax.broadcasted_iota(jnp.int32, (every, every), 1)

time: 160 us -> 154 us (0.963)
  waiting for transfers between devices: 21.6 us -> 14.1 us
    all_to_all x1, waiting for transfers between devices: 15 us -> 7.49 us  [over_groups(): lax.all_to_all(value, 'expert', 0, 0, axis_index_groups=members, tiled=True)]
    all_to_all x4, blocking collectives: 38 us -> 40.2 us  [over_slices(): lax.all_to_all(value, 'expert', 0, 0, axis_index_groups=members, tiled=True)]
where the time goes in v4:
time: 154 us; the launch traced here: 153 us
  blocking collectives  102 us (66%)
  starting transfers between devices  29.4 us (19%)
  waiting for transfers between devices  14.1 us (9%)
  other arithmetic  2.51 us (2%)
  matrix products  2.46 us (2%)
  Pallas kernels  2.12 us (1%)
    all_to_all x3, blocking collectives, over_groups(): lax.all_to_all(value, 'expert', 0, 0, axis_index_groups=members, tiled=True)  62.1 us
    all_to_all x4, blocking collectives, over_slices(): lax.all_to_all(value, 'expert', 0, 0, axis_index_groups=members, tiled=True)  40.2 us
    all_to_all x1, starting transfers between devices, over_groups(): lax.all_to_all(value, 'expert', 0, 0, axis_index_groups=members, tiled=True)  16.9 us
    ppermute x4, starting transfers between devices, shifted(): lax.ppermute(value, 'pipe', [(i, (i + steps) % count) for i in range(coun...  12.5 us
    all_to_all x1, waiting for transfers between devices, over_groups(): lax.all_to_all(value, 'expert', 0, 0, axis_index_groups=members, tiled=True)  7.49 us
    ppermute x4, waiting for transfers between devices, shifted(): lax.ppermute(value, 'pipe', [(i, (i + steps) % count) for i in range(coun...  6.58 us
  transfers between devices with their start and end apart: 5, of which 5 were waited for; matrix products, arithmetic and copies ran while one was open for 0% of the time, Pallas kernels for 0%

profile of v4, /device:TPU:1, one launch (start us, length us, event | category | flops | bytes accessed | tf_op | source)
XLA Modules:
  0.0 153.4 jit_solution(9213299001848871133)
XLA Ops:
  0.0 0.0 copy-start
  0.0 2.1 %prepare.1 = (bf16[128,896]{1,0:T(8,128)(2,1)}, bf16[1,128,32]{2,1,0:T(8,128)(2,1)}, f32[2,32,128]{2,1,0:T(8,128)}, f32[1,896]{1,0:T(1,128)}) custom-call(bf16[32,896]{1,0:T(8,128)(2,1)} %bitcast.70, s32[2,2,2,128]{3,2,1,0:T(2,128)} %bitcast.72, f32[2,2,2,128]{3,2,1,0:T(2,128)} %bitcast.73, f32[1,7168]{1,0:T(1,128)} %gain_hbm.1), custom_call_target="tpu_custom_call" | custom-call | tf_op jit(solution)/shard_map/prepare/pallas_call | solution.py:109
  2.1 16.9 %all-to-all-start = ((bf16[8,16,896]{2,1,0:T(8,128)(2,1)}), bf16[8,16,896]{2,1,0:T(8,128)(2,1)S(1)}, u32[]{:S(2)}, u32[]{:S(2)}) async-start(bf16[8,16,896]{2,1,0:T(8,128)(2,1)} %bitcast.69), calls=%async_computation | async-start | bytes 458752 | tf_op jit(solution)/shard_map/all_to_all | solution.py:20
  19.0 0.7 reduce.2
  19.7 7.5 %all-to-all-done = bf16[8,16,896]{2,1,0:T(8,128)(2,1)S(1)} async-done(((bf16[8,16,896]{2,1,0:T(8,128)(2,1)}), bf16[8,16,896]{2,1,0:T(8,128)(2,1)S(1)}, u32[]{:S(2)}, u32[]{:S(2)}) %all-to-all-start) | async-done | bytes 229408 | tf_op jit(solution)/shard_map/all_to_all | solution.py:20
  27.2 0.1 fusion.21
  27.3 0.1 reduce_sum.41
  27.4 0.0 copy-done
  27.4 0.4 fusion.8
  27.9 0.0 copy-start.1
  27.9 0.1 select_convert_fusion.1
  28.0 13.5 %all_to_all.40 = bf16[8,16,1152]{2,1,0:T(8,128)(2,1)S(1)} all-to-all(bf16[8,16,1152]{2,1,0:T(8,128)(2,1)S(1)} %bitcast.58), channel_id=1, replica_groups={{0,1,2,3,4,5,6,7},{8,9,10,11,12,13,14,15},{16,17,18,19,20,21,22,23},{24..., dimensions={0} | all-to-all | bytes 589824 | tf_op jit(solution)/shard_map/all_to_all | solution.py:25
  41.6 0.2 fusion.40
  41.8 0.0 copy-start.4
  41.8 0.1 multiply_convert_fusion.1
  41.9 0.0 copy-start.5
  41.9 8.5 %all_to_all.41 = bf16[8,16,1024]{2,1,0:T(8,128)(2,1)S(1)} all-to-all(bf16[8,16,1024]{2,1,0:T(8,128)(2,1)S(1)} %broadcast_in_dim.58), channel_id=1, replica_groups={{0,1,2,3,4,5,6,7},{8,9,10,11,12,13,14,15},{16,17,18,19,20,21,22,23},{24..., dimensions={0} | all-to-all | bytes 524288 | tf_op jit(solution)/shard_map/all_to_all | solution.py:25
  50.4 0.0 copy-done.1
  50.4 0.4 fusion.14
  50.8 21.3 %all_to_all.42 = bf16[8,16,896]{2,1,0:T(8,128)(2,1)S(1)} all-to-all(bf16[8,16,896]{2,1,0:T(8,128)(2,1)S(1)} %bitcast.64), channel_id=1, replica_groups={{40,48,56,0,8,16,24,32},{41,49,57,1,9,17,25,33},{42,50,58,2,10,18,26,34..., dimensions={0} | all-to-all | bytes 458752 | tf_op jit(solution)/shard_map/all_to_all | solution.py:20
  72.1 0.0 copy-done.3
  72.1 0.0 copy-done.4
  72.1 0.2 fusion.20
  72.4 6.3 %collective-permute-start = (bf16[16,896]{1,0:T(8,128)(2,1)S(1)}, bf16[16,896]{1,0:T(8,128)(2,1)S(1)}, u32[]{:S(2)}, u32[]{:S(2)}) collective-permute-start(bf16[16,896]{1,0:T(8,128)(2,1)S(1)} %get-tuple-element.20), channel_id=1, source_target_pairs={{0,64},{64,128},{128,192},{192,256},{256,320},{320,384},{384,448},... | collective-permute-start | bytes 86024 | tf_op jit(solution)/shard_map/ppermute | solution.py:30
  78.7 0.0 collective-permute-start.1
  78.7 1.0 collective-permute-done
  79.7 2.3 %collective-permute-done.1 = bf16[16,896]{1,0:T(8,128)(2,1)S(1)} collective-permute-done((bf16[16,896]{1,0:T(8,128)(2,1)S(1)}, bf16[16,896]{1,0:T(8,128)(2,1)S(1)}, u32[]{:S(2)}, u32[]{:S(2)}) %collective-permute-start.1) | collective-permute-done | bytes 28704 | tf_op jit(solution)/shard_map/ppermute | solution.py:30
  82.0 0.0 copy-done.5
  82.0 0.2 convolution_convert_fusion
  82.2 22.6 %all_to_all.43 = bf16[8,16,896]{2,1,0:T(8,128)(2,1)S(1)} all-to-all(bf16[8,16,896]{2,1,0:T(8,128)(2,1)S(1)} %bitcast.66), channel_id=1, replica_groups={{40,48,56,0,8,16,24,32},{41,49,57,1,9,17,25,33},{42,50,58,2,10,18,26,34..., dimensions={0} | all-to-all | bytes 458752 | tf_op jit(solution)/shard_map/all_to_all | solution.py:20
  104.8 0.1 fusion.23
  104.9 0.1 reduce_sum.44
  105.0 0.5 fusion.11
  105.5 0.0 copy-start.2
  105.5 0.1 select_convert_fusion
  105.6 9.2 %all_to_all.44 = bf16[8,16,1152]{2,1,0:T(8,128)(2,1)S(1)} all-to-all(bf16[8,16,1152]{2,1,0:T(8,128)(2,1)S(1)} %bitcast.59), channel_id=1, replica_groups={{0,1,2,3,4,5,6,7},{8,9,10,11,12,13,14,15},{16,17,18,19,20,21,22,23},{24..., dimensions={0} | all-to-all | bytes 589824 | tf_op jit(solution)/shard_map/all_to_all | solution.py:25
  114.9 0.2 fusion.36
  115.1 0.1 multiply_convert_fusion
  115.3 9.0 %all_to_all.45 = bf16[8,16,1024]{2,1,0:T(8,128)(2,1)S(1)} all-to-all(bf16[8,16,1024]{2,1,0:T(8,128)(2,1)S(1)} %broadcast_in_dim.61), channel_id=1, replica_groups={{0,1,2,3,4,5,6,7},{8,9,10,11,12,13,14,15},{16,17,18,19,20,21,22,23},{24..., dimensions={0} | all-to-all | bytes 524288 | tf_op jit(solution)/shard_map/all_to_all | solution.py:25
  124.3 0.0 copy-done.2
  124.3 0.5 fusion.17
  124.8 18.3 %all_to_all.46 = bf16[8,16,896]{2,1,0:T(8,128)(2,1)S(1)} all-to-all(bf16[8,16,896]{2,1,0:T(8,128)(2,1)S(1)} %bitcast.65), channel_id=1, replica_groups={{40,48,56,0,8,16,24,32},{41,49,57,1,9,17,25,33},{42,50,58,2,10,18,26,34..., dimensions={0} | all-to-all | bytes 458752 | tf_op jit(solution)/shard_map/all_to_all | solution.py:20
  143.0 0.2 add_convert_fusion
  143.3 6.1 %collective-permute-start.2 = (bf16[16,896]{1,0:T(8,128)(2,1)S(1)}, bf16[16,896]{1,0:T(8,128)(2,1)S(1)}, u32[]{:S(2)}, u32[]{:S(2)}) collective-permute-start(bf16[16,896]{1,0:T(8,128)(2,1)S(1)} %get-tuple-element.17), channel_id=1, source_target_pairs={{0,64},{64,128},{128,192},{192,256},{256,320},{320,384},{384,448},... | collective-permute-start | bytes 86024 | tf_op jit(solution)/shard_map/ppermute | solution.py:30
  149.4 0.0 collective-permute-start.3
  149.4 1.0 collective-permute-done.2
  150.4 2.3 %collective-permute-done.3 = bf16[16,896]{1,0:T(8,128)(2,1)S(1)} collective-permute-done((bf16[16,896]{1,0:T(8,128)(2,1)S(1)}, bf16[16,896]{1,0:T(8,128)(2,1)S(1)}, u32[]{:S(2)}, u32[]{:S(2)}) %collective-permute-start.3) | collective-permute-done | bytes 28704 | tf_op jit(solution)/shard_map/ppermute | solution.py:30
  152.7 0.6 pad_maximum_fusion.2
  (14 shorter events, 0.2 us)
Async XLA Ops:
  0.0 27.4 %copy-start = (bf16[1,1,896,1024]{3,2,1,0:T(8,128)(2,1)S(1)}, bf16[1,1,896,1024]{3,2,1,0:T(8,128)(2,1)}, u32[]{:S(2)}) copy-start(bf16[1,1,896,1024]{3,2,1,0:T(8,128)(2,1)} %param.7) | copy-start | bytes 5505028
  2.1 25.1 %all-to-all-start = ((bf16[8,16,896]{2,1,0:T(8,128)(2,1)}), bf16[8,16,896]{2,1,0:T(8,128)(2,1)S(1)}, u32[]{:S(2)}, u32[]{:S(2)}) async-start(bf16[8,16,896]{2,1,0:T(8,128)(2,1)} %bitcast.69), calls=%async_computation | async-start | bytes 458752 | tf_op jit(solution)/shard_map/all_to_all | solution.py:20
  27.9 22.5 %copy-start.1 = (bf16[1,1,1024,896]{3,2,1,0:T(8,128)(2,1)S(1)}, bf16[1,1,1024,896]{3,2,1,0:T(8,128)(2,1)}, u32[]{:S(2)}) copy-start(bf16[1,1,1024,896]{3,2,1,0:T(8,128)(2,1)} %param.8) | copy-start | bytes 5505028
  41.7 30.4 %copy-start.3 = (bf16[1,2,1,16,896]{4,3,2,1,0:T(8,128)(2,1)S(1)}, bf16[1,2,1,16,896]{4,3,2,1,0:T(8,128)(2,1)}, u32[]{:S(2)}) copy-start(bf16[1,2,1,16,896]{4,3,2,1,0:T(8,128)(2,1)} %param.6) | copy-start | bytes 172036
  41.8 30.4 %copy-start.4 = (f32[2,32,128]{2,1,0:T(8,128)S(1)}, f32[2,32,128]{2,1,0:T(8,128)}, u32[]{:S(2)}) copy-start(f32[2,32,128]{2,1,0:T(8,128)} %get-tuple-element.9) | copy-start | bytes 98308
  41.9 40.1 %copy-start.5 = (bf16[1,128,32]{2,1,0:T(8,128)(2,1)S(1)}, bf16[1,128,32]{2,1,0:T(8,128)(2,1)}, u32[]{:S(2)}) copy-start(bf16[1,128,32]{2,1,0:T(8,128)(2,1)} %get-tuple-element.12) | copy-start | bytes 24580
  72.4 7.3 %collective-permute-start = (bf16[16,896]{1,0:T(8,128)(2,1)S(1)}, bf16[16,896]{1,0:T(8,128)(2,1)S(1)}, u32[]{:S(2)}, u32[]{:S(2)}) collective-permute-start(bf16[16,896]{1,0:T(8,128)(2,1)S(1)} %get-tuple-element.20), channel_id=1, source_target_pairs={{0,64},{64,128},{128,192},{192,256},{256,320},{320,384},{384,448},... | collective-permute-start | bytes 86024 | tf_op jit(solution)/shard_map/ppermute | solution.py:30
  78.7 3.3 %collective-permute-start.1 = (bf16[16,896]{1,0:T(8,128)(2,1)S(1)}, bf16[16,896]{1,0:T(8,128)(2,1)S(1)}, u32[]{:S(2)}, u32[]{:S(2)}) collective-permute-start(bf16[16,896]{1,0:T(8,128)(2,1)S(1)} %get-tuple-element.19), channel_id=1, source_target_pairs={{0,448},{64,0},{128,64},{192,128},{256,192},{320,256},{384,320},{4... | collective-permute-start | bytes 86024 | tf_op jit(solution)/shard_map/ppermute | solution.py:30
  105.5 18.8 %copy-start.2 = (bf16[1,1,1024,896]{3,2,1,0:T(8,128)(2,1)S(1)}, bf16[1,1,1024,896]{3,2,1,0:T(8,128)(2,1)}, u32[]{:S(2)}) copy-start(bf16[1,1,1024,896]{3,2,1,0:T(8,128)(2,1)} %param.8) | copy-start | bytes 5505028
  143.3 7.1 %collective-permute-start.2 = (bf16[16,896]{1,0:T(8,128)(2,1)S(1)}, bf16[16,896]{1,0:T(8,128)(2,1)S(1)}, u32[]{:S(2)}, u32[]{:S(2)}) collective-permute-start(bf16[16,896]{1,0:T(8,128)(2,1)S(1)} %get-tuple-element.17), channel_id=1, source_target_pairs={{0,64},{64,128},{128,192},{192,256},{256,320},{320,384},{384,448},... | collective-permute-start | bytes 86024 | tf_op jit(solution)/shard_map/ppermute | solution.py:30
  149.4 3.3 %collective-permute-start.3 = (bf16[16,896]{1,0:T(8,128)(2,1)S(1)}, bf16[16,896]{1,0:T(8,128)(2,1)S(1)}, u32[]{:S(2)}, u32[]{:S(2)}) collective-permute-start(bf16[16,896]{1,0:T(8,128)(2,1)S(1)} %get-tuple-element.18), channel_id=1, source_target_pairs={{0,448},{64,0},{128,64},{192,128},{256,192},{320,256},{384,320},{4... | collective-permute-start | bytes 86024 | tf_op jit(solution)/shard_map/ppermute | solution.py:30

commit v5 on v4

--- a/solution.py
+++ b/solution.py
@@ -9,7 +9,8 @@
 SLICES = 8
 CAP = 8
 LANES = 128
-FIRST = 5
+FIRST = 4
+FIRST_SLICE = 3
 VMEM = pl.BlockSpec(memory_space=pltpu.VMEM)
 HBM = pl.BlockSpec(memory_space=pltpu.HBM)
 
@@ -21,7 +22,8 @@
 
 
 def over_slices(value):
-    members = [[g * SLICES + s for s in range(SLICES)] for g in range(GROUPS)]
+    order = [(i + FIRST_SLICE) % SLICES for i in range(SLICES)]
+    members = [[g * SLICES + s for s in order] for g in range(GROUPS)]
     return lax.all_to_all(value, "expert", 0, 0, axis_index_groups=members, tiled=True)
 
 

time: 154 us -> 151 us (0.981)
  starting transfers between devices: 29.4 us -> 24.7 us
  waiting for transfers between devices: 14.1 us -> 16.9 us
    ppermute x4, starting transfers between devices: 12.5 us -> 6.02 us  [shifted(): lax.ppermute(value, 'pipe', [(i, (i + steps) % count) for i in range(coun...]
    all_to_all x4, blocking collectives: 40.2 us -> 36.9 us  [over_slices(): lax.all_to_all(value, 'expert', 0, 0, axis_index_groups=members, tiled=True)]
    all_to_all x1, waiting for transfers between devices: 7.49 us -> 10.3 us  [over_groups(): lax.all_to_all(value, 'expert', 0, 0, axis_index_groups=members, tiled=True)]
    all_to_all x3, blocking collectives: 62.1 us -> 64.2 us  [over_groups(): lax.all_to_all(value, 'expert', 0, 0, axis_index_groups=members, tiled=True)]
    all_to_all x1, starting transfers between devices: 16.9 us -> 18.7 us  [over_groups(): lax.all_to_all(value, 'expert', 0, 0, axis_index_groups=members, tiled=True)]
where the time goes in v5:
time: 151 us; the launch traced here: 150 us
  blocking collectives  101 us (67%)
  starting transfers between devices  24.7 us (16%)
  waiting for transfers between devices  16.9 us (11%)
  other arithmetic  2.51 us (2%)
  matrix products  2.45 us (2%)
  Pallas kernels  2.12 us (1%)
    all_to_all x3, blocking collectives, over_groups(): lax.all_to_all(value, 'expert', 0, 0, axis_index_groups=members, tiled=True)  64.2 us
    all_to_all x4, blocking collectives, over_slices(): lax.all_to_all(value, 'expert', 0, 0, axis_index_groups=members, tiled=True)  36.9 us
    all_to_all x1, starting transfers between devices, over_groups(): lax.all_to_all(value, 'expert', 0, 0, axis_index_groups=members, tiled=True)  18.7 us
    all_to_all x1, waiting for transfers between devices, over_groups(): lax.all_to_all(value, 'expert', 0, 0, axis_index_groups=members, tiled=True)  10.3 us
    ppermute x4, waiting for transfers between devices, shifted(): lax.ppermute(value, 'pipe', [(i, (i + steps) % count) for i in range(coun...  6.58 us
    ppermute x4, starting transfers between devices, shifted(): lax.ppermute(value, 'pipe', [(i, (i + steps) % count) for i in range(coun...  6.02 us
  transfers between devices with their start and end apart: 5, of which 5 were waited for; matrix products, arithmetic and copies ran while one was open for 0% of the time, Pallas kernels for 0%

profile of v5, /device:TPU:1, one launch (start us, length us, event | category | flops | bytes accessed | tf_op | source)
XLA Modules:
  0.0 150.3 jit_solution(8826938283403767022)
XLA Ops:
  0.0 0.0 copy-start
  0.0 2.1 %prepare.1 = (bf16[128,896]{1,0:T(8,128)(2,1)}, bf16[1,128,32]{2,1,0:T(8,128)(2,1)}, f32[2,32,128]{2,1,0:T(8,128)}, f32[1,896]{1,0:T(1,128)}) custom-call(bf16[32,896]{1,0:T(8,128)(2,1)} %bitcast.70, s32[2,2,2,128]{3,2,1,0:T(2,128)} %bitcast.72, f32[2,2,2,128]{3,2,1,0:T(2,128)} %bitcast.73, f32[1,7168]{1,0:T(1,128)} %gain_hbm.1), custom_call_target="tpu_custom_call" | custom-call | tf_op jit(solution)/shard_map/prepare/pallas_call | solution.py:111
  2.1 18.7 %all-to-all-start = ((bf16[8,16,896]{2,1,0:T(8,128)(2,1)}), bf16[8,16,896]{2,1,0:T(8,128)(2,1)S(1)}, u32[]{:S(2)}, u32[]{:S(2)}) async-start(bf16[8,16,896]{2,1,0:T(8,128)(2,1)} %bitcast.69), calls=%async_computation | async-start | bytes 458752 | tf_op jit(solution)/shard_map/all_to_all | solution.py:21
  20.8 0.7 reduce.2
  21.5 10.3 %all-to-all-done = bf16[8,16,896]{2,1,0:T(8,128)(2,1)S(1)} async-done(((bf16[8,16,896]{2,1,0:T(8,128)(2,1)}), bf16[8,16,896]{2,1,0:T(8,128)(2,1)S(1)}, u32[]{:S(2)}, u32[]{:S(2)}) %all-to-all-start) | async-done | bytes 229408 | tf_op jit(solution)/shard_map/all_to_all | solution.py:21
  31.8 0.1 fusion.21
  32.0 0.1 reduce_sum.41
  32.1 0.0 copy-done
  32.1 0.4 fusion.8
  32.5 0.0 copy-start.1
  32.6 0.1 select_convert_fusion.1
  32.7 9.9 %all_to_all.40 = bf16[8,16,1152]{2,1,0:T(8,128)(2,1)S(1)} all-to-all(bf16[8,16,1152]{2,1,0:T(8,128)(2,1)S(1)} %bitcast.58), channel_id=1, replica_groups={{3,4,5,6,7,0,1,2},{11,12,13,14,15,8,9,10},{19,20,21,22,23,16,17,18},{27..., dimensions={0} | all-to-all | bytes 589824 | tf_op jit(solution)/shard_map/all_to_all | solution.py:27
  42.6 0.2 fusion.40
  42.8 0.0 copy-start.4
  42.8 0.1 multiply_convert_fusion.1
  43.0 0.0 copy-start.5
  43.0 8.4 %all_to_all.41 = bf16[8,16,1024]{2,1,0:T(8,128)(2,1)S(1)} all-to-all(bf16[8,16,1024]{2,1,0:T(8,128)(2,1)S(1)} %broadcast_in_dim.58), channel_id=1, replica_groups={{3,4,5,6,7,0,1,2},{11,12,13,14,15,8,9,10},{19,20,21,22,23,16,17,18},{27..., dimensions={0} | all-to-all | bytes 524288 | tf_op jit(solution)/shard_map/all_to_all | solution.py:27
  51.4 0.0 copy-done.1
  51.4 0.4 fusion.14
  51.8 20.7 %all_to_all.42 = bf16[8,16,896]{2,1,0:T(8,128)(2,1)S(1)} all-to-all(bf16[8,16,896]{2,1,0:T(8,128)(2,1)S(1)} %bitcast.64), channel_id=1, replica_groups={{32,40,48,56,0,8,16,24},{33,41,49,57,1,9,17,25},{34,42,50,58,2,10,18,26..., dimensions={0} | all-to-all | bytes 458752 | tf_op jit(solution)/shard_map/all_to_all | solution.py:21
  72.5 0.0 copy-done.3
  72.5 0.0 copy-done.4
  72.6 0.2 fusion.20
  72.8 3.2 %collective-permute-start = (bf16[16,896]{1,0:T(8,128)(2,1)S(1)}, bf16[16,896]{1,0:T(8,128)(2,1)S(1)}, u32[]{:S(2)}, u32[]{:S(2)}) collective-permute-start(bf16[16,896]{1,0:T(8,128)(2,1)S(1)} %get-tuple-element.20), channel_id=1, source_target_pairs={{0,64},{64,128},{128,192},{192,256},{256,320},{320,384},{384,448},... | collective-permute-start | bytes 86024 | tf_op jit(solution)/shard_map/ppermute | solution.py:32
  76.0 0.0 collective-permute-start.1
  76.0 1.0 collective-permute-done
  77.0 2.3 %collective-permute-done.1 = bf16[16,896]{1,0:T(8,128)(2,1)S(1)} collective-permute-done((bf16[16,896]{1,0:T(8,128)(2,1)S(1)}, bf16[16,896]{1,0:T(8,128)(2,1)S(1)}, u32[]{:S(2)}, u32[]{:S(2)}) %collective-permute-start.1) | collective-permute-done | bytes 28704 | tf_op jit(solution)/shard_map/ppermute | solution.py:32
  79.3 0.0 copy-done.5
  79.3 0.2 convolution_convert_fusion
  79.5 23.4 %all_to_all.43 = bf16[8,16,896]{2,1,0:T(8,128)(2,1)S(1)} all-to-all(bf16[8,16,896]{2,1,0:T(8,128)(2,1)S(1)} %bitcast.66), channel_id=1, replica_groups={{32,40,48,56,0,8,16,24},{33,41,49,57,1,9,17,25},{34,42,50,58,2,10,18,26..., dimensions={0} | all-to-all | bytes 458752 | tf_op jit(solution)/shard_map/all_to_all | solution.py:21
  102.9 0.1 fusion.23
  103.0 0.1 reduce_sum.44
  103.1 0.5 fusion.11
  103.6 0.0 copy-start.2
  103.6 0.1 select_convert_fusion
  103.7 10.2 %all_to_all.44 = bf16[8,16,1152]{2,1,0:T(8,128)(2,1)S(1)} all-to-all(bf16[8,16,1152]{2,1,0:T(8,128)(2,1)S(1)} %bitcast.59), channel_id=1, replica_groups={{3,4,5,6,7,0,1,2},{11,12,13,14,15,8,9,10},{19,20,21,22,23,16,17,18},{27..., dimensions={0} | all-to-all | bytes 589824 | tf_op jit(solution)/shard_map/all_to_all | solution.py:27
  114.0 0.2 fusion.36
  114.2 0.1 multiply_convert_fusion
  114.4 8.4 %all_to_all.45 = bf16[8,16,1024]{2,1,0:T(8,128)(2,1)S(1)} all-to-all(bf16[8,16,1024]{2,1,0:T(8,128)(2,1)S(1)} %broadcast_in_dim.61), channel_id=1, replica_groups={{3,4,5,6,7,0,1,2},{11,12,13,14,15,8,9,10},{19,20,21,22,23,16,17,18},{27..., dimensions={0} | all-to-all | bytes 524288 | tf_op jit(solution)/shard_map/all_to_all | solution.py:27
  122.7 0.0 copy-done.2
  122.7 0.4 fusion.17
  123.2 20.0 %all_to_all.46 = bf16[8,16,896]{2,1,0:T(8,128)(2,1)S(1)} all-to-all(bf16[8,16,896]{2,1,0:T(8,128)(2,1)S(1)} %bitcast.65), channel_id=1, replica_groups={{32,40,48,56,0,8,16,24},{33,41,49,57,1,9,17,25},{34,42,50,58,2,10,18,26..., dimensions={0} | all-to-all | bytes 458752 | tf_op jit(solution)/shard_map/all_to_all | solution.py:21
  143.2 0.2 add_convert_fusion
  143.5 2.9 %collective-permute-start.2 = (bf16[16,896]{1,0:T(8,128)(2,1)S(1)}, bf16[16,896]{1,0:T(8,128)(2,1)S(1)}, u32[]{:S(2)}, u32[]{:S(2)}) collective-permute-start(bf16[16,896]{1,0:T(8,128)(2,1)S(1)} %get-tuple-element.17), channel_id=1, source_target_pairs={{0,64},{64,128},{128,192},{192,256},{256,320},{320,384},{384,448},... | collective-permute-start | bytes 86024 | tf_op jit(solution)/shard_map/ppermute | solution.py:32
  146.3 0.0 collective-permute-start.3
  146.3 1.0 collective-permute-done.2
  147.3 2.3 %collective-permute-done.3 = bf16[16,896]{1,0:T(8,128)(2,1)S(1)} collective-permute-done((bf16[16,896]{1,0:T(8,128)(2,1)S(1)}, bf16[16,896]{1,0:T(8,128)(2,1)S(1)}, u32[]{:S(2)}, u32[]{:S(2)}) %collective-permute-start.3) | collective-permute-done | bytes 28704 | tf_op jit(solution)/shard_map/ppermute | solution.py:32
  149.6 0.6 pad_maximum_fusion.2
  (14 shorter events, 0.2 us)
Async XLA Ops:
  0.0 32.1 %copy-start = (bf16[1,1,896,1024]{3,2,1,0:T(8,128)(2,1)S(1)}, bf16[1,1,896,1024]{3,2,1,0:T(8,128)(2,1)}, u32[]{:S(2)}) copy-start(bf16[1,1,896,1024]{3,2,1,0:T(8,128)(2,1)} %param.7) | copy-start | bytes 5505028
  2.1 29.7 %all-to-all-start = ((bf16[8,16,896]{2,1,0:T(8,128)(2,1)}), bf16[8,16,896]{2,1,0:T(8,128)(2,1)S(1)}, u32[]{:S(2)}, u32[]{:S(2)}) async-start(bf16[8,16,896]{2,1,0:T(8,128)(2,1)} %bitcast.69), calls=%async_computation | async-start | bytes 458752 | tf_op jit(solution)/shard_map/all_to_all | solution.py:21
  32.5 18.8 %copy-start.1 = (bf16[1,1,1024,896]{3,2,1,0:T(8,128)(2,1)S(1)}, bf16[1,1,1024,896]{3,2,1,0:T(8,128)(2,1)}, u32[]{:S(2)}) copy-start(bf16[1,1,1024,896]{3,2,1,0:T(8,128)(2,1)} %param.8) | copy-start | bytes 5505028
  42.8 29.7 %copy-start.3 = (bf16[1,2,1,16,896]{4,3,2,1,0:T(8,128)(2,1)S(1)}, bf16[1,2,1,16,896]{4,3,2,1,0:T(8,128)(2,1)}, u32[]{:S(2)}) copy-start(bf16[1,2,1,16,896]{4,3,2,1,0:T(8,128)(2,1)} %param.6) | copy-start | bytes 172036
  42.8 29.7 %copy-start.4 = (f32[2,32,128]{2,1,0:T(8,128)S(1)}, f32[2,32,128]{2,1,0:T(8,128)}, u32[]{:S(2)}) copy-start(f32[2,32,128]{2,1,0:T(8,128)} %get-tuple-element.9) | copy-start | bytes 98308
  43.0 36.3 %copy-start.5 = (bf16[1,128,32]{2,1,0:T(8,128)(2,1)S(1)}, bf16[1,128,32]{2,1,0:T(8,128)(2,1)}, u32[]{:S(2)}) copy-start(bf16[1,128,32]{2,1,0:T(8,128)(2,1)} %get-tuple-element.12) | copy-start | bytes 24580
  72.8 4.1 %collective-permute-start = (bf16[16,896]{1,0:T(8,128)(2,1)S(1)}, bf16[16,896]{1,0:T(8,128)(2,1)S(1)}, u32[]{:S(2)}, u32[]{:S(2)}) collective-permute-start(bf16[16,896]{1,0:T(8,128)(2,1)S(1)} %get-tuple-element.20), channel_id=1, source_target_pairs={{0,64},{64,128},{128,192},{192,256},{256,320},{320,384},{384,448},... | collective-permute-start | bytes 86024 | tf_op jit(solution)/shard_map/ppermute | solution.py:32
  76.0 3.3 %collective-permute-start.1 = (bf16[16,896]{1,0:T(8,128)(2,1)S(1)}, bf16[16,896]{1,0:T(8,128)(2,1)S(1)}, u32[]{:S(2)}, u32[]{:S(2)}) collective-permute-start(bf16[16,896]{1,0:T(8,128)(2,1)S(1)} %get-tuple-element.19), channel_id=1, source_target_pairs={{0,448},{64,0},{128,64},{192,128},{256,192},{320,256},{384,320},{4... | collective-permute-start | bytes 86024 | tf_op jit(solution)/shard_map/ppermute | solution.py:32
  103.6 19.1 %copy-start.2 = (bf16[1,1,1024,896]{3,2,1,0:T(8,128)(2,1)S(1)}, bf16[1,1,1024,896]{3,2,1,0:T(8,128)(2,1)}, u32[]{:S(2)}) copy-start(bf16[1,1,1024,896]{3,2,1,0:T(8,128)(2,1)} %param.8) | copy-start | bytes 5505028
  143.5 3.8 %collective-permute-start.2 = (bf16[16,896]{1,0:T(8,128)(2,1)S(1)}, bf16[16,896]{1,0:T(8,128)(2,1)S(1)}, u32[]{:S(2)}, u32[]{:S(2)}) collective-permute-start(bf16[16,896]{1,0:T(8,128)(2,1)S(1)} %get-tuple-element.17), channel_id=1, source_target_pairs={{0,64},{64,128},{128,192},{192,256},{256,320},{320,384},{384,448},... | collective-permute-start | bytes 86024 | tf_op jit(solution)/shard_map/ppermute | solution.py:32
  146.3 3.3 %collective-permute-start.3 = (bf16[16,896]{1,0:T(8,128)(2,1)S(1)}, bf16[16,896]{1,0:T(8,128)(2,1)S(1)}, u32[]{:S(2)}, u32[]{:S(2)}) collective-permute-start(bf16[16,896]{1,0:T(8,128)(2,1)S(1)} %get-tuple-element.18), channel_id=1, source_target_pairs={{0,448},{64,0},{128,64},{192,128},{256,192},{320,256},{384,320},{4... | collective-permute-start | bytes 86024 | tf_op jit(solution)/shard_map/ppermute | solution.py:32

commit v6 on v5

--- a/solution.py
+++ b/solution.py
@@ -132,6 +132,7 @@
         norm_gain,
     )
     lane = jnp.arange(LANES)
+    half = LANES // 2
     for step in range(steps):
         if step > 0:
             outgoing = jnp.dot(
@@ -143,12 +144,14 @@
         scaled = (rows_f * gain).astype(jnp.bfloat16)
         partial = jnp.dot(scaled, up, preferred_element_type=jnp.float32).astype(jnp.bfloat16)
         high = lax.reduce_precision(squares, 8, 7)
-        tail = jnp.where(lane == 0, high, jnp.where(lane == 1, squares - high, 0.0))
+        tail = jnp.where(lane < half, high, squares - high)
         sent = jnp.concatenate([partial, tail.astype(jnp.bfloat16)], axis=1)
         parts = over_slices(sent.reshape(SLICES, slots, hidden_width + LANES)).astype(jnp.float32)
         total = jnp.sum(parts, axis=0)
-        summed = total[:, hidden_width : hidden_width + 1] + total[:, hidden_width + 1 : hidden_width + 2]
-        value = total[:, :hidden_width] * lax.rsqrt(summed / features + 1e-06)
+        tails = total[:, hidden_width:]
+        summed = tails + jnp.concatenate([tails[:, half:], tails[:, :half]], axis=1)
+        scale = lax.rsqrt(summed / features + 1e-06)
+        value = total[:, :hidden_width] * jnp.tile(scale, (1, hidden_width // LANES))
         active = jax.nn.silu(value).astype(jnp.bfloat16)
         hidden = over_slices(jnp.broadcast_to(active, (SLICES, slots, hidden_width)))
         produced = jnp.dot(

time: 151 us -> 151 us (level)
  no operation moved by 1% of the time
where the time goes in v6:
time: 151 us; the launch traced here: 150 us
  blocking collectives  101 us (67%)
  starting transfers between devices  24.7 us (16%)
  waiting for transfers between devices  16.9 us (11%)
  matrix products  2.46 us (2%)
  other arithmetic  2.17 us (1%)
  Pallas kernels  2.12 us (1%)
    all_to_all x3, blocking collectives, over_groups(): lax.all_to_all(value, 'expert', 0, 0, axis_index_groups=members, tiled=True)  64.1 us
    all_to_all x4, blocking collectives, over_slices(): lax.all_to_all(value, 'expert', 0, 0, axis_index_groups=members, tiled=True)  36.9 us
    all_to_all x1, starting transfers between devices, over_groups(): lax.all_to_all(value, 'expert', 0, 0, axis_index_groups=members, tiled=True)  18.7 us
    all_to_all x1, waiting for transfers between devices, over_groups(): lax.all_to_all(value, 'expert', 0, 0, axis_index_groups=members, tiled=True)  10.3 us
    ppermute x4, waiting for transfers between devices, shifted(): lax.ppermute(value, 'pipe', [(i, (i + steps) % count) for i in range(coun...  6.58 us
    ppermute x4, starting transfers between devices, shifted(): lax.ppermute(value, 'pipe', [(i, (i + steps) % count) for i in range(coun...  6.02 us
  transfers between devices with their start and end apart: 5, of which 5 were waited for; matrix products, arithmetic and copies ran while one was open for 0% of the time, Pallas kernels for 0%

profile of v6, /device:TPU:1, one launch (start us, length us, event | category | flops | bytes accessed | tf_op | source)
XLA Modules:
  0.0 150.1 jit_solution(4567567942976418808)
XLA Ops:
  0.0 0.0 copy-start
  0.0 2.1 %prepare.1 = (bf16[128,896]{1,0:T(8,128)(2,1)}, bf16[1,128,32]{2,1,0:T(8,128)(2,1)}, f32[2,32,128]{2,1,0:T(8,128)}, f32[1,896]{1,0:T(1,128)}) custom-call(bf16[32,896]{1,0:T(8,128)(2,1)} %bitcast.82, s32[2,2,2,128]{3,2,1,0:T(2,128)} %bitcast.84, f32[2,2,2,128]{3,2,1,0:T(2,128)} %bitcast.85, f32[1,7168]{1,0:T(1,128)} %gain_hbm.1), custom_call_target="tpu_custom_call" | custom-call | tf_op jit(solution)/shard_map/prepare/pallas_call | solution.py:111
  2.1 18.7 %all-to-all-start = ((bf16[8,16,896]{2,1,0:T(8,128)(2,1)}), bf16[8,16,896]{2,1,0:T(8,128)(2,1)S(1)}, u32[]{:S(2)}, u32[]{:S(2)}) async-start(bf16[8,16,896]{2,1,0:T(8,128)(2,1)} %bitcast.81), calls=%async_computation | async-start | bytes 458752 | tf_op jit(solution)/shard_map/all_to_all | solution.py:21
  20.8 0.7 reduce.2
  21.5 10.3 %all-to-all-done = bf16[8,16,896]{2,1,0:T(8,128)(2,1)S(1)} async-done(((bf16[8,16,896]{2,1,0:T(8,128)(2,1)}), bf16[8,16,896]{2,1,0:T(8,128)(2,1)S(1)}, u32[]{:S(2)}, u32[]{:S(2)}) %all-to-all-start) | async-done | bytes 229408 | tf_op jit(solution)/shard_map/all_to_all | solution.py:21
  31.8 0.1 fusion.21
  32.0 0.1 reduce_sum.41
  32.1 0.0 copy-done
  32.1 0.4 fusion.8
  32.5 0.0 copy-start.1
  32.6 0.1 select_convert_fusion.1
  32.7 9.9 %all_to_all.40 = bf16[8,16,1152]{2,1,0:T(8,128)(2,1)S(1)} all-to-all(bf16[8,16,1152]{2,1,0:T(8,128)(2,1)S(1)} %bitcast.68), channel_id=1, replica_groups={{3,4,5,6,7,0,1,2},{11,12,13,14,15,8,9,10},{19,20,21,22,23,16,17,18},{27..., dimensions={0} | all-to-all | bytes 589824 | tf_op jit(solution)/shard_map/all_to_all | solution.py:27
  42.6 0.1 fusion.40
  42.7 0.1 fusion.38
  42.8 0.0 copy-start.3
  42.9 0.0 copy-start.4
  42.9 0.0 copy-start.5
  42.9 8.4 %all_to_all.41 = bf16[8,16,1024]{2,1,0:T(8,128)(2,1)S(1)} all-to-all(bf16[8,16,1024]{2,1,0:T(8,128)(2,1)S(1)} %broadcast_in_dim.44), channel_id=1, replica_groups={{3,4,5,6,7,0,1,2},{11,12,13,14,15,8,9,10},{19,20,21,22,23,16,17,18},{27..., dimensions={0} | all-to-all | bytes 524288 | tf_op jit(solution)/shard_map/all_to_all | solution.py:27
  51.3 0.0 copy-done.1
  51.3 0.5 fusion.14
  51.8 20.7 %all_to_all.42 = bf16[8,16,896]{2,1,0:T(8,128)(2,1)S(1)} all-to-all(bf16[8,16,896]{2,1,0:T(8,128)(2,1)S(1)} %bitcast.74), channel_id=1, replica_groups={{32,40,48,56,0,8,16,24},{33,41,49,57,1,9,17,25},{34,42,50,58,2,10,18,26..., dimensions={0} | all-to-all | bytes 458752 | tf_op jit(solution)/shard_map/all_to_all | solution.py:21
  72.5 0.0 copy-done.3
  72.5 0.0 copy-done.4
  72.5 0.2 fusion.20
  72.7 3.2 %collective-permute-start = (bf16[16,896]{1,0:T(8,128)(2,1)S(1)}, bf16[16,896]{1,0:T(8,128)(2,1)S(1)}, u32[]{:S(2)}, u32[]{:S(2)}) collective-permute-start(bf16[16,896]{1,0:T(8,128)(2,1)S(1)} %get-tuple-element.24), channel_id=1, source_target_pairs={{0,64},{64,128},{128,192},{192,256},{256,320},{320,384},{384,448},... | collective-permute-start | bytes 86024 | tf_op jit(solution)/shard_map/ppermute | solution.py:32
  75.9 0.0 collective-permute-start.1
  75.9 1.0 collective-permute-done
  76.9 2.3 %collective-permute-done.1 = bf16[16,896]{1,0:T(8,128)(2,1)S(1)} collective-permute-done((bf16[16,896]{1,0:T(8,128)(2,1)S(1)}, bf16[16,896]{1,0:T(8,128)(2,1)S(1)}, u32[]{:S(2)}, u32[]{:S(2)}) %collective-permute-start.1) | collective-permute-done | bytes 28704 | tf_op jit(solution)/shard_map/ppermute | solution.py:32
  79.2 0.0 copy-done.5
  79.2 0.2 convolution_convert_fusion
  79.4 23.4 %all_to_all.43 = bf16[8,16,896]{2,1,0:T(8,128)(2,1)S(1)} all-to-all(bf16[8,16,896]{2,1,0:T(8,128)(2,1)S(1)} %bitcast.76), channel_id=1, replica_groups={{32,40,48,56,0,8,16,24},{33,41,49,57,1,9,17,25},{34,42,50,58,2,10,18,26..., dimensions={0} | all-to-all | bytes 458752 | tf_op jit(solution)/shard_map/all_to_all | solution.py:21
  102.8 0.1 fusion.23
  102.9 0.1 reduce_sum.44
  103.0 0.5 fusion.11
  103.5 0.0 copy-start.2
  103.5 0.1 select_convert_fusion
  103.6 10.3 %all_to_all.44 = bf16[8,16,1152]{2,1,0:T(8,128)(2,1)S(1)} all-to-all(bf16[8,16,1152]{2,1,0:T(8,128)(2,1)S(1)} %bitcast.69), channel_id=1, replica_groups={{3,4,5,6,7,0,1,2},{11,12,13,14,15,8,9,10},{19,20,21,22,23,16,17,18},{27..., dimensions={0} | all-to-all | bytes 589824 | tf_op jit(solution)/shard_map/all_to_all | solution.py:27
  113.9 0.1 fusion.39
  114.0 0.1 fusion.35
  114.2 8.4 %all_to_all.45 = bf16[8,16,1024]{2,1,0:T(8,128)(2,1)S(1)} all-to-all(bf16[8,16,1024]{2,1,0:T(8,128)(2,1)S(1)} %broadcast_in_dim.47), channel_id=1, replica_groups={{3,4,5,6,7,0,1,2},{11,12,13,14,15,8,9,10},{19,20,21,22,23,16,17,18},{27..., dimensions={0} | all-to-all | bytes 524288 | tf_op jit(solution)/shard_map/all_to_all | solution.py:27
  122.6 0.5 fusion.17
  123.0 20.0 %all_to_all.46 = bf16[8,16,896]{2,1,0:T(8,128)(2,1)S(1)} all-to-all(bf16[8,16,896]{2,1,0:T(8,128)(2,1)S(1)} %bitcast.75), channel_id=1, replica_groups={{32,40,48,56,0,8,16,24},{33,41,49,57,1,9,17,25},{34,42,50,58,2,10,18,26..., dimensions={0} | all-to-all | bytes 458752 | tf_op jit(solution)/shard_map/all_to_all | solution.py:21
  143.1 0.2 add_convert_fusion
  143.3 2.8 %collective-permute-start.2 = (bf16[16,896]{1,0:T(8,128)(2,1)S(1)}, bf16[16,896]{1,0:T(8,128)(2,1)S(1)}, u32[]{:S(2)}, u32[]{:S(2)}) collective-permute-start(bf16[16,896]{1,0:T(8,128)(2,1)S(1)} %get-tuple-element.21), channel_id=1, source_target_pairs={{0,64},{64,128},{128,192},{192,256},{256,320},{320,384},{384,448},... | collective-permute-start | bytes 86024 | tf_op jit(solution)/shard_map/ppermute | solution.py:32
  146.2 0.0 collective-permute-start.3
  146.2 1.0 collective-permute-done.2
  147.1 2.3 %collective-permute-done.3 = bf16[16,896]{1,0:T(8,128)(2,1)S(1)} collective-permute-done((bf16[16,896]{1,0:T(8,128)(2,1)S(1)}, bf16[16,896]{1,0:T(8,128)(2,1)S(1)}, u32[]{:S(2)}, u32[]{:S(2)}) %collective-permute-start.3) | collective-permute-done | bytes 28704 | tf_op jit(solution)/shard_map/ppermute | solution.py:32
  149.4 0.6 pad_maximum_fusion.2
  (18 shorter events, 0.3 us)
Async XLA Ops:
  0.0 32.1 %copy-start = (bf16[1,1,896,1024]{3,2,1,0:T(8,128)(2,1)S(1)}, bf16[1,1,896,1024]{3,2,1,0:T(8,128)(2,1)}, u32[]{:S(2)}) copy-start(bf16[1,1,896,1024]{3,2,1,0:T(8,128)(2,1)} %param.7) | copy-start | bytes 5505028
  2.1 29.7 %all-to-all-start = ((bf16[8,16,896]{2,1,0:T(8,128)(2,1)}), bf16[8,16,896]{2,1,0:T(8,128)(2,1)S(1)}, u32[]{:S(2)}, u32[]{:S(2)}) async-start(bf16[8,16,896]{2,1,0:T(8,128)(2,1)} %bitcast.81), calls=%async_computation | async-start | bytes 458752 | tf_op jit(solution)/shard_map/all_to_all | solution.py:21
  32.5 18.7 %copy-start.1 = (bf16[1,1,1024,896]{3,2,1,0:T(8,128)(2,1)S(1)}, bf16[1,1,1024,896]{3,2,1,0:T(8,128)(2,1)}, u32[]{:S(2)}) copy-start(bf16[1,1,1024,896]{3,2,1,0:T(8,128)(2,1)} %param.8) | copy-start | bytes 5505028
  42.8 29.6 %copy-start.3 = (bf16[1,2,1,16,896]{4,3,2,1,0:T(8,128)(2,1)S(1)}, bf16[1,2,1,16,896]{4,3,2,1,0:T(8,128)(2,1)}, u32[]{:S(2)}) copy-start(bf16[1,2,1,16,896]{4,3,2,1,0:T(8,128)(2,1)} %param.6) | copy-start | bytes 172036
  42.9 29.6 %copy-start.4 = (f32[2,32,128]{2,1,0:T(8,128)S(1)}, f32[2,32,128]{2,1,0:T(8,128)}, u32[]{:S(2)}) copy-start(f32[2,32,128]{2,1,0:T(8,128)} %get-tuple-element.9) | copy-start | bytes 98308
  42.9 36.3 %copy-start.5 = (bf16[1,128,32]{2,1,0:T(8,128)(2,1)S(1)}, bf16[1,128,32]{2,1,0:T(8,128)(2,1)}, u32[]{:S(2)}) copy-start(bf16[1,128,32]{2,1,0:T(8,128)(2,1)} %get-tuple-element.12) | copy-start | bytes 24580
  72.7 4.2 %collective-permute-start = (bf16[16,896]{1,0:T(8,128)(2,1)S(1)}, bf16[16,896]{1,0:T(8,128)(2,1)S(1)}, u32[]{:S(2)}, u32[]{:S(2)}) collective-permute-start(bf16[16,896]{1,0:T(8,128)(2,1)S(1)} %get-tuple-element.24), channel_id=1, source_target_pairs={{0,64},{64,128},{128,192},{192,256},{256,320},{320,384},{384,448},... | collective-permute-start | bytes 86024 | tf_op jit(solution)/shard_map/ppermute | solution.py:32
  75.9 3.3 %collective-permute-start.1 = (bf16[16,896]{1,0:T(8,128)(2,1)S(1)}, bf16[16,896]{1,0:T(8,128)(2,1)S(1)}, u32[]{:S(2)}, u32[]{:S(2)}) collective-permute-start(bf16[16,896]{1,0:T(8,128)(2,1)S(1)} %get-tuple-element.23), channel_id=1, source_target_pairs={{0,448},{64,0},{128,64},{192,128},{256,192},{320,256},{384,320},{4... | collective-permute-start | bytes 86024 | tf_op jit(solution)/shard_map/ppermute | solution.py:32
  103.5 19.1 %copy-start.2 = (bf16[1,1,1024,896]{3,2,1,0:T(8,128)(2,1)S(1)}, bf16[1,1,1024,896]{3,2,1,0:T(8,128)(2,1)}, u32[]{:S(2)}) copy-start(bf16[1,1,1024,896]{3,2,1,0:T(8,128)(2,1)} %param.8) | copy-start | bytes 5505028
  143.3 3.8 %collective-permute-start.2 = (bf16[16,896]{1,0:T(8,128)(2,1)S(1)}, bf16[16,896]{1,0:T(8,128)(2,1)S(1)}, u32[]{:S(2)}, u32[]{:S(2)}) collective-permute-start(bf16[16,896]{1,0:T(8,128)(2,1)S(1)} %get-tuple-element.21), channel_id=1, source_target_pairs={{0,64},{64,128},{128,192},{192,256},{256,320},{320,384},{384,448},... | collective-permute-start | bytes 86024 | tf_op jit(solution)/shard_map/ppermute | solution.py:32
  146.2 3.3 %collective-permute-start.3 = (bf16[16,896]{1,0:T(8,128)(2,1)S(1)}, bf16[16,896]{1,0:T(8,128)(2,1)S(1)}, u32[]{:S(2)}, u32[]{:S(2)}) collective-permute-start(bf16[16,896]{1,0:T(8,128)(2,1)S(1)} %get-tuple-element.22), channel_id=1, source_target_pairs={{0,448},{64,0},{128,64},{192,128},{256,192},{320,256},{384,320},{4... | collective-permute-start | bytes 86024 | tf_op jit(solution)/shard_map/ppermute | solution.py:32

commit v7 on v6

--- a/solution.py
+++ b/solution.py
@@ -9,14 +9,14 @@
 SLICES = 8
 CAP = 8
 LANES = 128
-FIRST = 4
+FIRST = 6
 FIRST_SLICE = 3
 VMEM = pl.BlockSpec(memory_space=pltpu.VMEM)
 HBM = pl.BlockSpec(memory_space=pltpu.HBM)
 
 
-def over_groups(value):
-    order = [(i + FIRST) % GROUPS for i in range(GROUPS)]
+def over_groups(value, first):
+    order = [(i + first) % GROUPS for i in range(GROUPS)]
     members = [[g * SLICES + s for g in order] for s in range(SLICES)]
     return lax.all_to_all(value, "expert", 0, 0, axis_index_groups=members, tiled=True)
 
@@ -69,7 +69,6 @@
 
     row = lax.broadcasted_iota(jnp.int32, (slots, every), 0)
     lane = lax.broadcasted_iota(jnp.int32, (slots, every), 1)
-    expert = (row // (streams * CAP) + FIRST) % GROUPS
     stream, slot = row // CAP % streams, row % CAP
     mine = lane // tokens == stream
     earlier_row = lax.broadcasted_iota(jnp.int32, (every, every), 0)
@@ -79,6 +78,7 @@
     for copy in copies:
         copy.wait()
     for step in range(steps):
+        expert = (row // (streams * CAP) + (FIRST - step) % GROUPS) % GROUPS
         named = [mine & (own(routes_ref, step, k) == expert) for k in range(topk)]
         hit = named[0]
         for k in range(1, topk):
@@ -89,7 +89,7 @@
         weight = jnp.zeros((slots, every), jnp.float32)
         for k in range(topk):
             weight = jnp.where(named[k], own(weights_ref, step, k), weight)
-        mix = jnp.transpose(placed * weight)
+        mix = jnp.transpose(pltpu.roll(placed * weight, streams * CAP, 0))
         mix_ref[step] = mix[: streams * tokens]
         narrow = placed[:, : streams * tokens].astype(jnp.bfloat16)
         if step == 0:
@@ -134,11 +134,12 @@
     lane = jnp.arange(LANES)
     half = LANES // 2
     for step in range(steps):
+        first = (FIRST - step) % GROUPS
         if step > 0:
             outgoing = jnp.dot(
                 place[step - 1], current, preferred_element_type=jnp.float32
             ).astype(jnp.bfloat16)
-        rows = over_groups(outgoing.reshape(GROUPS, slots, width)).reshape(GROUPS * slots, width)
+        rows = over_groups(outgoing.reshape(GROUPS, slots, width), first).reshape(GROUPS * slots, width)
         rows_f = rows.astype(jnp.float32)
         squares = jnp.sum(rows_f * rows_f, axis=1, keepdims=True)
         scaled = (rows_f * gain).astype(jnp.bfloat16)
@@ -146,6 +147,7 @@
         high = lax.reduce_precision(squares, 8, 7)
         tail = jnp.where(lane < half, high, squares - high)
         sent = jnp.concatenate([partial, tail.astype(jnp.bfloat16)], axis=1)
+        sent = jnp.concatenate([sent[-slots:], sent[:-slots]], axis=0)
         parts = over_slices(sent.reshape(SLICES, slots, hidden_width + LANES)).astype(jnp.float32)
         total = jnp.sum(parts, axis=0)
         tails = total[:, hidden_width:]
@@ -157,7 +159,7 @@
         produced = jnp.dot(
             hidden.reshape(GROUPS * slots, hidden_width), down, preferred_element_type=jnp.float32
         ).astype(jnp.bfloat16)
-        returned = over_groups(produced.reshape(GROUPS, slots, width)).reshape(GROUPS * slots, width)
+        returned = over_groups(produced.reshape(GROUPS, slots, width), first - 1).reshape(GROUPS * slots, width)
         added = jnp.dot(
             mix[step],
             returned.astype(jnp.float32),

time: 151 us -> 150 us (level)
  blocking collectives: 101 us -> 96 us
  waiting for transfers between devices: 16.9 us -> 19.1 us
  starting transfers between devices: 24.7 us -> 26.9 us
    ppermute x4, starting transfers between devices: 6.02 us -> 10.9 us  [shifted(): lax.ppermute(value, 'pipe', [(i, (i + steps) % count) for i in range(coun...]
    all_to_all x3, blocking collectives: 64.1 us -> 61.2 us  [over_groups(): lax.all_to_all(value, 'expert', 0, 0, axis_index_groups=members, tiled=True)]
    all_to_all x1, starting transfers between devices: 18.7 us -> 15.9 us  [over_groups(): lax.all_to_all(value, 'expert', 0, 0, axis_index_groups=members, tiled=True)]
    all_to_all x1, waiting for transfers between devices: 10.3 us -> 12.6 us  [over_groups(): lax.all_to_all(value, 'expert', 0, 0, axis_index_groups=members, tiled=True)]
    all_to_all x4, blocking collectives: 36.9 us -> 34.8 us  [over_slices(): lax.all_to_all(value, 'expert', 0, 0, axis_index_groups=members, tiled=True)]
where the time goes in v7:
time: 150 us; the launch traced here: 149 us
  blocking collectives  96 us (64%)
  starting transfers between devices  26.9 us (18%)
  waiting for transfers between devices  19.1 us (13%)
  matrix products  2.46 us (2%)
  other arithmetic  2.18 us (1%)
  Pallas kernels  2.14 us (1%)
    all_to_all x3, blocking collectives, over_groups(): lax.all_to_all(value, 'expert', 0, 0, axis_index_groups=members, tiled=True)  61.2 us
    all_to_all x4, blocking collectives, over_slices(): lax.all_to_all(value, 'expert', 0, 0, axis_index_groups=members, tiled=True)  34.8 us
    all_to_all x1, starting transfers between devices, over_groups(): lax.all_to_all(value, 'expert', 0, 0, axis_index_groups=members, tiled=True)  15.9 us
    all_to_all x1, waiting for transfers between devices, over_groups(): lax.all_to_all(value, 'expert', 0, 0, axis_index_groups=members, tiled=True)  12.6 us
    ppermute x4, starting transfers between devices, shifted(): lax.ppermute(value, 'pipe', [(i, (i + steps) % count) for i in range(coun...  10.9 us
    ppermute x4, waiting for transfers between devices, shifted(): lax.ppermute(value, 'pipe', [(i, (i + steps) % count) for i in range(coun...  6.58 us
  transfers between devices with their start and end apart: 5, of which 5 were waited for; matrix products, arithmetic and copies ran while one was open for 0% of the time, Pallas kernels for 0%

profile of v7, /device:TPU:1, one launch (start us, length us, event | category | flops | bytes accessed | tf_op | source)
XLA Modules:
  0.0 149.4 jit_solution(7846104124793458788)
XLA Ops:
  0.0 0.0 copy-start
  0.0 2.1 %prepare.1 = (bf16[128,896]{1,0:T(8,128)(2,1)}, bf16[1,128,32]{2,1,0:T(8,128)(2,1)}, f32[2,32,128]{2,1,0:T(8,128)}, f32[1,896]{1,0:T(1,128)}) custom-call(bf16[32,896]{1,0:T(8,128)(2,1)} %bitcast.82, s32[2,2,2,128]{3,2,1,0:T(2,128)} %bitcast.84, f32[2,2,2,128]{3,2,1,0:T(2,128)} %bitcast.85, f32[1,7168]{1,0:T(1,128)} %gain_hbm.1), custom_call_target="tpu_custom_call" | custom-call | tf_op jit(solution)/shard_map/prepare/pallas_call | solution.py:111
  2.1 15.9 %all-to-all-start = ((bf16[8,16,896]{2,1,0:T(8,128)(2,1)}), bf16[8,16,896]{2,1,0:T(8,128)(2,1)S(1)}, u32[]{:S(2)}, u32[]{:S(2)}) async-start(bf16[8,16,896]{2,1,0:T(8,128)(2,1)} %bitcast.81), calls=%async_computation | async-start | bytes 458752 | tf_op jit(solution)/shard_map/all_to_all | solution.py:21
  18.1 0.7 reduce.2
  18.8 12.6 %all-to-all-done = bf16[8,16,896]{2,1,0:T(8,128)(2,1)S(1)} async-done(((bf16[8,16,896]{2,1,0:T(8,128)(2,1)}), bf16[8,16,896]{2,1,0:T(8,128)(2,1)S(1)}, u32[]{:S(2)}, u32[]{:S(2)}) %all-to-all-start) | async-done | bytes 229408 | tf_op jit(solution)/shard_map/all_to_all | solution.py:21
  31.3 0.1 fusion.21
  31.5 0.1 reduce_sum.41
  31.6 0.0 copy-done
  31.6 0.4 fusion.8
  32.0 0.0 copy-start.1
  32.1 0.1 select_convert_fusion.1
  32.2 9.7 %all_to_all.40 = bf16[8,16,1152]{2,1,0:T(8,128)(2,1)S(1)} all-to-all(bf16[8,16,1152]{2,1,0:T(8,128)(2,1)S(1)} %bitcast.68), channel_id=1, replica_groups={{3,4,5,6,7,0,1,2},{11,12,13,14,15,8,9,10},{19,20,21,22,23,16,17,18},{27..., dimensions={0} | all-to-all | bytes 589824 | tf_op jit(solution)/shard_map/all_to_all | solution.py:27
  41.9 0.1 fusion.42
  42.0 0.1 fusion.40
  42.2 0.0 copy-start.3
  42.2 0.0 copy-start.4
  42.2 0.0 copy-start.5
  42.2 8.1 %all_to_all.41 = bf16[8,16,1024]{2,1,0:T(8,128)(2,1)S(1)} all-to-all(bf16[8,16,1024]{2,1,0:T(8,128)(2,1)S(1)} %broadcast_in_dim.44), channel_id=1, replica_groups={{3,4,5,6,7,0,1,2},{11,12,13,14,15,8,9,10},{19,20,21,22,23,16,17,18},{27..., dimensions={0} | all-to-all | bytes 524288 | tf_op jit(solution)/shard_map/all_to_all | solution.py:27
  50.3 0.0 copy-done.1
  50.3 0.4 fusion.14
  50.8 19.1 %all_to_all.42 = bf16[8,16,896]{2,1,0:T(8,128)(2,1)S(1)} all-to-all(bf16[8,16,896]{2,1,0:T(8,128)(2,1)S(1)} %bitcast.74), channel_id=1, replica_groups={{40,48,56,0,8,16,24,32},{41,49,57,1,9,17,25,33},{42,50,58,2,10,18,26,34..., dimensions={0} | all-to-all | bytes 458752 | tf_op jit(solution)/shard_map/all_to_all | solution.py:21
  69.9 0.0 copy-done.3
  69.9 0.0 copy-done.4
  69.9 0.2 fusion.20
  70.1 6.8 %collective-permute-start = (bf16[16,896]{1,0:T(8,128)(2,1)S(1)}, bf16[16,896]{1,0:T(8,128)(2,1)S(1)}, u32[]{:S(2)}, u32[]{:S(2)}) collective-permute-start(bf16[16,896]{1,0:T(8,128)(2,1)S(1)} %get-tuple-element.24), channel_id=1, source_target_pairs={{0,64},{64,128},{128,192},{192,256},{256,320},{320,384},{384,448},... | collective-permute-start | bytes 86024 | tf_op jit(solution)/shard_map/ppermute | solution.py:32
  76.9 0.0 collective-permute-start.1
  76.9 1.0 collective-permute-done
  77.9 2.3 %collective-permute-done.1 = bf16[16,896]{1,0:T(8,128)(2,1)S(1)} collective-permute-done((bf16[16,896]{1,0:T(8,128)(2,1)S(1)}, bf16[16,896]{1,0:T(8,128)(2,1)S(1)}, u32[]{:S(2)}, u32[]{:S(2)}) %collective-permute-start.1) | collective-permute-done | bytes 28704 | tf_op jit(solution)/shard_map/ppermute | solution.py:32
  80.2 0.0 copy-done.5
  80.2 0.2 convolution_convert_fusion
  80.4 22.3 %all_to_all.43 = bf16[8,16,896]{2,1,0:T(8,128)(2,1)S(1)} all-to-all(bf16[8,16,896]{2,1,0:T(8,128)(2,1)S(1)} %bitcast.76), channel_id=1, replica_groups={{40,48,56,0,8,16,24,32},{41,49,57,1,9,17,25,33},{42,50,58,2,10,18,26,34..., dimensions={0} | all-to-all | bytes 458752 | tf_op jit(solution)/shard_map/all_to_all | solution.py:21
  102.7 0.1 fusion.23
  102.8 0.1 reduce_sum.44
  102.9 0.5 fusion.11
  103.4 0.0 copy-start.2
  103.4 0.1 select_convert_fusion
  103.6 8.6 %all_to_all.44 = bf16[8,16,1152]{2,1,0:T(8,128)(2,1)S(1)} all-to-all(bf16[8,16,1152]{2,1,0:T(8,128)(2,1)S(1)} %bitcast.69), channel_id=1, replica_groups={{3,4,5,6,7,0,1,2},{11,12,13,14,15,8,9,10},{19,20,21,22,23,16,17,18},{27..., dimensions={0} | all-to-all | bytes 589824 | tf_op jit(solution)/shard_map/all_to_all | solution.py:27
  112.2 0.1 fusion.41
  112.3 0.1 fusion.37
  112.5 8.4 %all_to_all.45 = bf16[8,16,1024]{2,1,0:T(8,128)(2,1)S(1)} all-to-all(bf16[8,16,1024]{2,1,0:T(8,128)(2,1)S(1)} %broadcast_in_dim.47), channel_id=1, replica_groups={{3,4,5,6,7,0,1,2},{11,12,13,14,15,8,9,10},{19,20,21,22,23,16,17,18},{27..., dimensions={0} | all-to-all | bytes 524288 | tf_op jit(solution)/shard_map/all_to_all | solution.py:27
  120.8 0.4 fusion.17
  121.3 19.8 %all_to_all.46 = bf16[8,16,896]{2,1,0:T(8,128)(2,1)S(1)} all-to-all(bf16[8,16,896]{2,1,0:T(8,128)(2,1)S(1)} %bitcast.75), channel_id=1, replica_groups={{32,40,48,56,0,8,16,24},{33,41,49,57,1,9,17,25},{34,42,50,58,2,10,18,26..., dimensions={0} | all-to-all | bytes 458752 | tf_op jit(solution)/shard_map/all_to_all | solution.py:21
  141.1 0.2 add_convert_fusion
  141.3 4.2 %collective-permute-start.2 = (bf16[16,896]{1,0:T(8,128)(2,1)S(1)}, bf16[16,896]{1,0:T(8,128)(2,1)S(1)}, u32[]{:S(2)}, u32[]{:S(2)}) collective-permute-start(bf16[16,896]{1,0:T(8,128)(2,1)S(1)} %get-tuple-element.21), channel_id=1, source_target_pairs={{0,64},{64,128},{128,192},{192,256},{256,320},{320,384},{384,448},... | collective-permute-start | bytes 86024 | tf_op jit(solution)/shard_map/ppermute | solution.py:32
  145.5 0.0 collective-permute-start.3
  145.5 1.0 collective-permute-done.2
  146.5 2.3 %collective-permute-done.3 = bf16[16,896]{1,0:T(8,128)(2,1)S(1)} collective-permute-done((bf16[16,896]{1,0:T(8,128)(2,1)S(1)}, bf16[16,896]{1,0:T(8,128)(2,1)S(1)}, u32[]{:S(2)}, u32[]{:S(2)}) %collective-permute-start.3) | collective-permute-done | bytes 28704 | tf_op jit(solution)/shard_map/ppermute | solution.py:32
  148.8 0.6 pad_maximum_fusion.4
  (18 shorter events, 0.3 us)
Async XLA Ops:
  0.0 31.6 %copy-start = (bf16[1,1,896,1024]{3,2,1,0:T(8,128)(2,1)S(1)}, bf16[1,1,896,1024]{3,2,1,0:T(8,128)(2,1)}, u32[]{:S(2)}) copy-start(bf16[1,1,896,1024]{3,2,1,0:T(8,128)(2,1)} %param.7) | copy-start | bytes 5505028
  2.1 29.2 %all-to-all-start = ((bf16[8,16,896]{2,1,0:T(8,128)(2,1)}), bf16[8,16,896]{2,1,0:T(8,128)(2,1)S(1)}, u32[]{:S(2)}, u32[]{:S(2)}) async-start(bf16[8,16,896]{2,1,0:T(8,128)(2,1)} %bitcast.81), calls=%async_computation | async-start | bytes 458752 | tf_op jit(solution)/shard_map/all_to_all | solution.py:21
  32.0 18.3 %copy-start.1 = (bf16[1,1,1024,896]{3,2,1,0:T(8,128)(2,1)S(1)}, bf16[1,1,1024,896]{3,2,1,0:T(8,128)(2,1)}, u32[]{:S(2)}) copy-start(bf16[1,1,1024,896]{3,2,1,0:T(8,128)(2,1)} %param.8) | copy-start | bytes 5505028
  42.2 27.7 %copy-start.3 = (bf16[1,2,1,16,896]{4,3,2,1,0:T(8,128)(2,1)S(1)}, bf16[1,2,1,16,896]{4,3,2,1,0:T(8,128)(2,1)}, u32[]{:S(2)}) copy-start(bf16[1,2,1,16,896]{4,3,2,1,0:T(8,128)(2,1)} %param.6) | copy-start | bytes 172036
  42.2 27.7 %copy-start.4 = (f32[2,32,128]{2,1,0:T(8,128)S(1)}, f32[2,32,128]{2,1,0:T(8,128)}, u32[]{:S(2)}) copy-start(f32[2,32,128]{2,1,0:T(8,128)} %get-tuple-element.9) | copy-start | bytes 98308
  42.2 38.0 %copy-start.5 = (bf16[1,128,32]{2,1,0:T(8,128)(2,1)S(1)}, bf16[1,128,32]{2,1,0:T(8,128)(2,1)}, u32[]{:S(2)}) copy-start(bf16[1,128,32]{2,1,0:T(8,128)(2,1)} %get-tuple-element.12) | copy-start | bytes 24580
  70.1 7.7 %collective-permute-start = (bf16[16,896]{1,0:T(8,128)(2,1)S(1)}, bf16[16,896]{1,0:T(8,128)(2,1)S(1)}, u32[]{:S(2)}, u32[]{:S(2)}) collective-permute-start(bf16[16,896]{1,0:T(8,128)(2,1)S(1)} %get-tuple-element.24), channel_id=1, source_target_pairs={{0,64},{64,128},{128,192},{192,256},{256,320},{320,384},{384,448},... | collective-permute-start | bytes 86024 | tf_op jit(solution)/shard_map/ppermute | solution.py:32
  76.9 3.3 %collective-permute-start.1 = (bf16[16,896]{1,0:T(8,128)(2,1)S(1)}, bf16[16,896]{1,0:T(8,128)(2,1)S(1)}, u32[]{:S(2)}, u32[]{:S(2)}) collective-permute-start(bf16[16,896]{1,0:T(8,128)(2,1)S(1)} %get-tuple-element.23), channel_id=1, source_target_pairs={{0,448},{64,0},{128,64},{192,128},{256,192},{320,256},{384,320},{4... | collective-permute-start | bytes 86024 | tf_op jit(solution)/shard_map/ppermute | solution.py:32
  103.4 17.4 %copy-start.2 = (bf16[1,1,1024,896]{3,2,1,0:T(8,128)(2,1)S(1)}, bf16[1,1,1024,896]{3,2,1,0:T(8,128)(2,1)}, u32[]{:S(2)}) copy-start(bf16[1,1,1024,896]{3,2,1,0:T(8,128)(2,1)} %param.8) | copy-start | bytes 5505028
  141.3 5.2 %collective-permute-start.2 = (bf16[16,896]{1,0:T(8,128)(2,1)S(1)}, bf16[16,896]{1,0:T(8,128)(2,1)S(1)}, u32[]{:S(2)}, u32[]{:S(2)}) collective-permute-start(bf16[16,896]{1,0:T(8,128)(2,1)S(1)} %get-tuple-element.21), channel_id=1, source_target_pairs={{0,64},{64,128},{128,192},{192,256},{256,320},{320,384},{384,448},... | collective-permute-start | bytes 86024 | tf_op jit(solution)/shard_map/ppermute | solution.py:32
  145.5 3.3 %collective-permute-start.3 = (bf16[16,896]{1,0:T(8,128)(2,1)S(1)}, bf16[16,896]{1,0:T(8,128)(2,1)S(1)}, u32[]{:S(2)}, u32[]{:S(2)}) collective-permute-start(bf16[16,896]{1,0:T(8,128)(2,1)S(1)} %get-tuple-element.22), channel_id=1, source_target_pairs={{0,448},{64,0},{128,64},{192,128},{256,192},{320,256},{384,320},{4... | collective-permute-start | bytes 86024 | tf_op jit(solution)/shard_map/ppermute | solution.py:32

commit v8 on v7

--- a/solution.py
+++ b/solution.py
@@ -9,7 +9,7 @@
 SLICES = 8
 CAP = 8
 LANES = 128
-FIRST = 6
+FIRST = 5
 FIRST_SLICE = 3
 VMEM = pl.BlockSpec(memory_space=pltpu.VMEM)
 HBM = pl.BlockSpec(memory_space=pltpu.HBM)
@@ -78,7 +78,7 @@
     for copy in copies:
         copy.wait()
     for step in range(steps):
-        expert = (row // (streams * CAP) + (FIRST - step) % GROUPS) % GROUPS
+        expert = (row // (streams * CAP) + FIRST) % GROUPS
         named = [mine & (own(routes_ref, step, k) == expert) for k in range(topk)]
         hit = named[0]
         for k in range(1, topk):
@@ -134,7 +134,7 @@
     lane = jnp.arange(LANES)
     half = LANES // 2
     for step in range(steps):
-        first = (FIRST - step) % GROUPS
+        first = FIRST
         if step > 0:
             outgoing = jnp.dot(
                 place[step - 1], current, preferred_element_type=jnp.float32

time: 150 us -> 150 us (level)
  waiting for transfers between devices: 19.1 us -> 14.1 us
  blocking collectives: 96 us -> 101 us
    all_to_all x4, blocking collectives: 34.8 us -> 42.9 us  [over_slices(): lax.all_to_all(value, 'expert', 0, 0, axis_index_groups=members, tiled=True)]
    all_to_all x1, waiting for transfers between devices: 12.6 us -> 7.48 us  [over_groups(): lax.all_to_all(value, 'expert', 0, 0, axis_index_groups=members, tiled=True)]
    all_to_all x3, blocking collectives: 61.2 us -> 57.8 us  [over_groups(): lax.all_to_all(value, 'expert', 0, 0, axis_index_groups=members, tiled=True)]
where the time goes in v8:
time: 150 us
  blocking collectives  101 us (67%)
  starting transfers between devices  27.5 us (18%)
  waiting for transfers between devices  14.1 us (9%)
  matrix products  2.46 us (2%)
  other arithmetic  2.18 us (1%)
  Pallas kernels  2.14 us (1%)
    all_to_all x3, blocking collectives, over_groups(): lax.all_to_all(value, 'expert', 0, 0, axis_index_groups=members, tiled=True)  57.8 us
    all_to_all x4, blocking collectives, over_slices(): lax.all_to_all(value, 'expert', 0, 0, axis_index_groups=members, tiled=True)  42.9 us
    all_to_all x1, starting transfers between devices, over_groups(): lax.all_to_all(value, 'expert', 0, 0, axis_index_groups=members, tiled=True)  16.9 us
    ppermute x4, starting transfers between devices, shifted(): lax.ppermute(value, 'pipe', [(i, (i + steps) % count) for i in range(coun...  10.6 us
    all_to_all x1, waiting for transfers between devices, over_groups(): lax.all_to_all(value, 'expert', 0, 0, axis_index_groups=members, tiled=True)  7.48 us
    ppermute x4, waiting for transfers between devices, shifted(): lax.ppermute(value, 'pipe', [(i, (i + steps) % count) for i in range(coun...  6.58 us
  transfers between devices with their start and end apart: 5, of which 5 were waited for; matrix products, arithmetic and copies ran while one was open for 0% of the time, Pallas kernels for 0%

profile of v8, /device:TPU:1, one launch (start us, length us, event | category | flops | bytes accessed | tf_op | source)
XLA Modules:
  0.0 149.7 jit_solution(4502401715742207144)
XLA Ops:
  0.0 0.0 copy-start
  0.0 2.1 %prepare.1 = (bf16[128,896]{1,0:T(8,128)(2,1)}, bf16[1,128,32]{2,1,0:T(8,128)(2,1)}, f32[2,32,128]{2,1,0:T(8,128)}, f32[1,896]{1,0:T(1,128)}) custom-call(bf16[32,896]{1,0:T(8,128)(2,1)} %bitcast.82, s32[2,2,2,128]{3,2,1,0:T(2,128)} %bitcast.84, f32[2,2,2,128]{3,2,1,0:T(2,128)} %bitcast.85, f32[1,7168]{1,0:T(1,128)} %gain_hbm.1), custom_call_target="tpu_custom_call" | custom-call | tf_op jit(solution)/shard_map/prepare/pallas_call | solution.py:111
  2.2 16.9 %all-to-all-start = ((bf16[8,16,896]{2,1,0:T(8,128)(2,1)}), bf16[8,16,896]{2,1,0:T(8,128)(2,1)S(1)}, u32[]{:S(2)}, u32[]{:S(2)}) async-start(bf16[8,16,896]{2,1,0:T(8,128)(2,1)} %bitcast.81), calls=%async_computation | async-start | bytes 458752 | tf_op jit(solution)/shard_map/all_to_all | solution.py:21
  19.0 0.7 reduce.2
  19.7 7.5 %all-to-all-done = bf16[8,16,896]{2,1,0:T(8,128)(2,1)S(1)} async-done(((bf16[8,16,896]{2,1,0:T(8,128)(2,1)}), bf16[8,16,896]{2,1,0:T(8,128)(2,1)S(1)}, u32[]{:S(2)}, u32[]{:S(2)}) %all-to-all-start) | async-done | bytes 229408 | tf_op jit(solution)/shard_map/all_to_all | solution.py:21
  27.2 0.1 fusion.21
  27.3 0.1 reduce_sum.41
  27.4 0.0 copy-done
  27.5 0.4 fusion.8
  27.9 0.0 copy-start.1
  27.9 0.1 select_convert_fusion.1
  28.1 12.5 %all_to_all.40 = bf16[8,16,1152]{2,1,0:T(8,128)(2,1)S(1)} all-to-all(bf16[8,16,1152]{2,1,0:T(8,128)(2,1)S(1)} %bitcast.68), channel_id=1, replica_groups={{3,4,5,6,7,0,1,2},{11,12,13,14,15,8,9,10},{19,20,21,22,23,16,17,18},{27..., dimensions={0} | all-to-all | bytes 589824 | tf_op jit(solution)/shard_map/all_to_all | solution.py:27
  40.6 0.1 fusion.42
  40.7 0.1 fusion.40
  40.8 0.0 copy-start.3
  40.9 0.0 copy-start.4
  40.9 0.0 copy-start.5
  40.9 8.1 %all_to_all.41 = bf16[8,16,1024]{2,1,0:T(8,128)(2,1)S(1)} all-to-all(bf16[8,16,1024]{2,1,0:T(8,128)(2,1)S(1)} %broadcast_in_dim.44), channel_id=1, replica_groups={{3,4,5,6,7,0,1,2},{11,12,13,14,15,8,9,10},{19,20,21,22,23,16,17,18},{27..., dimensions={0} | all-to-all | bytes 524288 | tf_op jit(solution)/shard_map/all_to_all | solution.py:27
  49.0 0.0 copy-done.1
  49.0 0.4 fusion.14
  49.5 18.5 %all_to_all.42 = bf16[8,16,896]{2,1,0:T(8,128)(2,1)S(1)} all-to-all(bf16[8,16,896]{2,1,0:T(8,128)(2,1)S(1)} %bitcast.74), channel_id=1, replica_groups={{32,40,48,56,0,8,16,24},{33,41,49,57,1,9,17,25},{34,42,50,58,2,10,18,26..., dimensions={0} | all-to-all | bytes 458752 | tf_op jit(solution)/shard_map/all_to_all | solution.py:21
  68.0 0.0 copy-done.3
  68.0 0.0 copy-done.4
  68.0 0.2 fusion.20
  68.2 6.1 %collective-permute-start = (bf16[16,896]{1,0:T(8,128)(2,1)S(1)}, bf16[16,896]{1,0:T(8,128)(2,1)S(1)}, u32[]{:S(2)}, u32[]{:S(2)}) collective-permute-start(bf16[16,896]{1,0:T(8,128)(2,1)S(1)} %get-tuple-element.24), channel_id=1, source_target_pairs={{0,64},{64,128},{128,192},{192,256},{256,320},{320,384},{384,448},... | collective-permute-start | bytes 86024 | tf_op jit(solution)/shard_map/ppermute | solution.py:32
  74.3 0.0 collective-permute-start.1
  74.3 1.0 collective-permute-done
  75.3 2.3 %collective-permute-done.1 = bf16[16,896]{1,0:T(8,128)(2,1)S(1)} collective-permute-done((bf16[16,896]{1,0:T(8,128)(2,1)S(1)}, bf16[16,896]{1,0:T(8,128)(2,1)S(1)}, u32[]{:S(2)}, u32[]{:S(2)}) %collective-permute-start.1) | collective-permute-done | bytes 28704 | tf_op jit(solution)/shard_map/ppermute | solution.py:32
  77.6 0.0 copy-done.5
  77.6 0.2 convolution_convert_fusion
  77.8 18.9 %all_to_all.43 = bf16[8,16,896]{2,1,0:T(8,128)(2,1)S(1)} all-to-all(bf16[8,16,896]{2,1,0:T(8,128)(2,1)S(1)} %bitcast.76), channel_id=1, replica_groups={{40,48,56,0,8,16,24,32},{41,49,57,1,9,17,25,33},{42,50,58,2,10,18,26,34..., dimensions={0} | all-to-all | bytes 458752 | tf_op jit(solution)/shard_map/all_to_all | solution.py:21
  96.7 0.1 fusion.23
  96.8 0.1 reduce_sum.44
  96.9 0.5 fusion.11
  97.4 0.0 copy-start.2
  97.4 0.1 select_convert_fusion
  97.5 14.1 %all_to_all.44 = bf16[8,16,1152]{2,1,0:T(8,128)(2,1)S(1)} all-to-all(bf16[8,16,1152]{2,1,0:T(8,128)(2,1)S(1)} %bitcast.69), channel_id=1, replica_groups={{3,4,5,6,7,0,1,2},{11,12,13,14,15,8,9,10},{19,20,21,22,23,16,17,18},{27..., dimensions={0} | all-to-all | bytes 589824 | tf_op jit(solution)/shard_map/all_to_all | solution.py:27
  111.7 0.1 fusion.41
  111.7 0.1 fusion.37
  111.9 8.1 %all_to_all.45 = bf16[8,16,1024]{2,1,0:T(8,128)(2,1)S(1)} all-to-all(bf16[8,16,1024]{2,1,0:T(8,128)(2,1)S(1)} %broadcast_in_dim.47), channel_id=1, replica_groups={{3,4,5,6,7,0,1,2},{11,12,13,14,15,8,9,10},{19,20,21,22,23,16,17,18},{27..., dimensions={0} | all-to-all | bytes 524288 | tf_op jit(solution)/shard_map/all_to_all | solution.py:27
  120.0 0.5 fusion.17
  120.5 20.5 %all_to_all.46 = bf16[8,16,896]{2,1,0:T(8,128)(2,1)S(1)} all-to-all(bf16[8,16,896]{2,1,0:T(8,128)(2,1)S(1)} %bitcast.75), channel_id=1, replica_groups={{32,40,48,56,0,8,16,24},{33,41,49,57,1,9,17,25},{34,42,50,58,2,10,18,26..., dimensions={0} | all-to-all | bytes 458752 | tf_op jit(solution)/shard_map/all_to_all | solution.py:21
  141.0 0.2 add_convert_fusion
  141.2 4.5 %collective-permute-start.2 = (bf16[16,896]{1,0:T(8,128)(2,1)S(1)}, bf16[16,896]{1,0:T(8,128)(2,1)S(1)}, u32[]{:S(2)}, u32[]{:S(2)}) collective-permute-start(bf16[16,896]{1,0:T(8,128)(2,1)S(1)} %get-tuple-element.21), channel_id=1, source_target_pairs={{0,64},{64,128},{128,192},{192,256},{256,320},{320,384},{384,448},... | collective-permute-start | bytes 86024 | tf_op jit(solution)/shard_map/ppermute | solution.py:32
  145.7 0.0 collective-permute-start.3
  145.7 1.0 collective-permute-done.2
  146.7 2.3 %collective-permute-done.3 = bf16[16,896]{1,0:T(8,128)(2,1)S(1)} collective-permute-done((bf16[16,896]{1,0:T(8,128)(2,1)S(1)}, bf16[16,896]{1,0:T(8,128)(2,1)S(1)}, u32[]{:S(2)}, u32[]{:S(2)}) %collective-permute-start.3) | collective-permute-done | bytes 28704 | tf_op jit(solution)/shard_map/ppermute | solution.py:32
  149.0 0.6 pad_maximum_fusion.4
  (18 shorter events, 0.3 us)
Async XLA Ops:
  0.0 27.4 %copy-start = (bf16[1,1,896,1024]{3,2,1,0:T(8,128)(2,1)S(1)}, bf16[1,1,896,1024]{3,2,1,0:T(8,128)(2,1)}, u32[]{:S(2)}) copy-start(bf16[1,1,896,1024]{3,2,1,0:T(8,128)(2,1)} %param.7) | copy-start | bytes 5505028
  2.2 25.1 %all-to-all-start = ((bf16[8,16,896]{2,1,0:T(8,128)(2,1)}), bf16[8,16,896]{2,1,0:T(8,128)(2,1)S(1)}, u32[]{:S(2)}, u32[]{:S(2)}) async-start(bf16[8,16,896]{2,1,0:T(8,128)(2,1)} %bitcast.81), calls=%async_computation | async-start | bytes 458752 | tf_op jit(solution)/shard_map/all_to_all | solution.py:21
  27.9 21.1 %copy-start.1 = (bf16[1,1,1024,896]{3,2,1,0:T(8,128)(2,1)S(1)}, bf16[1,1,1024,896]{3,2,1,0:T(8,128)(2,1)}, u32[]{:S(2)}) copy-start(bf16[1,1,1024,896]{3,2,1,0:T(8,128)(2,1)} %param.8) | copy-start | bytes 5505028
  40.8 27.1 %copy-start.3 = (bf16[1,2,1,16,896]{4,3,2,1,0:T(8,128)(2,1)S(1)}, bf16[1,2,1,16,896]{4,3,2,1,0:T(8,128)(2,1)}, u32[]{:S(2)}) copy-start(bf16[1,2,1,16,896]{4,3,2,1,0:T(8,128)(2,1)} %param.6) | copy-start | bytes 172036
  40.9 27.1 %copy-start.4 = (f32[2,32,128]{2,1,0:T(8,128)S(1)}, f32[2,32,128]{2,1,0:T(8,128)}, u32[]{:S(2)}) copy-start(f32[2,32,128]{2,1,0:T(8,128)} %get-tuple-element.9) | copy-start | bytes 98308
  40.9 36.7 %copy-start.5 = (bf16[1,128,32]{2,1,0:T(8,128)(2,1)S(1)}, bf16[1,128,32]{2,1,0:T(8,128)(2,1)}, u32[]{:S(2)}) copy-start(bf16[1,128,32]{2,1,0:T(8,128)(2,1)} %get-tuple-element.12) | copy-start | bytes 24580
  68.2 7.1 %collective-permute-start = (bf16[16,896]{1,0:T(8,128)(2,1)S(1)}, bf16[16,896]{1,0:T(8,128)(2,1)S(1)}, u32[]{:S(2)}, u32[]{:S(2)}) collective-permute-start(bf16[16,896]{1,0:T(8,128)(2,1)S(1)} %get-tuple-element.24), channel_id=1, source_target_pairs={{0,64},{64,128},{128,192},{192,256},{256,320},{320,384},{384,448},... | collective-permute-start | bytes 86024 | tf_op jit(solution)/shard_map/ppermute | solution.py:32
  74.3 3.3 %collective-permute-start.1 = (bf16[16,896]{1,0:T(8,128)(2,1)S(1)}, bf16[16,896]{1,0:T(8,128)(2,1)S(1)}, u32[]{:S(2)}, u32[]{:S(2)}) collective-permute-start(bf16[16,896]{1,0:T(8,128)(2,1)S(1)} %get-tuple-element.23), channel_id=1, source_target_pairs={{0,448},{64,0},{128,64},{192,128},{256,192},{320,256},{384,320},{4... | collective-permute-start | bytes 86024 | tf_op jit(solution)/shard_map/ppermute | solution.py:32
  97.4 22.6 %copy-start.2 = (bf16[1,1,1024,896]{3,2,1,0:T(8,128)(2,1)S(1)}, bf16[1,1,1024,896]{3,2,1,0:T(8,128)(2,1)}, u32[]{:S(2)}) copy-start(bf16[1,1,1024,896]{3,2,1,0:T(8,128)(2,1)} %param.8) | copy-start | bytes 5505028
  141.2 5.5 %collective-permute-start.2 = (bf16[16,896]{1,0:T(8,128)(2,1)S(1)}, bf16[16,896]{1,0:T(8,128)(2,1)S(1)}, u32[]{:S(2)}, u32[]{:S(2)}) collective-permute-start(bf16[16,896]{1,0:T(8,128)(2,1)S(1)} %get-tuple-element.21), channel_id=1, source_target_pairs={{0,64},{64,128},{128,192},{192,256},{256,320},{320,384},{384,448},... | collective-permute-start | bytes 86024 | tf_op jit(solution)/shard_map/ppermute | solution.py:32
  145.7 3.3 %collective-permute-start.3 = (bf16[16,896]{1,0:T(8,128)(2,1)S(1)}, bf16[16,896]{1,0:T(8,128)(2,1)S(1)}, u32[]{:S(2)}, u32[]{:S(2)}) collective-permute-start(bf16[16,896]{1,0:T(8,128)(2,1)S(1)} %get-tuple-element.22), channel_id=1, source_target_pairs={{0,448},{64,0},{128,64},{192,128},{256,192},{320,256},{384,320},{4... | collective-permute-start | bytes 86024 | tf_op jit(solution)/shard_map/ppermute | solution.py:32
